TPU v7x, 128 devices: a whole 4x4x4 slice. The times are simulated.
128 devices in a mesh: dp: 16 (over y, z), seq: 8 (over x, core).
Axes of the slice: x: 4, y: 4, z: 4, core: 2. Of those that a mesh axis runs over, the one named last changes fastest.
Arguments:
- queries: bfloat16 [16, 2048, 2048], P('dp', 'seq'), may hold values from -4.5 to 4.5
- key_states: bfloat16 [16, 2048, 2048], P('dp', 'seq'), may hold values from -4.5 to 4.5
- value_states: bfloat16 [16, 2048, 2048], P('dp', 'seq'), may hold values from -6 to 6
- grad_output: bfloat16 [16, 2048, 2048], P('dp', 'seq'), may hold values from -6 to 6
- out_weight: bfloat16 [2048, 2048], P('dp'), may hold values from -0.125 to 0.125
- key_tiles: int32 [16, 16, 16, 7], P('dp'), may hold values from 0 to 15, as said below
- tile_count: int32 [16, 16, 16], P('dp'), may hold values from 1 to 7, as said below
Outputs:
- output: bfloat16 [16, 2048, 2048], P('dp', 'seq')
- grad_query: bfloat16 [16, 2048, 2048], P('dp', 'seq')
- grad_key: bfloat16 [16, 2048, 2048], P('dp', 'seq')
- grad_value: bfloat16 [16, 2048, 2048], P('dp', 'seq')
- grad_weight: float32 [2048, 2048], P('dp')
Inputs may be any that keep to these rules, and one draw needn't show every extreme that they name: `key_tiles`: entry 0 of every list is the query tile itself; the first tile_count entries of a list are distinct tiles, the others are ignored. For every clip and query tile, tile_count of head h plus tile_count of head h + 8 is exactly 8.
All inputs are finite; a program needn't handle non-finite values.
Results may differ from a plain program's by a relative error of at most 0.024.
Values may be sent and summed in bfloat16 or wider, within the bound.
No kernel may reach another device: no remote copies, remote signals or barrier semaphores. Data moves between devices by JAX's collectives and lax.ppermute only.
A program may use at most 192 MiB of HBM per device.

v0:
```python
import math

import jax
import jax.numpy as jnp
from jax import lax
from jax.sharding import PartitionSpec as P


def tile_attention(q_units, k_tiles, v_tiles, g_units, pair_unit, pair_tile, pair_valid):
    unit_count = q_units.shape[0]
    table_size = k_tiles.shape[0]
    score_scale = 1.0 / math.sqrt(q_units.shape[-1])
    q_pair = q_units[pair_unit]
    k_pair = k_tiles[pair_tile]
    v_pair = v_tiles[pair_tile]
    g_pair = g_units[pair_unit]
    scores = (
        jnp.einsum("prd,psd->prs", q_pair, k_pair, preferred_element_type=jnp.float32) * score_scale
    )
    pair_live = pair_valid[:, None, None]
    row_top = jnp.where(pair_valid[:, None], jnp.max(scores, axis=-1), -jnp.inf)
    member = pair_unit[None, :] == jnp.arange(unit_count)[:, None]
    unit_top = jnp.max(jnp.where(member[:, :, None], row_top[None, :, :], -jnp.inf), axis=1)
    probabilities = jnp.where(pair_live, jnp.exp(scores - unit_top[pair_unit][:, :, None]), 0.0)
    row_total = jax.ops.segment_sum(jnp.sum(probabilities, axis=-1), pair_unit, unit_count)
    mixed_rows = jnp.einsum(
        "prs,psd->prd",
        probabilities.astype(jnp.bfloat16),
        v_pair,
        preferred_element_type=jnp.float32,
    )
    attention = (
        jax.ops.segment_sum(mixed_rows, pair_unit, unit_count) / row_total[:, :, None]
    ).astype(jnp.bfloat16)
    log_total = unit_top + jnp.log(row_total)
    row_delta = jnp.sum(g_units.astype(jnp.float32) * attention.astype(jnp.float32), axis=-1)
    replayed = jnp.where(pair_live, jnp.exp(scores - log_total[pair_unit][:, :, None]), 0.0)
    value_parts = jnp.einsum(
        "prs,prd->psd", replayed.astype(jnp.bfloat16), g_pair, preferred_element_type=jnp.float32
    )
    grad_prob = jnp.einsum("prd,psd->prs", g_pair, v_pair, preferred_element_type=jnp.float32)
    grad_score = (replayed * (grad_prob - row_delta[pair_unit][:, :, None])).astype(jnp.bfloat16)
    query_parts = jnp.einsum("prs,psd->prd", grad_score, k_pair, preferred_element_type=jnp.float32)
    grad_query = jax.ops.segment_sum(query_parts, pair_unit, unit_count) * score_scale
    key_parts = (
        jnp.einsum("prs,prd->psd", grad_score, q_pair, preferred_element_type=jnp.float32)
        * score_scale
    )
    grad_key = jax.ops.segment_sum(key_parts, pair_tile, table_size)
    grad_value = jax.ops.segment_sum(value_parts, pair_tile, table_size)
    return (
        attention,
        grad_query.astype(jnp.bfloat16),
        grad_key.astype(jnp.bfloat16),
        grad_value.astype(jnp.bfloat16),
    )


def head_batch(bundle):
    q_head, k_head, v_head, g_head, counts, tile_lists = bundle
    tile_total, list_width = tile_lists.shape
    head_dim = q_head.shape[-1]
    pair_slots = jnp.arange(tile_total * list_width)
    pair_unit = pair_slots // list_width
    pair_valid = pair_slots % list_width < counts[pair_unit]
    outcome = tile_attention(
        q_head.reshape(tile_total, -1, head_dim),
        k_head.reshape(tile_total, -1, head_dim),
        v_head.reshape(tile_total, -1, head_dim),
        g_head.reshape(tile_total, -1, head_dim),
        pair_unit,
        tile_lists.reshape(-1),
        pair_valid,
    )
    return (
        outcome[0].reshape(-1, head_dim),
        outcome[1].reshape(-1, head_dim),
        outcome[2].reshape(-1, head_dim),
        outcome[3].reshape(-1, head_dim),
    )


def per_device(queries, key_states, value_states, grad_output, out_weight, key_tiles, tile_count):
    seq_count = lax.axis_size("seq")
    seq_index = lax.axis_index("seq")
    tokens = queries.shape[1]
    columns = queries.shape[2]
    head_count = tile_count.shape[1]
    head_dim = columns // head_count
    own_heads = head_count // seq_count
    weights = lax.all_gather(out_weight, "dp", axis=0, tiled=True)
    grad_attn = jnp.dot(grad_output[0], weights, preferred_element_type=jnp.float32).astype(
        jnp.bfloat16
    )
    head_order = jnp.arange(head_count, dtype=jnp.int32)

    def to_owners(values):
        by_head = values.reshape(tokens, head_count, head_dim)
        return by_head.reshape(tokens, seq_count, own_heads, head_dim).transpose(1, 2, 0, 3)

    q_all, k_all, v_all, g_all = (
        lax.all_to_all(to_owners(queries[0]), "seq", split_axis=0, concat_axis=2, tiled=True),
        lax.all_to_all(to_owners(key_states[0]), "seq", split_axis=0, concat_axis=2, tiled=True),
        lax.all_to_all(to_owners(value_states[0]), "seq", split_axis=0, concat_axis=2, tiled=True),
        lax.all_to_all(to_owners(grad_attn), "seq", split_axis=0, concat_axis=2, tiled=True),
    )
    own_list = lax.dynamic_slice_in_dim(head_order, seq_index * own_heads, own_heads)
    counts = jnp.take(tile_count[0], own_list, axis=0)
    tile_lists = jnp.take(key_tiles[0], own_list, axis=0)
    results = lax.map(head_batch, (q_all[0], k_all[0], v_all[0], g_all[0], counts, tile_lists))

    def to_homes(values):
        return values.reshape(own_heads, seq_count, tokens, head_dim)

    returned = (
        lax.all_to_all(to_homes(results[0]), "seq", split_axis=1, concat_axis=0, tiled=True),
        lax.all_to_all(to_homes(results[1]), "seq", split_axis=1, concat_axis=0, tiled=True),
        lax.all_to_all(to_homes(results[2]), "seq", split_axis=1, concat_axis=0, tiled=True),
        lax.all_to_all(to_homes(results[3]), "seq", split_axis=1, concat_axis=0, tiled=True),
    )

    def from_owners(values):
        by_head = values.reshape(head_count, tokens, head_dim)
        return by_head.transpose(1, 0, 2).reshape(tokens, columns)

    attention = from_owners(returned[0])
    output = jnp.einsum("tc,oc->to", attention, weights, preferred_element_type=jnp.float32).astype(
        jnp.bfloat16
    )
    picked = grad_output[0]
    partial_rows = lax.psum_scatter(
        lax.dot_general(
            picked, attention, (((0,), (0,)), ((), ())), preferred_element_type=jnp.float32
        ),
        ("dp", "seq"),
        scatter_dimension=0,
        tiled=True,
    )
    grad_weight = lax.all_gather(
        partial_rows.astype(jnp.bfloat16), "seq", axis=0, tiled=True
    ).astype(partial_rows.dtype)
    return (
        output[None],
        from_owners(returned[1])[None],
        from_owners(returned[2])[None],
        from_owners(returned[3])[None],
        grad_weight,
    )


def solution(mesh):
    in_specs = (
        P("dp", "seq", None),
        P("dp", "seq", None),
        P("dp", "seq", None),
        P("dp", "seq", None),
        P("dp", None),
        P("dp", None, None, None),
        P("dp", None, None),
    )
    out_specs = (
        P("dp", "seq", None),
        P("dp", "seq", None),
        P("dp", "seq", None),
        P("dp", "seq", None),
        P("dp", None),
    )
    return jax.shard_map(
        per_device, mesh=mesh, in_specs=in_specs, out_specs=out_specs, check_vma=False
    )
```

profile of v0, /device:TPU:1, one launch (start us, length us, event | category | flops | bytes accessed | tf_op | source)
XLA Modules:
  0.0 1184.4 jit_solution(1922470156209656980)
XLA Ops:
  10.7 5.8 all-to-all-start
  19.3 12.3 %all-to-all-done = bf16[8,2,256,128]{3,2,1,0:T(8,128)(2,1)S(1)} async-done(((bf16[8,2,256,128]{3,2,1,0:T(8,128)(2,1)}), bf16[8,2,256,128]{3,2,1,0:T(8,128)(2,1)S(1)}, u32[]{:S(2)}, u32[]{:S(2)}) %all-to-all-start) | async-done | bytes 1048608 | tf_op jit(solution)/shard_map/all_to_all | solution.py:102
  31.6 4.3 all-to-all-start.1
  38.2 2.3 copy.139
  40.5 10.6 all-to-all-done.1
  51.1 5.0 all-to-all-start.2
  56.1 28.2 %all-gather.2.cloned.1.call-done = bf16[2048,2048]{1,0:T(8,128)(2,1)} async-done(((bf16[128,2048]{1,0:T(8,128)(2,1)}), bf16[2048,2048]{1,0:T(8,128)(2,1)}) %all-gather.2.cloned.1.call-update) | async-done | bytes 8388624 | tf_op jit(solution)/shard_map/all_gather | solution.py:91
  84.3 6.7 convolution_convert_fusion.1
  91.0 2.6 reshape_reshape.3
  93.5 3.0 copy.162
  96.5 4.9 all-to-all-start.3
  105.0 2.3 copy.140
  107.3 9.3 all-to-all-done.3
  116.6 2.3 copy.143
  119.0 324.4 %while.18 = (s32[]{:T(128)}, bf16[2,2048,128]{2,1,0:T(8,128)(2,1)}, bf16[2,2048,128]{2,1,0:T(8,128)(2,1)}, bf16[2,2048,128]{2,1,0:T(8,128)(2,1)}, bf16[2,2048,12...) while((s32[]{:T(128)}, bf16[2,2048,128]{2,1,0:T(8,128)(2,1)}, ...), condition=%wide.region_10.11_spmd, body=%wide.region_0.10_spmd.sunk | while | flops 2867538176 | bytes 288309728 | solution.py:110
  134.5 2.9 gather_fusion
  138.7 2.9 gather_fusion.1
  141.7 8.8 multiply_reduce_fusion.4
  152.6 2.9 gather_fusion.2
  156.2 10.2 fusion.83
  167.4 9.3 fusion.84
  176.8 15.0 %scatter_fusion = f32[16,128,128]{2,1,0:T(8,128)S(1)} fusion(f32[16,128,128]{2,1,0:T(8,128)S(1)} %broadcast.524.clone.1, s32[112]{0:T(128)S(1)} %fusion.79, f32[112,128,128]{2,1,0:T(8,128)} %fusion.84), kind=kCustom, calls=%fused_computation.9.clone.1 | custom fusion | flops 1835008 | bytes 22020544 | tf_op jit(solution)/shard_map/while/body/eval_jaxpr/scatter-add | solution.py:33
  191.8 4.5 fusion.85
  199.5 2.9 gather_fusion.6
  202.3 8.1 multiply_convert_fusion.4
  210.4 4.3 fusion.86
  214.8 15.0 %scatter_fusion.1 = f32[16,128,128]{2,1,0:T(8,128)S(1)} fusion(f32[16,128,128]{2,1,0:T(8,128)S(1)} %broadcast.524.clone, s32[112]{0:T(128)S(1)} %fusion.79, f32[112,128,128]{2,1,0:T(8,128)} %fusion.86), kind=kCustom, calls=%fused_computation.11.clone.1 | custom fusion | flops 1835008 | bytes 22020544 | tf_op jit(solution)/shard_map/while/body/eval_jaxpr/scatter-add | solution.py:44
  231.0 8.4 fusion.87
  239.6 15.0 %scatter_fusion.2 = f32[16,128,128]{2,1,0:T(8,128)S(1)} fusion(f32[16,128,128]{2,1,0:T(8,128)S(1)} %broadcast.524.clone.2, s32[112]{0:T(128)S(1)} %reshape.492, f32[112,128,128]{2,1,0:T(8,128)} %fusion.87), kind=kCustom, calls=%fused_computation.13.clone.1 | custom fusion | flops 1835008 | bytes 22020544 | tf_op jit(solution)/shard_map/while/body/eval_jaxpr/scatter-add | solution.py:50
  254.7 8.8 broadcast_multiply_fusion.2
  263.5 8.7 copy.167
  272.3 15.0 %scatter_fusion.3 = f32[16,128,128]{2,1,0:T(8,128)S(1)} fusion(f32[16,128,128]{2,1,0:T(8,128)S(1)} %broadcast.524.clone.3, s32[112]{0:T(128)S(1)} %reshape.492, f32[112,128,128]{2,1,0:T(8,128)} %copy.167), kind=kCustom, calls=%fused_computation.12.clone.1 | custom fusion | flops 1835008 | bytes 22020544 | tf_op jit(solution)/shard_map/while/body/eval_jaxpr/scatter-add | solution.py:49
  289.5 2.9 gather_fusion
  293.7 2.9 gather_fusion.1
  296.7 8.8 multiply_reduce_fusion.4
  307.6 2.9 gather_fusion.2
  311.2 10.2 fusion.83
  322.5 9.3 fusion.84
  331.8 15.0 %scatter_fusion = f32[16,128,128]{2,1,0:T(8,128)S(1)} fusion(f32[16,128,128]{2,1,0:T(8,128)S(1)} %broadcast.524.clone.1, s32[112]{0:T(128)S(1)} %fusion.79, f32[112,128,128]{2,1,0:T(8,128)} %fusion.84), kind=kCustom, calls=%fused_computation.9.clone.1 | custom fusion | flops 1835008 | bytes 22020544 | tf_op jit(solution)/shard_map/while/body/eval_jaxpr/scatter-add | solution.py:33
  346.8 4.5 fusion.85
  354.5 2.9 gather_fusion.6
  357.3 8.1 multiply_convert_fusion.4
  365.4 4.3 fusion.86
  369.8 15.0 %scatter_fusion.1 = f32[16,128,128]{2,1,0:T(8,128)S(1)} fusion(f32[16,128,128]{2,1,0:T(8,128)S(1)} %broadcast.524.clone, s32[112]{0:T(128)S(1)} %fusion.79, f32[112,128,128]{2,1,0:T(8,128)} %fusion.86), kind=kCustom, calls=%fused_computation.11.clone.1 | custom fusion | flops 1835008 | bytes 22020544 | tf_op jit(solution)/shard_map/while/body/eval_jaxpr/scatter-add | solution.py:44
  386.0 8.4 fusion.87
  394.6 15.0 %scatter_fusion.2 = f32[16,128,128]{2,1,0:T(8,128)S(1)} fusion(f32[16,128,128]{2,1,0:T(8,128)S(1)} %broadcast.524.clone.2, s32[112]{0:T(128)S(1)} %reshape.492, f32[112,128,128]{2,1,0:T(8,128)} %fusion.87), kind=kCustom, calls=%fused_computation.13.clone.1 | custom fusion | flops 1835008 | bytes 22020544 | tf_op jit(solution)/shard_map/while/body/eval_jaxpr/scatter-add | solution.py:50
  409.7 8.8 broadcast_multiply_fusion.2
  418.5 8.7 copy.167
  427.2 15.0 %scatter_fusion.3 = f32[16,128,128]{2,1,0:T(8,128)S(1)} fusion(f32[16,128,128]{2,1,0:T(8,128)S(1)} %broadcast.524.clone.3, s32[112]{0:T(128)S(1)} %reshape.492, f32[112,128,128]{2,1,0:T(8,128)} %copy.167), kind=kCustom, calls=%fused_computation.12.clone.1 | custom fusion | flops 1835008 | bytes 22020544 | tf_op jit(solution)/shard_map/while/body/eval_jaxpr/scatter-add | solution.py:49
  444.7 18.4 %all_to_all.120 = bf16[2,8,256,128]{3,2,0,1:T(8,128)(2,1)S(1)} all-to-all(bf16[2,8,256,128]{3,2,0,1:T(8,128)(2,1)S(1)} %copy.144), channel_id=1, replica_groups=mesh['dp'=16,'seq'=8] {'seq'}, dimensions={1} | all-to-all | bytes 2097152 | tf_op jit(solution)/shard_map/all_to_all | solution.py:116
  463.6 8.1 convolution_bitcast_fusion
  471.6 17.6 %copy.157 = f32[2048,2048]{1,0:T(8,128)} copy(f32[2048,2048]{0,1:T(8,128)} %convolution_bitcast_fusion) | data formatting | bytes 33554432
  491.5 4.5 all-to-all-start.5
  496.0 2.3 copy.148
  498.3 15.7 %all-to-all-done.5 = bf16[2,8,256,128]{3,2,0,1:T(8,128)(2,1)S(1)} async-done(((bf16[2,8,256,128]{3,2,0,1:T(8,128)(2,1)}), bf16[2,8,256,128]{3,2,0,1:T(8,128)(2,1)S(1)}, u32[]{:S(2)}, u32[]{:S(2)}) %all-to-all-start.5) | async-done | bytes 1048608 | tf_op jit(solution)/shard_map/all_to_all | solution.py:117
  514.0 4.9 all-to-all-start.6
  518.9 2.3 copy.150
  521.2 14.7 %all-to-all-done.6 = bf16[2,8,256,128]{3,2,0,1:T(8,128)(2,1)} async-done(((bf16[2,8,256,128]{3,2,0,1:T(8,128)(2,1)}), bf16[2,8,256,128]{3,2,0,1:T(8,128)(2,1)}, u32[]{:S(2)}, u32[]{:S(2)}) %all-to-all-start.6) | async-done | bytes 1048608 | tf_op jit(solution)/shard_map/all_to_all | solution.py:118
  535.9 4.8 all-to-all-start.7
  542.3 2.3 broadcast_in_dim_reshape.9
  547.8 9.4 all-to-all-done.7
  560.4 6.8 fusion.25
  567.2 590.9 %reduce-scatter.4.cloned.1.call-done = f32[16,2048]{1,0:T(8,128)} async-done(((f32[2048,2048]{1,0:T(8,128)}), f32[16,2048]{1,0:T(8,128)}) %reduce-scatter.4.cloned.1.call-update) | async-done | bytes 131088 | tf_op jit(solution)/shard_map/reduce_scatter | solution.py:131
  1159.0 17.1 %all_gather.7 = bf16[128,2048]{1,0:T(8,128)(2,1)S(1)} all-gather(bf16[16,2048]{1,0:T(8,128)(2,1)S(1)} %convert_element_type.68), channel_id=1, replica_groups=mesh['dp'=16,'seq'=8] {'seq'}, dimensions={0}, use_global_device_ids=true | all-gather | bytes 589824 | tf_op jit(solution)/shard_map/all_gather | solution.py:139
  (118 shorter events, 50.8 us)
Async XLA Ops:
  7.2 77.1 %copy-start = (bf16[1,256,2048]{2,1,0:T(8,128)(2,1)S(1)}, bf16[1,256,2048]{2,1,0:T(8,128)(2,1)}, u32[]{:S(2)}) copy-start(bf16[1,256,2048]{2,1,0:T(8,128)(2,1)} %param.12) | copy-start | bytes 3145732
  7.2 77.1 %all-gather.2.cloned.1.call-start = ((), (), s32[]{:S(2)}) async-start(), calls=%async_computation.9 | async-start | bytes 8912896 | tf_op jit(solution)/shard_map/all_gather | solution.py:91
  10.7 20.9 %all-to-all-start = ((bf16[8,2,256,128]{3,2,1,0:T(8,128)(2,1)}), bf16[8,2,256,128]{3,2,1,0:T(8,128)(2,1)S(1)}, u32[]{:S(2)}, u32[]{:S(2)}) async-start(bf16[8,2,256,128]{3,2,1,0:T(8,128)(2,1)} %copy.132), calls=%async_computation | async-start | bytes 2097152 | tf_op jit(solution)/shard_map/all_to_all | solution.py:102
  31.6 19.5 %all-to-all-start.1 = ((bf16[8,2,256,128]{3,2,1,0:T(8,128)(2,1)}), bf16[8,2,256,128]{3,2,1,0:T(8,128)(2,1)S(1)}, u32[]{:S(2)}, u32[]{:S(2)}) async-start(bf16[8,2,256,128]{3,2,1,0:T(8,128)(2,1)} %copy.135), calls=%async_computation.1 | async-start | bytes 2097152 | tf_op jit(solution)/shard_map/all_to_all | solution.py:103
  51.1 45.4 %all-to-all-start.2 = ((bf16[8,2,256,128]{3,2,1,0:T(8,128)(2,1)}), bf16[8,2,256,128]{3,2,1,0:T(8,128)(2,1)}, u32[]{:S(2)}, u32[]{:S(2)}) async-start(bf16[8,2,256,128]{3,2,1,0:T(8,128)(2,1)} %copy.139), calls=%async_computation.2 | async-start | bytes 2097152 | tf_op jit(solution)/shard_map/all_to_all | solution.py:104
  56.1 45.4 %copy-start.4 = (s32[1,16,16,7]{2,1,3,0:T(8,128)S(1)}, s32[1,16,16,7]{2,1,3,0:T(8,128)}, u32[]{:S(2)}) copy-start(s32[1,16,16,7]{2,1,3,0:T(8,128)} %param.14) | copy-start | bytes 21508
  56.1 45.5 %copy-start.5 = (s32[1,16,16]{2,1,0:T(8,128)S(1)}, s32[1,16,16]{2,1,0:T(8,128)}, u32[]{:S(2)}) copy-start(s32[1,16,16]{2,1,0:T(8,128)} %param.15) | copy-start | bytes 3076
  96.5 20.1 %all-to-all-start.3 = ((bf16[8,2,256,128]{3,1,2,0:T(2,128)(2,1)}), bf16[8,2,256,128]{3,1,2,0:T(2,128)(2,1)}, u32[]{:S(2)}, u32[]{:S(2)}) async-start(bf16[8,2,256,128]{3,1,2,0:T(2,128)(2,1)} %bitcast.214), calls=%async_computation.3 | async-start | bytes 2097152 | tf_op jit(solution)/shard_map/all_to_all | solution.py:105
  101.4 1056.6 %reduce-scatter.4.cloned.1.call-start = ((), (), s32[]{:S(2)}) async-start(), calls=%async_computation.10 | async-start | bytes 16908288 | tf_op jit(solution)/shard_map/reduce_scatter | solution.py:131
  202.3 8.1 copy-start.1
  210.4 4.3 copy-start.2
  357.3 8.1 copy-start.1
  365.4 4.3 copy-start.2
  489.3 1.2 copy-start.3
  491.5 22.5 %all-to-all-start.5 = ((bf16[2,8,256,128]{3,2,0,1:T(8,128)(2,1)}), bf16[2,8,256,128]{3,2,0,1:T(8,128)(2,1)S(1)}, u32[]{:S(2)}, u32[]{:S(2)}) async-start(bf16[2,8,256,128]{3,2,0,1:T(8,128)(2,1)} %copy.146), calls=%async_computation.5 | async-start | bytes 2097152 | tf_op jit(solution)/shard_map/all_to_all | solution.py:117
  514.0 21.8 %all-to-all-start.6 = ((bf16[2,8,256,128]{3,2,0,1:T(8,128)(2,1)}), bf16[2,8,256,128]{3,2,0,1:T(8,128)(2,1)}, u32[]{:S(2)}, u32[]{:S(2)}) async-start(bf16[2,8,256,128]{3,2,0,1:T(8,128)(2,1)} %copy.148), calls=%async_computation.6 | async-start | bytes 2097152 | tf_op jit(solution)/shard_map/all_to_all | solution.py:118
  535.9 21.3 %all-to-all-start.7 = ((bf16[2,8,256,128]{3,2,0,1:T(8,128)(2,1)}), bf16[2,8,256,128]{3,2,0,1:T(8,128)(2,1)}, u32[]{:S(2)}, u32[]{:S(2)}) async-start(bf16[2,8,256,128]{3,2,0,1:T(8,128)(2,1)} %copy.150), calls=%async_computation.7 | async-start | bytes 2097152 | tf_op jit(solution)/shard_map/all_to_all | solution.py:119
Sparse Core Ops, SparseCore 0:
  10.2 74.0 all-gather.1
  489.4 668.6 reduce-scatter.3
where the time goes:
time: 1190 us; the launch traced here: 1180 us
  waiting for transfers between devices  692 us (58%)
  other arithmetic  157 us (13%)
  local copies, waits for them, and re-layouts  120 us (10%)
  matrix products  117 us (10%)
  blocking collectives  35.5 us (3%)
  starting transfers between devices  34.3 us (3%)
  loops' own time  14.9 us (1%)
  between operations  14.5 us (1%)
    reduce_scatter x1, waiting for transfers between devices, per_device(): lax.psum_scatter(lax.dot_general(picked, attention, (((0,), (0,)), ((), (...  591 us
    scatter-add x2, other arithmetic, tile_attention(): grad_value = jax.ops.segment_sum(value_parts, pair_tile, table_size)  30 us
    scatter-add x2, other arithmetic, tile_attention(): grad_key = jax.ops.segment_sum(key_parts, pair_tile, table_size)  30 us
    scatter-add x2, other arithmetic, tile_attention(): jax.ops.segment_sum(mixed_rows, pair_unit, unit_count)  29.9 us
    scatter-add x2, other arithmetic, tile_attention(): jax.ops.segment_sum(query_parts, pair_unit, unit_count) * score_scale  29.9 us
    all_gather x1, waiting for transfers between devices, per_device(): weights = lax.all_gather(out_weight, 'dp', axis=0, tiled=True)  28.2 us
    unnamed x13, local copies, waits for them, and re-layouts  24.1 us
  transfers between devices with their start and end apart: 9, of which 8 were waited for; matrix products, arithmetic and copies ran while one was open for 4% of the time, Pallas kernels for 0%

commit v1 on v0

v1 whole, which is shorter than its diff:
```python
import functools
import math

import jax
import jax.numpy as jnp
from jax import lax
from jax.experimental import pallas as pl
from jax.experimental.pallas import tpu as pltpu
from jax.sharding import PartitionSpec as P

NN = (((1,), (0,)), ((), ()))
NT = (((1,), (1,)), ((), ()))
TN = (((0,), (0,)), ((), ()))
F32 = jnp.float32
BF16 = jnp.bfloat16
MIB = 2**20
SMEM = pl.BlockSpec(memory_space=pltpu.SMEM)
VMEM = pl.BlockSpec(memory_space=pltpu.VMEM)
ANY = pl.BlockSpec(memory_space=pl.ANY)
TILE = 128


def mm(a, b, dims=NN):
    return lax.dot_general(a, b, dims, preferred_element_type=F32)


def cost(flops, moved, exps=0):
    return pl.CostEstimate(flops=flops, bytes_accessed=moved, transcendentals=exps)


def pack_kernel(q_ref, k_ref, v_ref, out_ref, sems):
    seq, _, halves, _, width = out_ref.shape
    copies = []
    for n, ref in enumerate((q_ref, k_ref, v_ref)):
        for s in range(seq):
            for half in range(halves):
                source = ref.at[0, :, pl.ds((s + seq * half) * width, width)]
                copies.append(pltpu.make_async_copy(source, out_ref.at[s, n, half], sems.at[len(copies)]))
    for copy in copies:
        copy.start()
    for copy in copies:
        copy.wait()


def pack(q, k, v, seq, head_dim):
    _, tokens, columns = q.shape
    halves = columns // (seq * head_dim)
    return pl.pallas_call(
        pack_kernel,
        out_shape=jax.ShapeDtypeStruct((seq, 3, halves, tokens, head_dim), q.dtype),
        in_specs=[ANY] * 3,
        out_specs=ANY,
        scratch_shapes=[pltpu.SemaphoreType.DMA((3 * seq * halves,))],
        cost_estimate=cost(0, 12 * tokens * columns),
        name="pack_heads",
    )(q, k, v)


def unpack_kernel(in_ref, q_ref, k_ref, v_ref, sems):
    seq, _, halves, _, width = in_ref.shape
    copies = []
    for n, ref in enumerate((q_ref, k_ref, v_ref)):
        for s in range(seq):
            for half in range(halves):
                target = ref.at[0, :, pl.ds((s + seq * half) * width, width)]
                copies.append(pltpu.make_async_copy(in_ref.at[s, n, half], target, sems.at[len(copies)]))
    for copy in copies:
        copy.start()
    for copy in copies:
        copy.wait()


def unpack(blocks):
    seq, _, halves, tokens, head_dim = blocks.shape
    columns = seq * halves * head_dim
    return pl.pallas_call(
        unpack_kernel,
        out_shape=(jax.ShapeDtypeStruct((1, tokens, columns), blocks.dtype),) * 3,
        in_specs=[ANY],
        out_specs=(ANY,) * 3,
        scratch_shapes=[pltpu.SemaphoreType.DMA((3 * seq * halves,))],
        cost_estimate=cost(0, 12 * tokens * columns),
        name="unpack_heads",
    )(blocks)


def slot_plan(place_ref, tiles_ref, counts_ref, unit, slot, units, width):
    first_head = place_ref[0]
    split = counts_ref[first_head * units + unit]
    in_first = slot < split
    head = jnp.where(in_first, first_head, first_head + place_ref[1])
    entry = jnp.minimum(jnp.where(in_first, slot, width - slot), width - 1)
    tile = tiles_ref[(head * units + unit) * width + entry]
    return in_first, jnp.where(in_first, 0, 1), tile


def rows_of(ref, half, tile):
    per_block = ref.shape[2] // TILE
    start = pl.multiple_of(lax.rem(tile, per_block) * TILE, TILE)
    return ref.at[lax.div(tile, per_block), half, pl.ds(start, TILE), :]


def forward_kernel(slots, units, width, scale, place_ref, tiles_ref, counts_ref, qkv_ref, a_ref, lse_ref, vt_ref, s_ref, p_ref):
    scale2 = scale * math.log2(math.e)
    q_ref, k_ref, v_ref = (qkv_ref.at[:, n] for n in range(3))

    @pl.loop(0, units)
    def _(t):
        for half in range(2):
            vt_ref[half * units + t] = rows_of(v_ref, half, t)[...].T

    @pl.loop(0, units)
    def _(unit):
        plans = [slot_plan(place_ref, tiles_ref, counts_ref, unit, j, units, width) for j in range(slots)]
        tops = []
        for j, (in_first, half, tile) in enumerate(plans):
            q = rows_of(q_ref, half, unit)[...]
            s = mm(rows_of(k_ref, half, tile)[...], q, NT)
            s_ref[j] = s
            tops.append(jnp.max(s.reshape(TILE // 8, 8, TILE), axis=0))
        low = jnp.full((8, TILE), -jnp.inf, F32)
        top = []
        for half in range(2):
            m = low
            for (in_first, _, _), t8 in zip(plans, tops):
                use = in_first if half == 0 else jnp.logical_not(in_first)
                m = jnp.maximum(m, jnp.where(use, t8, low))
            top.append(jnp.max(m, axis=0, keepdims=True) * scale2)
        totals = [jnp.zeros((8, TILE), F32)] * 2
        zero = jnp.zeros((TILE, TILE), BF16)
        for j, (in_first, half, tile) in enumerate(plans):
            p = jnp.exp2(s_ref[j] * scale2 - jnp.where(in_first, top[0], top[1]))
            l8 = jnp.sum(p.reshape(TILE // 8, 8, TILE), axis=0)
            totals[0] = totals[0] + jnp.where(in_first, l8, 0.0)
            totals[1] = totals[1] + jnp.where(in_first, 0.0, l8)
            pb = p.astype(BF16)
            p_ref[pl.ds(j * TILE, TILE), 0:TILE] = jnp.where(in_first, pb, zero)
            p_ref[pl.ds(j * TILE, TILE), TILE : 2 * TILE] = jnp.where(in_first, zero, pb)
        vt = jnp.concatenate([vt_ref[half * units + tile] for _, half, tile in plans], axis=1)
        mixed = mm(vt, p_ref[...])
        for half in range(2):
            total = jnp.sum(totals[half], axis=0, keepdims=True)
            a_t = mixed[:, half * TILE : (half + 1) * TILE] / total
            rows_of(a_ref, half, unit)[...] = a_t.T.astype(BF16)
            lse_ref[half * units + unit] = jnp.broadcast_to(top[half] + jnp.log2(total), (8, TILE))


def attention_forward(place, tiles, counts, qkv, chips, width):
    seq, _, halves, tokens, head_dim = qkv.shape
    units = seq * tokens // TILE
    slots = width + 1
    return pl.pallas_call(
        functools.partial(forward_kernel, slots, units, width, 1.0 / math.sqrt(head_dim)),
        out_shape=(
            jax.ShapeDtypeStruct((chips, halves, seq * tokens // chips, head_dim), BF16),
            jax.ShapeDtypeStruct((halves * units, 8, TILE), F32),
        ),
        in_specs=[SMEM] * 3 + [VMEM],
        out_specs=(VMEM, VMEM),
        scratch_shapes=[
            pltpu.VMEM((halves * units, head_dim, TILE), BF16),
            pltpu.VMEM((slots, TILE, TILE), F32),
            pltpu.VMEM((slots * TILE, 2 * TILE), BF16),
        ],
        compiler_params=pltpu.CompilerParams(vmem_limit_bytes=24 * MIB),
        cost_estimate=cost(16 * units * slots * TILE**3, 5 * MIB, units * slots * TILE * TILE),
        name="attention_forward",
    )(place, tiles, counts, qkv)


def backward_kernel(slots, units, width, scale, place_ref, tiles_ref, counts_ref, qkv_ref, g_ref, a_ref, lse_ref, out_ref, kt_ref, dk_acc, dv_acc, d_ref):
    scale2 = scale * math.log2(math.e)
    q_ref, k_ref, v_ref = (qkv_ref.at[:, n] for n in range(3))
    dq_ref, dk_ref, dv_ref = (out_ref.at[:, n] for n in range(3))

    @pl.loop(0, units)
    def _(t):
        for half in range(2):
            kt_ref[half * units + t] = rows_of(k_ref, half, t)[...].T
            dk_acc[half * units + t] = jnp.zeros((TILE, TILE), F32)
            dv_acc[half * units + t] = jnp.zeros((TILE, TILE), F32)

    @pl.loop(0, units)
    def _(unit):
        plans = [slot_plan(place_ref, tiles_ref, counts_ref, unit, j, units, width) for j in range(slots)]
        delta = []
        lse = []
        for half in range(2):
            prod = rows_of(g_ref, half, unit)[...].astype(F32) * rows_of(a_ref, half, unit)[...].astype(F32)
            delta.append(jnp.sum(prod.T, axis=0, keepdims=True))
            lse.append(lse_ref[half * units + unit][0:1])
        zero = jnp.zeros((TILE, TILE), BF16)
        for j, (in_first, half, tile) in enumerate(plans):
            q = rows_of(q_ref, half, unit)[...]
            g = rows_of(g_ref, half, unit)[...]
            s = mm(rows_of(k_ref, half, tile)[...], q, NT)
            p = jnp.exp2(s * scale2 - jnp.where(in_first, lse[0], lse[1]))
            dp = mm(rows_of(v_ref, half, tile)[...], g, NT)
            ds = (p * (dp - jnp.where(in_first, delta[0], delta[1]))).astype(BF16)
            dv_acc[half * units + tile] += mm(p.astype(BF16), g)
            dk_acc[half * units + tile] += mm(ds, q)
            d_ref[pl.ds(j * TILE, TILE), 0:TILE] = jnp.where(in_first, ds, zero)
            d_ref[pl.ds(j * TILE, TILE), TILE : 2 * TILE] = jnp.where(in_first, zero, ds)
        kt = jnp.concatenate([kt_ref[half * units + tile] for _, half, tile in plans], axis=1)
        dq_t = mm(kt, d_ref[...]) * scale
        for half in range(2):
            rows_of(dq_ref, half, unit)[...] = dq_t[:, half * TILE : (half + 1) * TILE].T.astype(BF16)

    @pl.loop(0, units)
    def _(t):
        for half in range(2):
            rows_of(dk_ref, half, t)[...] = (dk_acc[half * units + t] * scale).astype(BF16)
            rows_of(dv_ref, half, t)[...] = dv_acc[half * units + t].astype(BF16)


def attention_backward(place, tiles, counts, qkv, g, a, lse, width):
    seq, _, halves, tokens, head_dim = qkv.shape
    units = seq * tokens // TILE
    slots = width + 1
    return pl.pallas_call(
        functools.partial(backward_kernel, slots, units, width, 1.0 / math.sqrt(head_dim)),
        out_shape=jax.ShapeDtypeStruct(qkv.shape, BF16),
        in_specs=[SMEM] * 3 + [VMEM] * 4,
        out_specs=VMEM,
        scratch_shapes=[
            pltpu.VMEM((halves * units, head_dim, TILE), BF16),
            pltpu.VMEM((halves * units, TILE, head_dim), F32),
            pltpu.VMEM((halves * units, TILE, head_dim), F32),
            pltpu.VMEM((slots * TILE, 2 * TILE), BF16),
        ],
        compiler_params=pltpu.CompilerParams(vmem_limit_bytes=32 * MIB),
        cost_estimate=cost(36 * units * slots * TILE**3, 9 * MIB, units * slots * TILE * TILE),
        name="attention_backward",
    )(place, tiles, counts, qkv, g, a, lse)


def grad_attn_kernel(place_ref, own_ref, other_ref, w_ref, g_ref):
    tokens = own_ref.shape[0]
    core = place_ref[2]
    for ref, slot in ((own_ref, core), (other_ref, 1 - core)):
        g = mm(ref[...], w_ref[...]).astype(BF16)
        start = pl.multiple_of(slot * tokens, tokens)
        for half in range(2):
            g_ref[0, half, pl.ds(start, tokens), :] = g[:, half * TILE : (half + 1) * TILE]


def grad_attn(place, own, other, weights, chips):
    tokens, depth = own.shape
    columns = weights.shape[1]
    block = columns // chips
    return pl.pallas_call(
        grad_attn_kernel,
        grid=(chips,),
        out_shape=jax.ShapeDtypeStruct((chips, 2, 2 * tokens, block // 2), BF16),
        in_specs=[
            SMEM,
            pl.BlockSpec((tokens, depth), lambda i: (0, 0)),
            pl.BlockSpec((tokens, depth), lambda i: (0, 0)),
            pl.BlockSpec((depth, block), lambda i: (0, i)),
        ],
        out_specs=pl.BlockSpec((1, 2, 2 * tokens, block // 2), lambda i: (i, 0, 0, 0)),
        compiler_params=pltpu.CompilerParams(vmem_limit_bytes=24 * MIB),
        cost_estimate=cost(4 * tokens * depth * columns, 7 * MIB),
        name="grad_attn",
    )(place, own, other, weights)


def token_rows(a_ref, slot):
    chips, halves, rows, _ = a_ref.shape
    tokens = rows // 2
    start = pl.multiple_of(slot * tokens, tokens)
    return jnp.concatenate([a_ref[x, half, pl.ds(start, tokens), :] for x in range(chips) for half in range(halves)], axis=1)


def project_kernel(place_ref, a_ref, w_ref, own_ref, other_ref):
    core = place_ref[2]
    own_ref[...] = mm(token_rows(a_ref, core), w_ref[...], NT)
    other_ref[...] = mm(token_rows(a_ref, 1 - core), w_ref[...], NT).astype(BF16)


def project(place, a, weights):
    chips, halves, rows, width = a.shape
    features, columns = weights.shape
    tokens = rows // 2
    block = 256
    return pl.pallas_call(
        project_kernel,
        grid=(features // block,),
        out_shape=(jax.ShapeDtypeStruct((tokens, features), F32), jax.ShapeDtypeStruct((tokens, features), BF16)),
        in_specs=[
            SMEM,
            pl.BlockSpec(a.shape, lambda i: (0, 0, 0, 0)),
            pl.BlockSpec((block, columns), lambda i: (i, 0)),
        ],
        out_specs=(pl.BlockSpec((tokens, block), lambda i: (0, i)), pl.BlockSpec((tokens, block), lambda i: (0, i))),
        compiler_params=pltpu.CompilerParams(vmem_limit_bytes=24 * MIB),
        cost_estimate=cost(4 * tokens * features * columns, 8 * MIB),
        name="project",
    )(place, a, weights)


def grad_weight_kernel(side, place_ref, own_ref, other_ref, a_ref, *out_refs):
    core, y, z = place_ref[2], place_ref[3], place_ref[4]
    rows = out_refs[0].shape[1]
    a_own = token_rows(a_ref, core)
    a_other = token_rows(a_ref, 1 - core)
    half = a_own.shape[1] // 2
    for ky in range(side):
        for kz in range(side):
            row = lax.rem(y + ky, side) * side + lax.rem(z + kz, side)
            start = pl.multiple_of(row * rows, rows)
            part = mm(own_ref[:, pl.ds(start, rows)], a_own, TN) + mm(other_ref[:, pl.ds(start, rows)], a_other, TN)
            out_refs[kz][ky] = part[:, :half].astype(BF16)
            out_refs[side + ky][kz] = part[:, half:].astype(BF16)


def grad_weight_parts(place, own, other, a, side):
    tokens, features = own.shape
    columns = a.shape[0] * a.shape[1] * a.shape[3]
    rows = features // side**2
    return pl.pallas_call(
        functools.partial(grad_weight_kernel, side),
        out_shape=(jax.ShapeDtypeStruct((side, rows, columns // 2), BF16),) * (2 * side),
        in_specs=[SMEM] + [VMEM] * 3,
        out_specs=(VMEM,) * (2 * side),
        compiler_params=pltpu.CompilerParams(vmem_limit_bytes=32 * MIB),
        cost_estimate=cost(4 * tokens * features * columns, 7 * MIB),
        name="grad_weight_parts",
    )(place, own, other, a)


def summed(parts):
    total = parts[0].astype(F32)
    for part in parts[1:]:
        total = total + part.astype(F32)
    return total


def per_device(queries, key_states, value_states, grad_output, out_weight, key_tiles, tile_count):
    seq = lax.axis_size("seq")
    ranks = lax.axis_size("dp")
    side = math.isqrt(ranks)
    chips = seq // 2
    s_index = lax.axis_index("seq")
    d_index = lax.axis_index("dp")
    core = lax.rem(s_index, 2)
    tokens, columns = queries.shape[1:]
    heads, units, width = key_tiles.shape[1:]
    head_dim = columns // heads
    rows = out_weight.shape[0]
    place = jnp.stack([s_index, jnp.int32(seq), core, lax.div(d_index, side), lax.rem(d_index, side)]).astype(jnp.int32)
    lists = key_tiles.reshape(-1)
    counts = tile_count.reshape(-1)
    same_core = [list(range(c, seq, 2)) for c in range(2)]
    across = [(i, i ^ 1) for i in range(seq)]

    def y_shift(k):
        return [(i, (i // side + k) % side * side + i % side) for i in range(ranks)]

    def z_shift(k):
        return [(i, i // side * side + (i % side + k) % side) for i in range(ranks)]

    def x_swap(k):
        return [(i, i ^ (2 * k)) for i in range(seq)]

    def over_chips(values):
        return lax.all_to_all(values, "seq", split_axis=0, concat_axis=0, tiled=True, axis_index_groups=same_core)

    by_core = out_weight.reshape(rows, 2, chips, 2, head_dim)
    half_shard = lax.dynamic_index_in_dim(by_core, core, axis=3, keepdims=False)
    half_shard = half_shard.transpose(0, 2, 1, 3).reshape(rows, columns // 2)
    weights = lax.all_gather(half_shard, "dp", axis=0, tiled=True)

    qkv = lax.all_to_all(pack(queries, key_states, value_states, seq, head_dim), "seq", split_axis=0, concat_axis=0, tiled=True)
    own_rows = grad_output[0]
    other_rows = lax.ppermute(own_rows, "seq", across)
    g = over_chips(grad_attn(place, own_rows, other_rows, weights, chips))
    a, lse = attention_forward(place, lists, counts, qkv, chips, width)
    a_home = over_chips(a)
    grads = attention_backward(place, lists, counts, qkv, g, a, lse, width)
    parts = grad_weight_parts(place, own_rows, other_rows, a_home, side)
    grads_home = lax.all_to_all(grads, "seq", split_axis=0, concat_axis=0, tiled=True)

    z_first = [parts[0]] + [lax.ppermute(parts[k], "dp", z_shift(k)) for k in range(1, side)]
    y_first = [parts[side]] + [lax.ppermute(parts[side + k], "dp", y_shift(k)) for k in range(1, side)]
    out_own, out_other = project(place, a_home, weights)
    output = (out_own + lax.ppermute(out_other, "seq", across).astype(F32)).astype(BF16)
    z_sum = summed(z_first).astype(BF16)
    y_sum = summed(y_first).astype(BF16)
    z_done = summed([z_sum[0]] + [lax.ppermute(z_sum[k], "dp", y_shift(k)) for k in range(1, side)])
    y_done = summed([y_sum[0]] + [lax.ppermute(y_sum[k], "dp", z_shift(k)) for k in range(1, side)])
    chip_share = jnp.concatenate([z_done, y_done], axis=1).astype(BF16)
    by_chip = [chip_share] + [lax.ppermute(chip_share, "seq", x_swap(k)) for k in range(1, chips)]
    while len(by_chip) > 1:
        by_chip = [summed(by_chip[i : i + 2]) for i in range(0, len(by_chip), 2)]
    own_half = by_chip[0].astype(BF16)
    other_half = lax.ppermute(own_half, "seq", across)
    even = jnp.where(core == 0, own_half, other_half).reshape(rows, chips, 2, head_dim)
    odd = jnp.where(core == 0, other_half, own_half).reshape(rows, chips, 2, head_dim)
    grad_weight = jnp.stack([even, odd], axis=2).transpose(0, 3, 1, 2, 4).reshape(rows, columns).astype(F32)

    grad_query, grad_key, grad_value = unpack(grads_home)
    return output[None], grad_query, grad_key, grad_value, grad_weight


def solution(mesh):
    in_specs = (
        P("dp", "seq", None),
        P("dp", "seq", None),
        P("dp", "seq", None),
        P("dp", "seq", None),
        P("dp", None),
        P("dp", None, None, None),
        P("dp", None, None),
    )
    out_specs = (
        P("dp", "seq", None),
        P("dp", "seq", None),
        P("dp", "seq", None),
        P("dp", "seq", None),
        P("dp", None),
    )
    return jax.shard_map(per_device, mesh=mesh, in_specs=in_specs, out_specs=out_specs, check_vma=False)
```

time: 1190 us -> 438 us (0.37)
  waiting for transfers between devices: 692 us -> 84.3 us
  Pallas kernels: 0 us -> 255 us
  other arithmetic: 157 us -> 10.5 us
  matrix products: 117 us -> 0 us
  local copies, waits for them, and re-layouts: 120 us -> 24.8 us
  blocking collectives: 35.5 us -> 0 us
  loops' own time: 14.9 us -> 0 us
  starting transfers between devices: 34.3 us -> 48.1 us
    reduce_scatter x1 -> x0, waiting for transfers between devices: 591 us -> none  [per_device(): lax.psum_scatter(lax.dot_general(picked, attention, (((0,), (0,)), ((), (...]
    pallas_call x0 -> x7, Pallas kernels: none -> 255 us  [the longest x1 96.8 us: pack(): pl.pallas_call(pack_kernel, out_shape=jax.ShapeDtypeStruct((seq, 3, halve...]
    scatter-add x10 -> x0, other arithmetic: 122 us -> none  [the longest x2 30 us: tile_attention(): grad_value = jax.ops.segment_sum(value_parts, pair_tile, table_size)]
    dot_general x15 -> x0, matrix products: 117 us -> none  [the longest x2 18.6 us: tile_attention(): jnp.einsum('prs,psd->prd', probabilities.astype(jnp.bfloat16), v_pair, pr...]
    ppermute x0 -> x18, waiting for transfers between devices: none -> 32.9 us  [the longest x3 24.4 us: per_device(): lax.ppermute(chip_share, 'seq', x_swap(k))]
    gather x18 -> x0, local copies, waits for them, and re-layouts: 29.6 us -> none  [the longest x2 5.88 us: tile_attention(): q_pair = q_units[pair_unit]]
    all_gather x1, waiting for transfers between devices: 28.2 us -> 0.01 us  [per_device(): weights = lax.all_gather(half_shard, 'dp', axis=0, tiled=True)]
    ppermute x0 -> x18, starting transfers between devices: none -> 26.5 us  [the longest x3 5.68 us: per_device(): lax.ppermute(parts[k], 'dp', z_shift(k))]
  transfers between devices with their start and end apart: 9 -> 23, of which waited for: 8 -> 10; matrix products, arithmetic and copies ran while one was open for 4% -> 4% of each run, Pallas kernels for 0% -> 36%
where the time goes in v1:
time: 438 us; the launch traced here: 437 us
  Pallas kernels  255 us (58%)
  waiting for transfers between devices  84.3 us (19%)
  starting transfers between devices  48.1 us (11%)
  local copies, waits for them, and re-layouts  24.8 us (6%)
  between operations  14.3 us (3%)
  other arithmetic  10.5 us (2%)
    pallas_call x1, Pallas kernels, pack(): pl.pallas_call(pack_kernel, out_shape=jax.ShapeDtypeStruct((seq, 3, halve...  96.8 us
    pallas_call x1, Pallas kernels, unpack(): pl.pallas_call(unpack_kernel, out_shape=(jax.ShapeDtypeStruct((1, tokens,...  96.8 us
    all_to_all x1, waiting for transfers between devices, per_device(): lax.all_to_all(pack(queries, key_states, value_states, seq, head_dim), 's...  37 us
    pallas_call x1, Pallas kernels, attention_backward(): pl.pallas_call(functools.partial(backward_kernel, slots, units, width, 1....  31.9 us
    ppermute x3, waiting for transfers between devices, per_device(): lax.ppermute(chip_share, 'seq', x_swap(k))  24.4 us
    pallas_call x1, Pallas kernels, attention_forward(): pl.pallas_call(functools.partial(forward_kernel, slots, units, width, 1.0...  14.8 us
    all_to_all x2, waiting for transfers between devices, over_chips(): lax.all_to_all(values, 'seq', split_axis=0, concat_axis=0, tiled=True, ax...  14.3 us
    unnamed x35, local copies, waits for them, and re-layouts  12.9 us
  transfers between devices with their start and end apart: 23, of which 10 were waited for; matrix products, arithmetic and copies ran while one was open for 4% of the time, Pallas kernels for 36%

profile of v1, /device:TPU:1, one launch (start us, length us, event | category | flops | bytes accessed | tf_op | source)
XLA Modules:
  0.0 437.2 jit_solution(10449488692413380939)
XLA Ops:
  7.2 1.4 reshape.31
  8.6 0.5 constant_dynamic-slice_fusion
  9.5 0.9 reshape.32
  10.4 96.8 %pack_heads.1 = bf16[8,3,2,256,128]{4,3,2,1,0:T(8,128)(2,1)} custom-call(bf16[1,256,2048]{2,1,0:T(8,128)(2,1)} %q_ref.1, bf16[1,256,2048]{2,1,0:T(8,128)(2,1)} %k_ref.1, bf16[1,256,2048]{2,1,0:T(8,128)(2,1)} %v_ref.1), custom_call_target="tpu_custom_call" | custom-call | bytes 6291456 | tf_op jit(solution)/shard_map/pack_heads/pallas_call | solution.py:48
  107.2 5.9 %all-to-all-start = ((bf16[8,3,2,256,128]{4,3,2,1,0:T(8,128)(2,1)}), bf16[8,3,2,256,128]{4,3,2,1,0:T(8,128)(2,1)S(1)}, u32[]{:S(2)}, u32[]{:S(2)}) async-start(bf16[8,3,2,256,128]{4,3,2,1,0:T(8,128)(2,1)} %pack_heads.1), calls=%async_computation | async-start | bytes 6291456 | tf_op jit(solution)/shard_map/all_to_all | solution.py:374
  113.7 37.0 %all-to-all-done.qkv_ref = bf16[8,3,2,256,128]{4,3,2,1,0:T(8,128)(2,1)S(1)} async-done(((bf16[8,3,2,256,128]{4,3,2,1,0:T(8,128)(2,1)}), bf16[8,3,2,256,128]{4,3,2,1,0:T(8,128)(2,1)S(1)}, u32[]{:S(2)}, u32[]{:S(2)}) %all-to-all-start) | async-done | bytes 3145760 | tf_op jit(solution)/shard_map/all_to_all | solution.py:374
  150.7 14.8 %attention_forward.1 = (bf16[4,2,512,128]{3,2,1,0:T(8,128)(2,1)S(1)}, f32[32,8,128]{2,1,0:T(8,128)S(1)}) custom-call(s32[5]{0:T(128)S(1)} %stack.22.place_ref, s32[1792]{0:T(1024)S(1)} %reshape.29.tiles_ref, s32[256]{0:T(256)S(1)} %reshape.30.counts_ref, bf16[8,3,2,256,128]{4,3,2,1,0:T(8,128)(2,1)S(1)} %all-to-all-done.qkv_ref), custom_call_target="tpu_custom_call" | custom-call | flops 4294967296 | bytes 5242880 | tf_op jit(solution)/shard_map/attention_forward/pallas_call | solution.py:152
  165.6 1.0 copy-done
  166.5 4.3 all-to-all-start.1
  170.8 14.3 %all-to-all-done.1.a_ref = bf16[4,2,512,128]{3,2,1,0:T(8,128)(2,1)} async-done(((bf16[4,2,512,128]{3,2,1,0:T(8,128)(2,1)}), bf16[4,2,512,128]{3,2,1,0:T(8,128)(2,1)}, u32[]{:S(2)}, u32[]{:S(2)}) %all-to-all-start.1) | async-done | bytes 1048608 | tf_op jit(solution)/shard_map/all_to_all | solution.py:367
  185.1 1.2 copy-done.8
  186.4 4.8 %grad_weight_parts.1 = (bf16[4,128,512]{2,1,0:T(8,128)(2,1)S(1)}, bf16[4,128,512]{2,1,0:T(8,128)(2,1)}, bf16[4,128,512]{2,1,0:T(8,128)(2,1)}, bf16[4,128,512]{2,...) custom-call(s32[5]{0:T(128)S(1)} %stack.22.place_ref, ...), custom_call_target="tpu_custom_call" | custom-call | flops 2147483648 | bytes 7340032 | tf_op jit(solution)/shard_map/grad_weight_parts/pallas_call | solution.py:321
  191.2 0.8 copy-done.3
  192.0 0.8 copy-done.5
  192.8 0.8 copy-done.10
  193.6 0.8 copy-done.11
  194.5 0.8 copy-done.12
  195.3 1.7 collective-permute-start.2
  196.9 3.3 collective-permute-start.3
  200.2 0.7 collective-permute-start.4
  201.0 2.2 copy-done.6
  203.2 1.2 copy-done.9
  204.4 4.6 %grad_attn.1 = bf16[4,2,512,128]{3,2,1,0:T(8,128)(2,1)S(1)} custom-call(s32[5]{0:T(128)S(1)} %stack.22.place_ref, bf16[256,2048]{1,0:T(8,128)(2,1)S(1)} %bitcast.40, bf16[256,2048]{1,0:T(8,128)(2,1)} %collective-permute-done.1.other_ref, bf16[2048,1024]{1,0:T(8,128)(2,1)S(1)} %copy-done.6), custom_call_target="tpu_custom_call" | custom-call | flops 2147483648 | bytes 7340032 | tf_op jit(solution)/shard_map/grad_attn/pallas_call | solution.py:251
  209.0 1.0 copy-done.2
  210.0 4.3 all-to-all-start.2
  214.2 1.4 collective-permute-start.8
  215.6 2.6 collective-permute-start.9
  218.2 1.1 collective-permute-start.10
  219.3 2.7 collective-permute-done.3
  222.0 0.6 collective-permute-done.4
  222.5 1.8 add_convert_fusion.2
  224.3 0.8 copy-done.13
  225.1 0.7 slice_bitcast_fusion.6
  225.9 1.3 collective-permute-start.5
  227.2 1.4 collective-permute-start.7
  228.6 1.2 copy-done.1
  229.8 31.9 %attention_backward.1 = bf16[8,3,2,256,128]{4,3,2,1,0:T(8,128)(2,1)} custom-call(s32[5]{0:T(128)S(1)} %stack.22.place_ref, s32[1792]{0:T(1024)S(1)} %reshape.29.tiles_ref, s32[256]{0:T(256)S(1)} %reshape.30.counts_ref, bf16[8,3,2,256,128]{4,3,2,1,0:T(8,128)(2,1)S(1)} %all-to-all-done.qkv_ref, bf16[4,2,512,128]{3,2,1,0:T(8,128)(2,1)} %all-to-all-done.2.g_ref, ...), custom_call_target="tpu_custom_call" | custom-call | flops 9663676416 | bytes 9437184 | tf_op jit(solution)/shard_map/attention_backward/pallas_call | solution.py:220
  261.7 7.1 %all-to-all-start.3 = ((bf16[8,3,2,256,128]{4,3,2,1,0:T(8,128)(2,1)}), bf16[8,3,2,256,128]{4,3,2,1,0:T(8,128)(2,1)}, u32[]{:S(2)}, u32[]{:S(2)}) async-start(bf16[8,3,2,256,128]{4,3,2,1,0:T(8,128)(2,1)} %attention_backward.1), calls=%async_computation.3 | async-start | bytes 6291456 | tf_op jit(solution)/shard_map/all_to_all | solution.py:382
  268.9 2.1 collective-permute-start.6
  271.0 1.6 add_convert_fusion.1
  272.7 1.0 collective-permute-start.11
  273.7 1.9 collective-permute-start.13
  275.6 0.7 collective-permute-start.12
  276.3 1.0 fusion.6
  277.3 1.6 collective-permute-done.11
  278.9 2.4 collective-permute-done.12
  281.4 2.6 collective-permute-start.15
  284.0 0.3 collective-permute-start.14
  284.3 0.6 collective-permute-start.16
  284.9 5.3 %project.1 = (f32[256,2048]{1,0:T(8,128)S(1)}, bf16[256,2048]{1,0:T(8,128)(2,1)S(1)}) custom-call(s32[5]{0:T(128)S(1)} %stack.22.place_ref, bf16[4,2,512,128]{3,2,1,0:T(8,128)(2,1)} %all-to-all-done.1.a_ref, bf16[2048,1024]{1,0:T(8,128)(2,1)S(1)} %copy-done.7), custom_call_target="tpu_custom_call" | custom-call | flops 2147483648 | bytes 8388608 | tf_op jit(solution)/shard_map/project/pallas_call | solution.py:286
  290.2 3.0 collective-permute-start
  293.2 18.9 %collective-permute-done.15 = bf16[128,1024]{1,0:T(8,128)(2,1)S(1)} collective-permute-done((bf16[128,1024]{1,0:T(8,128)(2,1)S(1)}, bf16[128,1024]{1,0:T(8,128)(2,1)S(1)}, u32[]{:S(2)}, u32[]{:S(2)}) %collective-permute-start.15) | collective-permute-done | bytes 262176 | tf_op jit(solution)/shard_map/ppermute | solution.py:393
  312.1 4.1 collective-permute-done.14
  316.2 1.4 collective-permute-done.16
  317.7 0.8 collective-permute-start.17
  318.5 1.3 collective-permute-done.17
  319.8 1.8 broadcast_select_fusion.1
  321.6 1.1 stack_reshape.6
  322.7 1.8 stack_reshape.7
  324.5 1.6 convert_bitcast_fusion
  326.2 1.8 copy.16
  327.9 3.0 reshape.35
  331.0 2.5 fusion
  333.5 96.8 %unpack_heads.1 = (bf16[1,256,2048]{2,1,0:T(8,128)(2,1)}, bf16[1,256,2048]{2,1,0:T(8,128)(2,1)}, bf16[1,256,2048]{2,1,0:T(8,128)(2,1)}) custom-call(bf16[8,3,2,256,128]{4,3,2,1,0:T(8,128)(2,1)} %all-to-all-done.3.in_ref), custom_call_target="tpu_custom_call" | custom-call | bytes 6291456 | tf_op jit(solution)/shard_map/unpack_heads/pallas_call | solution.py:76
  (47 shorter events, 1.2 us)
Async XLA Ops:
  7.2 193.8 %all-gather.2.cloned.1.call-start = ((), (), s32[]{:S(2)}) async-start(), calls=%async_computation.4 | async-start | bytes 4456448 | tf_op jit(solution)/shard_map/all_gather | solution.py:372
  107.2 6.0 %copy-start.16 = (s32[1,16,16]{2,1,0:T(8,128)S(1)}, s32[1,16,16]{2,1,0:T(8,128)}, u32[]{:S(2)}) copy-start(s32[1,16,16]{2,1,0:T(8,128)} %param.13) | copy-start | bytes 3076
  107.2 6.0 %copy-start.15 = (s32[1,16,16,7]{2,1,3,0:T(8,128)S(1)}, s32[1,16,16,7]{2,1,3,0:T(8,128)}, u32[]{:S(2)}) copy-start(s32[1,16,16,7]{2,1,3,0:T(8,128)} %param.12) | copy-start | bytes 21508
  107.2 43.5 %all-to-all-start = ((bf16[8,3,2,256,128]{4,3,2,1,0:T(8,128)(2,1)}), bf16[8,3,2,256,128]{4,3,2,1,0:T(8,128)(2,1)S(1)}, u32[]{:S(2)}, u32[]{:S(2)}) async-start(bf16[8,3,2,256,128]{4,3,2,1,0:T(8,128)(2,1)} %pack_heads.1), calls=%async_computation | async-start | bytes 6291456 | tf_op jit(solution)/shard_map/all_to_all | solution.py:374
  113.2 57.6 %collective-permute-start.1 = (bf16[256,2048]{1,0:T(8,128)(2,1)}, bf16[256,2048]{1,0:T(8,128)(2,1)}, u32[]{:S(2)}, u32[]{:S(2)}) collective-permute-start(bf16[256,2048]{1,0:T(8,128)(2,1)} %bitcast.38), channel_id=1, source_target_pairs={{0,1},{1,0},{2,3},{3,2},{4,5},{5,4},{6,7},{7,6},{8,9},{9,8},{10,11... | collective-permute-start | bytes 3145736 | tf_op jit(solution)/shard_map/ppermute | solution.py:376
  165.6 1.0 copy-start
  166.5 18.6 %all-to-all-start.1 = ((bf16[4,2,512,128]{3,2,1,0:T(8,128)(2,1)}), bf16[4,2,512,128]{3,2,1,0:T(8,128)(2,1)}, u32[]{:S(2)}, u32[]{:S(2)}) async-start(bf16[4,2,512,128]{3,2,1,0:T(8,128)(2,1)} %copy-done), calls=%async_computation.1 | async-start | bytes 2097152 | tf_op jit(solution)/shard_map/all_to_all | solution.py:367
  185.1 1.2 copy-start.8
  191.2 0.8 copy-start.3
  192.0 0.8 copy-start.5
  192.8 0.8 copy-start.10
  193.6 0.8 copy-start.11
  194.5 0.8 copy-start.12
  195.3 23.0 %collective-permute-start.2 = (bf16[4,128,512]{2,1,0:T(8,128)(2,1)}, bf16[4,128,512]{2,1,0:T(8,128)(2,1)}, u32[]{:S(2)}, u32[]{:S(2)}) collective-permute-start(bf16[4,128,512]{2,1,0:T(8,128)(2,1)} %get-tuple-element.28), channel_id=1, source_target_pairs={{0,8},{8,16},{16,24},{24,0},{32,40},{40,48},{48,56},{56,32},{64,72... | collective-permute-start | bytes 1572872 | tf_op jit(solution)/shard_map/ppermute | solution.py:384
  196.9 25.1 %collective-permute-start.3 = (bf16[4,128,512]{2,1,0:T(8,128)(2,1)}, bf16[4,128,512]{2,1,0:T(8,128)(2,1)}, u32[]{:S(2)}, u32[]{:S(2)}) collective-permute-start(bf16[4,128,512]{2,1,0:T(8,128)(2,1)} %get-tuple-element.29), channel_id=1, source_target_pairs={{0,16},{8,24},{16,0},{24,8},{32,48},{40,56},{48,32},{56,40},{64,80... | collective-permute-start | bytes 1572872 | tf_op jit(solution)/shard_map/ppermute | solution.py:384
  200.2 22.3 %collective-permute-start.4 = (bf16[4,128,512]{2,1,0:T(8,128)(2,1)}, bf16[4,128,512]{2,1,0:T(8,128)(2,1)}, u32[]{:S(2)}, u32[]{:S(2)}) collective-permute-start(bf16[4,128,512]{2,1,0:T(8,128)(2,1)} %get-tuple-element.30), channel_id=1, source_target_pairs={{0,24},{8,0},{16,8},{24,16},{32,56},{40,32},{48,40},{56,48},{64,88... | collective-permute-start | bytes 1572872 | tf_op jit(solution)/shard_map/ppermute | solution.py:384
  201.0 2.2 copy-start.6
  203.2 1.2 copy-start.9
  209.0 1.0 copy-start.2
  210.0 18.6 %all-to-all-start.2 = ((bf16[4,2,512,128]{3,2,1,0:T(8,128)(2,1)}), bf16[4,2,512,128]{3,2,1,0:T(8,128)(2,1)}, u32[]{:S(2)}, u32[]{:S(2)}) async-start(bf16[4,2,512,128]{3,2,1,0:T(8,128)(2,1)} %copy-done.2), calls=%async_computation.2 | async-start | bytes 2097152 | tf_op jit(solution)/shard_map/all_to_all | solution.py:367
  214.2 54.6 %collective-permute-start.8 = (bf16[4,128,512]{2,1,0:T(8,128)(2,1)}, bf16[4,128,512]{2,1,0:T(8,128)(2,1)}, u32[]{:S(2)}, u32[]{:S(2)}) collective-permute-start(bf16[4,128,512]{2,1,0:T(8,128)(2,1)} %copy-done.12), channel_id=1, source_target_pairs={{0,32},{8,40},{16,48},{24,56},{32,64},{40,72},{48,80},{56,88},{64,... | collective-permute-start | bytes 1572872 | tf_op jit(solution)/shard_map/ppermute | solution.py:385
  215.6 55.4 %collective-permute-start.9 = (bf16[4,128,512]{2,1,0:T(8,128)(2,1)}, bf16[4,128,512]{2,1,0:T(8,128)(2,1)}, u32[]{:S(2)}, u32[]{:S(2)}) collective-permute-start(bf16[4,128,512]{2,1,0:T(8,128)(2,1)} %copy-done.11), channel_id=1, source_target_pairs={{0,64},{8,72},{16,80},{24,88},{32,96},{40,104},{48,112},{56,120},{... | collective-permute-start | bytes 1572872 | tf_op jit(solution)/shard_map/ppermute | solution.py:385
  218.2 52.8 %collective-permute-start.10 = (bf16[4,128,512]{2,1,0:T(8,128)(2,1)}, bf16[4,128,512]{2,1,0:T(8,128)(2,1)}, u32[]{:S(2)}, u32[]{:S(2)}) collective-permute-start(bf16[4,128,512]{2,1,0:T(8,128)(2,1)} %copy-done.10), channel_id=1, source_target_pairs={{0,96},{8,104},{16,112},{24,120},{32,0},{40,8},{48,16},{56,24},{64... | collective-permute-start | bytes 1572872 | tf_op jit(solution)/shard_map/ppermute | solution.py:385
  224.3 0.8 copy-start.13
  225.9 49.8 %collective-permute-start.5 = (bf16[128,512]{1,0:T(8,128)(2,1)}, bf16[128,512]{1,0:T(8,128)(2,1)S(1)}, u32[]{:S(2)}, u32[]{:S(2)}) collective-permute-start(bf16[128,512]{1,0:T(8,128)(2,1)} %get-tuple-element.37), channel_id=1, source_target_pairs={{0,32},{8,40},{16,48},{24,56},{32,64},{40,72},{48,80},{56,88},{64,... | collective-permute-start | bytes 393224 | tf_op jit(solution)/shard_map/ppermute | solution.py:390
  227.2 49.2 %collective-permute-start.7 = (bf16[128,512]{1,0:T(8,128)(2,1)}, bf16[128,512]{1,0:T(8,128)(2,1)S(1)}, u32[]{:S(2)}, u32[]{:S(2)}) collective-permute-start(bf16[128,512]{1,0:T(8,128)(2,1)} %get-tuple-element.38), channel_id=1, source_target_pairs={{0,96},{8,104},{16,112},{24,120},{32,0},{40,8},{48,16},{56,24},{64... | collective-permute-start | bytes 393224 | tf_op jit(solution)/shard_map/ppermute | solution.py:390
  228.6 1.2 copy-start.1
  261.7 7.1 %copy-start.14 = (bf16[128,512]{1,0:T(8,128)(2,1)S(1)}, bf16[128,512]{1,0:T(8,128)(2,1)}, u32[]{:S(2)}) copy-start(bf16[128,512]{1,0:T(8,128)(2,1)} %get-tuple-element.39) | copy-start | bytes 393220
  261.7 9.3 %copy-start.4 = (bf16[4,128,512]{2,1,0:T(8,128)(2,1)S(1)}, bf16[4,128,512]{2,1,0:T(8,128)(2,1)}, u32[]{:S(2)}) copy-start(bf16[4,128,512]{2,1,0:T(8,128)(2,1)} %copy-done.3) | copy-start | bytes 1572868
  261.7 71.7 %all-to-all-start.3 = ((bf16[8,3,2,256,128]{4,3,2,1,0:T(8,128)(2,1)}), bf16[8,3,2,256,128]{4,3,2,1,0:T(8,128)(2,1)}, u32[]{:S(2)}, u32[]{:S(2)}) async-start(bf16[8,3,2,256,128]{4,3,2,1,0:T(8,128)(2,1)} %attention_backward.1), calls=%async_computation.3 | async-start | bytes 6291456 | tf_op jit(solution)/shard_map/all_to_all | solution.py:382
  268.9 16.0 %copy-start.7 = (bf16[2048,1024]{1,0:T(8,128)(2,1)S(1)}, bf16[2048,1024]{1,0:T(8,128)(2,1)}, u32[]{:S(2)}) copy-start(bf16[2048,1024]{1,0:T(8,128)(2,1)} %all-gather.2.cloned.1.call-done.w_ref) | copy-start | bytes 12582916
  268.9 7.4 %collective-permute-start.6 = (bf16[128,512]{1,0:T(8,128)(2,1)S(1)}, bf16[128,512]{1,0:T(8,128)(2,1)S(1)}, u32[]{:S(2)}, u32[]{:S(2)}) collective-permute-start(bf16[128,512]{1,0:T(8,128)(2,1)S(1)} %copy-done.14), channel_id=1, source_target_pairs={{0,64},{8,72},{16,80},{24,88},{32,96},{40,104},{48,112},{56,120},{... | collective-permute-start | bytes 393224 | tf_op jit(solution)/shard_map/ppermute | solution.py:390
  272.7 6.2 %collective-permute-start.11 = (bf16[128,512]{1,0:T(8,128)(2,1)S(1)}, bf16[128,512]{1,0:T(8,128)(2,1)S(1)}, u32[]{:S(2)}, u32[]{:S(2)}) collective-permute-start(bf16[128,512]{1,0:T(8,128)(2,1)S(1)} %get-tuple-element.40), channel_id=1, source_target_pairs={{0,8},{8,16},{16,24},{24,0},{32,40},{40,48},{48,56},{56,32},{64,72... | collective-permute-start | bytes 393224 | tf_op jit(solution)/shard_map/ppermute | solution.py:391
  273.7 5.2 %collective-permute-start.13 = (bf16[128,512]{1,0:T(8,128)(2,1)S(1)}, bf16[128,512]{1,0:T(8,128)(2,1)S(1)}, u32[]{:S(2)}, u32[]{:S(2)}) collective-permute-start(bf16[128,512]{1,0:T(8,128)(2,1)S(1)} %get-tuple-element.41), channel_id=1, source_target_pairs={{0,24},{8,0},{16,8},{24,16},{32,56},{40,32},{48,40},{56,48},{64,88... | collective-permute-start | bytes 393224 | tf_op jit(solution)/shard_map/ppermute | solution.py:391
  275.6 5.7 %collective-permute-start.12 = (bf16[128,512]{1,0:T(8,128)(2,1)S(1)}, bf16[128,512]{1,0:T(8,128)(2,1)S(1)}, u32[]{:S(2)}, u32[]{:S(2)}) collective-permute-start(bf16[128,512]{1,0:T(8,128)(2,1)S(1)} %get-tuple-element.42), channel_id=1, source_target_pairs={{0,16},{8,24},{16,0},{24,8},{32,48},{40,56},{48,32},{56,40},{64,80... | collective-permute-start | bytes 393224 | tf_op jit(solution)/shard_map/ppermute | solution.py:391
  281.4 30.7 %collective-permute-start.15 = (bf16[128,1024]{1,0:T(8,128)(2,1)S(1)}, bf16[128,1024]{1,0:T(8,128)(2,1)S(1)}, u32[]{:S(2)}, u32[]{:S(2)}) collective-permute-start(bf16[128,1024]{1,0:T(8,128)(2,1)S(1)} %pad_maximum_fusion), channel_id=1, source_target_pairs={{0,4},{1,5},{2,6},{3,7},{4,0},{5,1},{6,2},{7,3},{8,12},{9,13},{10,... | collective-permute-start | bytes 786440 | tf_op jit(solution)/shard_map/ppermute | solution.py:393
  284.0 32.2 %collective-permute-start.14 = (bf16[128,1024]{1,0:T(8,128)(2,1)S(1)}, bf16[128,1024]{1,0:T(8,128)(2,1)S(1)}, u32[]{:S(2)}, u32[]{:S(2)}) collective-permute-start(bf16[128,1024]{1,0:T(8,128)(2,1)S(1)} %pad_maximum_fusion), channel_id=1, source_target_pairs={{0,2},{1,3},{2,0},{3,1},{4,6},{5,7},{6,4},{7,5},{8,10},{9,11},{10,... | collective-permute-start | bytes 786440 | tf_op jit(solution)/shard_map/ppermute | solution.py:393
  284.3 33.2 %collective-permute-start.16 = (bf16[128,1024]{1,0:T(8,128)(2,1)S(1)}, bf16[128,1024]{1,0:T(8,128)(2,1)S(1)}, u32[]{:S(2)}, u32[]{:S(2)}) collective-permute-start(bf16[128,1024]{1,0:T(8,128)(2,1)S(1)} %pad_maximum_fusion), channel_id=1, source_target_pairs={{0,6},{1,7},{2,4},{3,5},{4,2},{5,3},{6,0},{7,1},{8,14},{9,15},{10,... | collective-permute-start | bytes 786440 | tf_op jit(solution)/shard_map/ppermute | solution.py:393
  290.2 40.7 %collective-permute-start = (bf16[256,2048]{1,0:T(8,128)(2,1)S(1)}, bf16[256,2048]{1,0:T(8,128)(2,1)}, u32[]{:S(2)}, u32[]{:S(2)}) collective-permute-start(bf16[256,2048]{1,0:T(8,128)(2,1)S(1)} %get-tuple-element.22), channel_id=1, source_target_pairs={{0,1},{1,0},{2,3},{3,2},{4,5},{5,4},{6,7},{7,6},{8,9},{9,8},{10,11... | collective-permute-start | bytes 3145736 | tf_op jit(solution)/shard_map/ppermute | solution.py:387
  317.7 2.1 collective-permute-start.17
Sparse Core Ops, SparseCore 0:
  10.7 54.8 all-gather.1

commit v2 on v1

v2 whole, which is shorter than its diff:
```python
import functools
import math

import jax
import jax.numpy as jnp
from jax import lax
from jax.experimental import pallas as pl
from jax.experimental.pallas import tpu as pltpu
from jax.sharding import PartitionSpec as P

NN = (((1,), (0,)), ((), ()))
NT = (((1,), (1,)), ((), ()))
TN = (((0,), (0,)), ((), ()))
F32 = jnp.float32
BF16 = jnp.bfloat16
MIB = 2**20
SMEM = pl.BlockSpec(memory_space=pltpu.SMEM)
VMEM = pl.BlockSpec(memory_space=pltpu.VMEM)
ANY = pl.BlockSpec(memory_space=pl.ANY)
HBM = pl.BlockSpec(memory_space=pltpu.HBM)
TILE = 128
UNITS_AT_ONCE = 4
VMEM_LIMIT = 60 * MIB


def mm(a, b, dims=NN):
    return lax.dot_general(a, b, dims, preferred_element_type=F32)


def cost(flops, moved, exps=0):
    return pl.CostEstimate(flops=flops, bytes_accessed=moved, transcendentals=exps)


def pack_kernel(q_ref, k_ref, v_ref, out_ref):
    seq, _, halves, _, width = out_ref.shape
    for n, ref in enumerate((q_ref, k_ref, v_ref)):
        for s in range(seq):
            for half in range(halves):
                column = (s + seq * half) * width
                out_ref[s, n, half] = ref[0, :, column : column + width]


def pack(q, k, v, seq, head_dim):
    _, tokens, columns = q.shape
    halves = columns // (seq * head_dim)
    rows = tokens // 4
    return pl.pallas_call(
        pack_kernel,
        grid=(tokens // rows,),
        out_shape=jax.ShapeDtypeStruct((seq, 3, halves, tokens, head_dim), q.dtype),
        in_specs=[pl.BlockSpec((1, rows, columns), lambda i: (0, i, 0))] * 3,
        out_specs=pl.BlockSpec((seq, 3, halves, rows, head_dim), lambda i: (0, 0, 0, i, 0)),
        compiler_params=pltpu.CompilerParams(vmem_limit_bytes=VMEM_LIMIT),
        cost_estimate=cost(0, 12 * tokens * columns),
        name="pack_heads",
    )(q, k, v)


def unpack_kernel(in_ref, q_ref, k_ref, v_ref):
    seq, _, halves, _, width = in_ref.shape
    for n, ref in enumerate((q_ref, k_ref, v_ref)):
        for s in range(seq):
            for half in range(halves):
                column = (s + seq * half) * width
                ref[0, :, column : column + width] = in_ref[s, n, half]


def unpack(blocks):
    seq, _, halves, tokens, head_dim = blocks.shape
    columns = seq * halves * head_dim
    rows = tokens // 4
    return pl.pallas_call(
        unpack_kernel,
        grid=(tokens // rows,),
        out_shape=(jax.ShapeDtypeStruct((1, tokens, columns), blocks.dtype),) * 3,
        in_specs=[pl.BlockSpec((seq, 3, halves, rows, head_dim), lambda i: (0, 0, 0, i, 0))],
        out_specs=(pl.BlockSpec((1, rows, columns), lambda i: (0, i, 0)),) * 3,
        compiler_params=pltpu.CompilerParams(vmem_limit_bytes=VMEM_LIMIT),
        cost_estimate=cost(0, 12 * tokens * columns),
        name="unpack_heads",
    )(blocks)


def core_columns(core, chips):
    return [pl.multiple_of((2 * x + core + 2 * chips * half) * TILE, TILE) for x in range(chips) for half in range(2)]


def pack_weight_kernel(chips, place_ref, in_ref, after_ref, out_ref):
    for i, column in enumerate(core_columns(place_ref[2], chips)):
        out_ref[:, pl.ds(i * TILE, TILE)] = in_ref[:, pl.ds(column, TILE)]


def pack_weight(place, shard, after, chips):
    rows, columns = shard.shape
    return pl.pallas_call(
        functools.partial(pack_weight_kernel, chips),
        out_shape=jax.ShapeDtypeStruct((rows, columns // 2), shard.dtype),
        in_specs=[SMEM, VMEM, HBM],
        out_specs=VMEM,
        compiler_params=pltpu.CompilerParams(vmem_limit_bytes=VMEM_LIMIT),
        cost_estimate=cost(0, 3 * rows * columns),
        name="pack_weight",
    )(place, shard, after)


def unpack_weight_kernel(chips, place_ref, own_ref, other_ref, out_ref):
    for ref, core in ((own_ref, place_ref[2]), (other_ref, 1 - place_ref[2])):
        for i, column in enumerate(core_columns(core, chips)):
            out_ref[:, pl.ds(column, TILE)] = ref[:, pl.ds(i * TILE, TILE)].astype(F32)


def unpack_weight(place, own, other, chips):
    rows, columns = own.shape
    return pl.pallas_call(
        functools.partial(unpack_weight_kernel, chips),
        out_shape=jax.ShapeDtypeStruct((rows, 2 * columns), F32),
        in_specs=[SMEM, VMEM, VMEM],
        out_specs=VMEM,
        compiler_params=pltpu.CompilerParams(vmem_limit_bytes=VMEM_LIMIT),
        cost_estimate=cost(0, 12 * rows * columns),
        name="unpack_weight",
    )(place, own, other)


def slot_plan(place_ref, tiles_ref, counts_ref, unit, slot, units, width):
    first_head = place_ref[0]
    split = counts_ref[first_head * units + unit]
    in_first = slot < split
    head = jnp.where(in_first, first_head, first_head + place_ref[1])
    entry = jnp.minimum(jnp.where(in_first, slot, width - slot), width - 1)
    tile = tiles_ref[(head * units + unit) * width + entry]
    return in_first, jnp.where(in_first, 0, 1), tile


def rows_of(ref, half, tile):
    per_block = ref.shape[2] // TILE
    start = pl.multiple_of(lax.rem(tile, per_block) * TILE, TILE)
    return ref.at[lax.div(tile, per_block), half, pl.ds(start, TILE), :]


def forward_kernel(multi, slots, units, width, scale, place_ref, tiles_ref, counts_ref, qkv_ref, a_ref, lse_ref, *refs):
    block_refs, (vt_ref, s_ref, p_ref) = refs[:-3], refs[-3:]
    scale2 = scale * math.log2(math.e)
    q_ref, k_ref, v_ref = (qkv_ref.at[:, n] for n in range(3))

    @pl.loop(0, units, unroll=2)
    def _(t):
        for half in range(2):
            vt_ref[half * units + t] = rows_of(v_ref, half, t)[...].T

    @pl.loop(0, units // multi)
    def _(step):
        plans = [[slot_plan(place_ref, tiles_ref, counts_ref, step * multi + u, j, units, width) for j in range(slots)] for u in range(multi)]
        all_tops = []
        for u in range(multi):
            tops = []
            for j, (in_first, half, tile) in enumerate(plans[u]):
                s = mm(rows_of(k_ref, half, tile)[...], rows_of(q_ref, half, step * multi + u)[...], NT)
                s_ref[u * slots + j] = s
                tops.append(jnp.max(s.reshape(TILE // 8, 8, TILE), axis=0))
            all_tops.append(tops)
        low = jnp.full((8, TILE), -jnp.inf, F32)
        zero = jnp.zeros((TILE, TILE), BF16)
        stats = []
        for u in range(multi):
            top = []
            for half in range(2):
                m = low
                for (in_first, _, _), t8 in zip(plans[u], all_tops[u]):
                    use = in_first if half == 0 else jnp.logical_not(in_first)
                    m = jnp.maximum(m, jnp.where(use, t8, low))
                top.append(jnp.max(m, axis=0, keepdims=True) * scale2)
            totals = [jnp.zeros((8, TILE), F32)] * 2
            for j, (in_first, half, tile) in enumerate(plans[u]):
                p = jnp.exp2(s_ref[u * slots + j] * scale2 - jnp.where(in_first, top[0], top[1]))
                l8 = jnp.sum(p.reshape(TILE // 8, 8, TILE), axis=0)
                totals[0] = totals[0] + jnp.where(in_first, l8, 0.0)
                totals[1] = totals[1] + jnp.where(in_first, 0.0, l8)
                pb = p.astype(BF16)
                p_ref[u, pl.ds(j * TILE, TILE), 0:TILE] = jnp.where(in_first, pb, zero)
                p_ref[u, pl.ds(j * TILE, TILE), TILE : 2 * TILE] = jnp.where(in_first, zero, pb)
            stats.append((top, totals))
        for u in range(multi):
            unit = step * multi + u
            top, totals = stats[u]
            vt = jnp.concatenate([vt_ref[half * units + tile] for _, half, tile in plans[u]], axis=1)
            mixed = mm(vt, p_ref[u])
            for half in range(2):
                total = jnp.sum(totals[half], axis=0, keepdims=True)
                a_t = mixed[:, half * TILE : (half + 1) * TILE] / total
                rows_of(a_ref, half, unit)[...] = a_t.T.astype(BF16)
                lse_ref[half * units + unit] = jnp.broadcast_to(top[half] + jnp.log2(total), (8, TILE))

    chips = len(block_refs)
    for k, ref in enumerate(block_refs):
        ref[...] = a_ref[lax.rem(place_ref[5] + k, chips)]


def attention_forward(place, tiles, counts, qkv, chips, width):
    seq, _, halves, tokens, head_dim = qkv.shape
    units = seq * tokens // TILE
    slots = width + 1
    rows = seq * tokens // chips
    return pl.pallas_call(
        functools.partial(forward_kernel, UNITS_AT_ONCE, slots, units, width, 1.0 / math.sqrt(head_dim)),
        out_shape=(
            jax.ShapeDtypeStruct((chips, halves, rows, head_dim), BF16),
            jax.ShapeDtypeStruct((halves * units, 8, TILE), F32),
        )
        + (jax.ShapeDtypeStruct((halves, rows, head_dim), BF16),) * chips,
        in_specs=[SMEM] * 3 + [VMEM],
        out_specs=(VMEM,) * (2 + chips),
        scratch_shapes=[
            pltpu.VMEM((halves * units, head_dim, TILE), BF16),
            pltpu.VMEM((UNITS_AT_ONCE * slots, TILE, TILE), F32),
            pltpu.VMEM((UNITS_AT_ONCE, slots * TILE, 2 * TILE), BF16),
        ],
        compiler_params=pltpu.CompilerParams(vmem_limit_bytes=VMEM_LIMIT),
        cost_estimate=cost(16 * units * slots * TILE**3, 6 * MIB, units * slots * TILE * TILE),
        name="attention_forward",
    )(place, tiles, counts, qkv)


def backward_kernel(multi, slots, units, width, scale, place_ref, tiles_ref, counts_ref, qkv_ref, g_ref, a_ref, lse_ref, *refs):
    out_ref, kt_ref, dk_acc, dv_acc, s_ref, dp_ref, p_ref, d_ref = refs[-8:]
    scale2 = scale * math.log2(math.e)
    q_ref, k_ref, v_ref = (qkv_ref.at[:, n] for n in range(3))
    dq_ref, dk_ref, dv_ref = (out_ref.at[:, n] for n in range(3))

    @pl.loop(0, units, unroll=2)
    def _(t):
        for half in range(2):
            kt_ref[half * units + t] = rows_of(k_ref, half, t)[...].T
            dk_acc[half * units + t] = jnp.zeros((TILE, TILE), F32)
            dv_acc[half * units + t] = jnp.zeros((TILE, TILE), F32)

    @pl.loop(0, units // multi)
    def _(step):
        plans = [[slot_plan(place_ref, tiles_ref, counts_ref, step * multi + u, j, units, width) for j in range(slots)] for u in range(multi)]
        zero = jnp.zeros((TILE, TILE), BF16)
        deltas, lses = [], []
        for u in range(multi):
            unit = step * multi + u
            delta, lse = [], []
            for half in range(2):
                prod = rows_of(g_ref, half, unit)[...].astype(F32) * rows_of(a_ref, half, unit)[...].astype(F32)
                delta.append(jnp.sum(prod.T, axis=0, keepdims=True))
                lse.append(lse_ref[half * units + unit][0:1])
            deltas.append(delta)
            lses.append(lse)
            for j, (in_first, half, tile) in enumerate(plans[u]):
                s_ref[u * slots + j] = mm(rows_of(k_ref, half, tile)[...], rows_of(q_ref, half, unit)[...], NT)
                dp_ref[u * slots + j] = mm(rows_of(v_ref, half, tile)[...], rows_of(g_ref, half, unit)[...], NT)
        for u in range(multi):
            for j, (in_first, half, tile) in enumerate(plans[u]):
                p = jnp.exp2(s_ref[u * slots + j] * scale2 - jnp.where(in_first, lses[u][0], lses[u][1]))
                ds = (p * (dp_ref[u * slots + j] - jnp.where(in_first, deltas[u][0], deltas[u][1]))).astype(BF16)
                p_ref[u * slots + j] = p.astype(BF16)
                d_ref[u, pl.ds(j * TILE, TILE), 0:TILE] = jnp.where(in_first, ds, zero)
                d_ref[u, pl.ds(j * TILE, TILE), TILE : 2 * TILE] = jnp.where(in_first, zero, ds)
        for u in range(multi):
            unit = step * multi + u
            for j, (in_first, half, tile) in enumerate(plans[u]):
                ds = d_ref[u, pl.ds(j * TILE, TILE), pl.ds(pl.multiple_of(half * TILE, TILE), TILE)]
                dv_acc[half * units + tile] += mm(p_ref[u * slots + j], rows_of(g_ref, half, unit)[...])
                dk_acc[half * units + tile] += mm(ds, rows_of(q_ref, half, unit)[...])
            kt = jnp.concatenate([kt_ref[half * units + tile] for _, half, tile in plans[u]], axis=1)
            dq_t = mm(kt, d_ref[u]) * scale
            for half in range(2):
                rows_of(dq_ref, half, unit)[...] = dq_t[:, half * TILE : (half + 1) * TILE].T.astype(BF16)

    @pl.loop(0, units, unroll=2)
    def _(t):
        for half in range(2):
            rows_of(dk_ref, half, t)[...] = (dk_acc[half * units + t] * scale).astype(BF16)
            rows_of(dv_ref, half, t)[...] = dv_acc[half * units + t].astype(BF16)


def attention_backward(place, tiles, counts, qkv, g, a, lse, after, width):
    seq, _, halves, tokens, head_dim = qkv.shape
    units = seq * tokens // TILE
    slots = width + 1
    return pl.pallas_call(
        functools.partial(backward_kernel, UNITS_AT_ONCE, slots, units, width, 1.0 / math.sqrt(head_dim)),
        out_shape=jax.ShapeDtypeStruct(qkv.shape, BF16),
        in_specs=[SMEM] * 3 + [VMEM] * 4 + [HBM] * len(after),
        out_specs=VMEM,
        scratch_shapes=[
            pltpu.VMEM((halves * units, head_dim, TILE), BF16),
            pltpu.VMEM((halves * units, TILE, head_dim), F32),
            pltpu.VMEM((halves * units, TILE, head_dim), F32),
            pltpu.VMEM((UNITS_AT_ONCE * slots, TILE, TILE), F32),
            pltpu.VMEM((UNITS_AT_ONCE * slots, TILE, TILE), F32),
            pltpu.VMEM((UNITS_AT_ONCE * slots, TILE, TILE), BF16),
            pltpu.VMEM((UNITS_AT_ONCE, slots * TILE, 2 * TILE), BF16),
        ],
        compiler_params=pltpu.CompilerParams(vmem_limit_bytes=VMEM_LIMIT),
        cost_estimate=cost(3*10**11, MIB),
        name="attention_backward",
    )(place, tiles, counts, qkv, g, a, lse, *after)


def grad_attn_kernel(place_ref, own_ref, other_ref, w_ref, after_ref, g_ref):
    tokens = own_ref.shape[0]
    core = place_ref[2]
    rows = jnp.concatenate([own_ref[...], other_ref[...]], axis=0)
    g = mm(rows, w_ref[...]).astype(BF16)
    for slot, first in ((core, 0), (1 - core, tokens)):
        target = pl.ds(pl.multiple_of(slot * tokens, tokens), tokens)
        for half in range(2):
            g_ref[0, half, target, :] = g[first : first + tokens, half * TILE : (half + 1) * TILE]


def grad_attn(place, own, other, weights, after, chips):
    tokens, depth = own.shape
    columns = weights.shape[1]
    block = columns // chips
    return pl.pallas_call(
        grad_attn_kernel,
        grid=(chips,),
        out_shape=jax.ShapeDtypeStruct((chips, 2, 2 * tokens, TILE), BF16),
        in_specs=[
            SMEM,
            pl.BlockSpec((tokens, depth), lambda i: (0, 0)),
            pl.BlockSpec((tokens, depth), lambda i: (0, 0)),
            pl.BlockSpec((depth, block), lambda i: (0, i)),
            HBM,
        ],
        out_specs=pl.BlockSpec((1, 2, 2 * tokens, TILE), lambda i: (i, 0, 0, 0)),
        compiler_params=pltpu.CompilerParams(vmem_limit_bytes=VMEM_LIMIT),
        cost_estimate=cost(4 * tokens * depth * columns, 7 * MIB),
        name="grad_attn",
    )(place, own, other, weights, after)


def gather_rows(place_ref, block_refs, rows_ref):
    chips = len(block_refs)
    halves, rows, width = block_refs[0].shape
    tokens = rows // 2
    core = place_ref[2]
    for k, ref in enumerate(block_refs):
        chip = lax.rem(place_ref[5] + chips - k, chips)
        for half in range(halves):
            target = pl.ds(pl.multiple_of((chip * halves + half) * width, width), width)
            for slot, first in ((core, 0), (1 - core, tokens)):
                source = pl.ds(pl.multiple_of(slot * tokens, tokens), tokens)
                rows_ref[first : first + tokens, target] = ref[half, source, :]


def project_kernel(place_ref, *refs):
    block_refs, w_ref, own_ref, other_ref, rows_ref = refs[:-5], refs[-5], refs[-3], refs[-2], refs[-1]

    @pl.when(pl.program_id(0) == 0)
    def _():
        gather_rows(place_ref, block_refs, rows_ref)

    tokens = own_ref.shape[0]
    out = mm(rows_ref[...], w_ref[...], NT)
    own_ref[...] = out[:tokens]
    other_ref[...] = out[tokens:].astype(BF16)


def project(place, blocks, weights, after):
    features, columns = weights.shape
    tokens = blocks[0].shape[1] // 2
    step = 2 * TILE
    return pl.pallas_call(
        project_kernel,
        grid=(features // step,),
        out_shape=(jax.ShapeDtypeStruct((tokens, features), F32), jax.ShapeDtypeStruct((tokens, features), BF16)),
        in_specs=[SMEM]
        + [pl.BlockSpec(block.shape, lambda i: (0, 0, 0)) for block in blocks]
        + [pl.BlockSpec((step, columns), lambda i: (i, 0)), HBM],
        out_specs=(pl.BlockSpec((tokens, step), lambda i: (0, i)),) * 2,
        scratch_shapes=[pltpu.VMEM((2 * tokens, columns), BF16)],
        compiler_params=pltpu.CompilerParams(vmem_limit_bytes=VMEM_LIMIT),
        cost_estimate=cost(4 * tokens * features * columns, 8 * MIB),
        name="project",
    )(place, *blocks, weights, after)


def grad_weight_kernel(side, chips, place_ref, own_ref, other_ref, *refs):
    block_refs, out_refs, (rows_ref, part_ref, sems) = refs[:chips], refs[chips:-3], refs[-3:]
    gather_rows(place_ref, block_refs, rows_ref)
    rows = part_ref.shape[2]
    half = part_ref.shape[3]
    copies = [pltpu.make_async_copy(part_ref.at[n], out_refs[n], sems.at[n]) for n in range(2 * side)]
    for ky in range(side):
        for kz in range(side):
            row = lax.rem(place_ref[3] + ky, side) * side + lax.rem(place_ref[4] + kz, side)
            columns = pl.ds(pl.multiple_of(row * rows, rows), rows)
            left = jnp.concatenate([own_ref[:, columns], other_ref[:, columns]], axis=0)
            part = mm(left, rows_ref[...], TN)
            part_ref[kz, ky] = part[:, :half].astype(BF16)
            part_ref[side + ky, kz] = part[:, half:].astype(BF16)
            if ky == side - 1:
                copies[kz].start()
        copies[side + ky].start()
    for copy in copies:
        copy.wait()


def grad_weight_parts(place, own, other, blocks, side):
    tokens, features = own.shape
    chips = len(blocks)
    columns = chips * blocks[0].shape[0] * blocks[0].shape[2]
    rows = features // side**2
    return pl.pallas_call(
        functools.partial(grad_weight_kernel, side, chips),
        out_shape=(jax.ShapeDtypeStruct((side, rows, columns // 2), BF16),) * (2 * side),
        in_specs=[SMEM] + [VMEM] * (2 + chips),
        out_specs=(HBM,) * (2 * side),
        scratch_shapes=[
            pltpu.VMEM((2 * tokens, columns), BF16),
            pltpu.VMEM((2 * side, side, rows, columns // 2), BF16),
            pltpu.SemaphoreType.DMA((2 * side,)),
        ],
        compiler_params=pltpu.CompilerParams(vmem_limit_bytes=VMEM_LIMIT),
        cost_estimate=cost(4 * tokens * features * columns, 7 * MIB),
        name="grad_weight_parts",
    )(place, own, other, *blocks)


def gate_kernel(*refs):
    del refs


def gate(values, *after):
    return pl.pallas_call(
        gate_kernel,
        out_shape=jax.ShapeDtypeStruct(values.shape, values.dtype),
        in_specs=[ANY] * (1 + len(after)),
        out_specs=ANY,
        input_output_aliases={0: 0},
        compiler_params=pltpu.CompilerParams(vmem_limit_bytes=VMEM_LIMIT),
        name="gate",
    )(values, *after)


def sum_kernel(*refs):
    side = len(refs) // 4
    for n in range(2):
        in_refs = refs[n * side : (n + 1) * side]
        for k in range(side):
            total = in_refs[0][k].astype(F32)
            for ref in in_refs[1:]:
                total = total + ref[k].astype(F32)
            refs[2 * side + n * side + k][...] = total.astype(BF16)


def summed(first, second):
    side, rows, width = first[0].shape
    sums = pl.pallas_call(
        sum_kernel,
        out_shape=(jax.ShapeDtypeStruct((rows, width), BF16),) * (2 * side),
        in_specs=[VMEM] * (2 * side),
        out_specs=(VMEM,) * (2 * side),
        compiler_params=pltpu.CompilerParams(vmem_limit_bytes=VMEM_LIMIT),
        cost_estimate=cost(10**12, MIB),
        name="summed",
    )(*first, *second)
    return sums[:side], sums[side:]


def sum_pair_kernel(*refs):
    out_ref = refs[-1]
    count = len(refs) // 2
    width = refs[0].shape[1]
    for side in range(2):
        total = refs[side * count][...].astype(F32)
        for ref in refs[side * count + 1 : (side + 1) * count]:
            total = total + ref[...].astype(F32)
        out_ref[:, side * width : (side + 1) * width] = total.astype(BF16)


def summed_side_by_side(first, second):
    rows, width = first[0].shape
    return pl.pallas_call(
        sum_pair_kernel,
        out_shape=jax.ShapeDtypeStruct((rows, 2 * width), BF16),
        in_specs=[VMEM] * (2 * len(first)),
        out_specs=VMEM,
        compiler_params=pltpu.CompilerParams(vmem_limit_bytes=VMEM_LIMIT),
        cost_estimate=cost(0, 4 * (len(first) + 1) * rows * width),
        name="summed_side_by_side",
    )(*first, *second)


def sum_chips_kernel(a_ref, b_ref, c_ref, d_ref, *refs):
    first = a_ref[...].astype(F32) + b_ref[...].astype(F32)
    second = c_ref[...].astype(F32) + d_ref[...].astype(F32)
    refs[-1][...] = (first + second).astype(BF16)


def summed_over_chips(parts, after):
    return pl.pallas_call(
        sum_chips_kernel,
        out_shape=jax.ShapeDtypeStruct(parts[0].shape, BF16),
        in_specs=[VMEM] * len(parts) + [HBM] * len(after),
        out_specs=VMEM,
        compiler_params=pltpu.CompilerParams(vmem_limit_bytes=VMEM_LIMIT),
        cost_estimate=cost(0, 10 * math.prod(parts[0].shape)),
        name="summed_over_chips",
    )(*parts, *after)


def per_device(queries, key_states, value_states, grad_output, out_weight, key_tiles, tile_count):
    seq = lax.axis_size("seq")
    ranks = lax.axis_size("dp")
    side = math.isqrt(ranks)
    chips = seq // 2
    s_index = lax.axis_index("seq")
    d_index = lax.axis_index("dp")
    core = lax.rem(s_index, 2)
    tokens, columns = queries.shape[1:]
    heads, units, width = key_tiles.shape[1:]
    head_dim = columns // heads
    rows = out_weight.shape[0]
    place = jnp.stack([s_index, jnp.int32(seq), core, lax.div(d_index, side), lax.rem(d_index, side), lax.div(s_index, 2)]).astype(jnp.int32)
    lists = key_tiles.reshape(-1)
    counts = tile_count.reshape(-1)
    same_core = [list(range(c, seq, 2)) for c in range(2)]
    across = [(i, i ^ 1) for i in range(seq)]

    def y_shift(k):
        return [(i, (i // side + k) % side * side + i % side) for i in range(ranks)]

    def z_shift(k):
        return [(i, i // side * side + (i % side + k) % side) for i in range(ranks)]

    def x_shift(k):
        return [(i, (i + 2 * k) % seq) for i in range(seq)]

    def x_swap(k):
        return [(i, i ^ (2 * k)) for i in range(seq)]

    def over_chips(values):
        return lax.all_to_all(values, "seq", split_axis=0, concat_axis=0, tiled=True, axis_index_groups=same_core)

    packed = pack(queries, key_states, value_states, seq, head_dim)
    weights = lax.all_gather(pack_weight(place, out_weight, packed, chips), "dp", axis=0, tiled=True)
    qkv = lax.all_to_all(packed, "seq", split_axis=0, concat_axis=0, tiled=True)
    own_rows = grad_output[0]
    other_rows = lax.ppermute(own_rows, "seq", across)
    a, lse, *a_blocks = attention_forward(place, lists, counts, qkv, chips, width)
    a_home = [a_blocks[0]] + [lax.ppermute(a_blocks[k], "seq", x_shift(k)) for k in range(1, chips)]
    g = over_chips(gate(grad_attn(place, own_rows, other_rows, weights, lse, chips), *a_home))
    parts = grad_weight_parts(place, own_rows, other_rows, a_home, side)
    z_first = [parts[0]] + [lax.ppermute(parts[k], "dp", z_shift(k)) for k in range(1, side)]
    y_first = [parts[side]] + [lax.ppermute(parts[side + k], "dp", y_shift(k)) for k in (1, side - 1)]
    grads = attention_backward(place, lists, counts, qkv, g, a, lse, (parts[0],), width)
    grads_home = lax.all_to_all(grads, "seq", split_axis=0, concat_axis=0, tiled=True)
    y_first += [lax.ppermute(gate(parts[side + k], grads), "dp", y_shift(k)) for k in range(2, side - 1)]

    z_sum, y_sum = summed(z_first, y_first)
    out_own, out_other = project(place, a_home, weights, grads)
    output = (out_own + lax.ppermute(out_other, "seq", across).astype(F32)).astype(BF16)
    chip_share = summed_side_by_side(
        [z_sum[0]] + [lax.ppermute(z_sum[k], "dp", y_shift(k)) for k in range(1, side)],
        [y_sum[0]] + [lax.ppermute(y_sum[k], "dp", z_shift(k)) for k in range(1, side)],
    )
    grad_query, grad_key, grad_value = unpack(grads_home)
    by_chip = [chip_share] + [lax.ppermute(chip_share, "seq", x_swap(k)) for k in range(1, chips)]
    own_half = summed_over_chips(by_chip, (grad_query, output))
    grad_weight = unpack_weight(place, own_half, lax.ppermute(own_half, "seq", across), chips)
    return output[None], grad_query, grad_key, grad_value, grad_weight


def solution(mesh):
    in_specs = (
        P("dp", "seq", None),
        P("dp", "seq", None),
        P("dp", "seq", None),
        P("dp", "seq", None),
        P("dp", None),
        P("dp", None, None, None),
        P("dp", None, None),
    )
    out_specs = (
        P("dp", "seq", None),
        P("dp", "seq", None),
        P("dp", "seq", None),
        P("dp", "seq", None),
        P("dp", None),
    )
    return jax.shard_map(per_device, mesh=mesh, in_specs=in_specs, out_specs=out_specs, check_vma=False)
```

time: 438 us -> 196 us (0.45)
  Pallas kernels: 255 us -> 67 us
  waiting for transfers between devices: 84.3 us -> 55.1 us
  local copies, waits for them, and re-layouts: 24.8 us -> 8.68 us
  other arithmetic: 10.5 us -> 2.48 us
    pallas_call x6 -> x13, Pallas kernels: 251 us -> 60.8 us  [the longest x1 15.5 us: attention_backward(): pl.pallas_call(functools.partial(backward_kernel, UNITS_AT_ONCE, slots, u...]
    ppermute x3, waiting for transfers between devices: 24.4 us -> 4.03 us  [per_device(): lax.ppermute(chip_share, 'seq', x_swap(k))]
    all_to_all x2 -> x1, waiting for transfers between devices: 14.3 us -> 0.01 us  [over_chips(): lax.all_to_all(values, 'seq', split_axis=0, concat_axis=0, tiled=True, ax...]
    ppermute x1 -> x5, starting transfers between devices: 0.79 us -> 7.75 us  [the longest x1 3.02 us: per_device(): lax.ppermute(gate(parts[side + k], grads), 'dp', y_shift(k))]
    unnamed x35 -> x39, local copies, waits for them, and re-layouts: 12.9 us -> 6.61 us
    ppermute x1 -> x5, waiting for transfers between devices: 1.29 us -> 6.93 us  [the longest x3 5.55 us: per_device(): lax.ppermute(a_blocks[k], 'seq', x_shift(k))]
    convert_element_type x2 -> x0, local copies, waits for them, and re-layouts: 4.81 us -> none  [per_device(): jnp.stack([even, odd], axis=2).transpose(0, 3, 1, 2, 4)]
    ppermute x3, waiting for transfers between devices: 0.01 us -> 4.76 us  [per_device(): lax.ppermute(z_sum[k], 'dp', y_shift(k))]
  transfers between devices with their start and end apart: 23 -> 25, of which waited for: 10 -> 8; matrix products, arithmetic and copies ran while one was open for 4% -> 2% of each run, Pallas kernels for 36% -> 29%
where the time goes in v2:
time: 196 us
  Pallas kernels  67 us (34%)
  waiting for transfers between devices  55.1 us (28%)
  starting transfers between devices  48.1 us (25%)
  between operations  14.2 us (7%)
  local copies, waits for them, and re-layouts  8.68 us (4%)
  other arithmetic  2.48 us (1%)
    all_to_all x1, waiting for transfers between devices, per_device(): qkv = lax.all_to_all(packed, 'seq', split_axis=0, concat_axis=0, tiled=True)  35.9 us
    pallas_call x1, Pallas kernels, attention_backward(): pl.pallas_call(functools.partial(backward_kernel, UNITS_AT_ONCE, slots, u...  15.5 us
    pallas_call x1, Pallas kernels, attention_forward(): pl.pallas_call(functools.partial(forward_kernel, UNITS_AT_ONCE, slots, un...  10.6 us
    pallas_call x1, Pallas kernels, project(): pl.pallas_call(project_kernel, grid=(features // step,), out_shape=(jax.S...  8.34 us
    ppermute x3, starting transfers between devices, per_device(): lax.ppermute(chip_share, 'seq', x_swap(k))  7.01 us
    unnamed x39, local copies, waits for them, and re-layouts  6.61 us
    all_to_all x1, starting transfers between devices, per_device(): lax.all_to_all(grads, 'seq', split_axis=0, concat_axis=0, tiled=True)  6.47 us
    pallas_call x1, Pallas kernels, grad_attn(): pl.pallas_call(grad_attn_kernel, grid=(chips,), out_shape=jax.ShapeDtypeS...  6.2 us
  transfers between devices with their start and end apart: 25, of which 8 were waited for; matrix products, arithmetic and copies ran while one was open for 2% of the time, Pallas kernels for 29%

profile of v2, /device:TPU:1, one launch (start us, length us, event | category | flops | bytes accessed | tf_op | source)
XLA Modules:
  0.0 195.5 jit_solution(17364739062068147442)
XLA Ops:
  7.2 0.0 all-gather.2.cloned.1.call-start
  7.2 4.5 %pack_heads.1.after_ref = bf16[8,3,2,256,128]{4,3,2,1,0:T(8,128)(2,1)} custom-call(bf16[1,256,2048]{2,1,0:T(8,128)(2,1)} %q_ref.1, bf16[1,256,2048]{2,1,0:T(8,128)(2,1)} %k_ref.1, bf16[1,256,2048]{2,1,0:T(8,128)(2,1)} %v_ref.1), custom_call_target="tpu_custom_call" | custom-call | bytes 6291456 | tf_op jit(solution)/shard_map/pack_heads/pallas_call | solution.py:47
  11.7 0.6 stack.23.place_ref
  12.3 1.8 pack_weight.1
  14.1 0.0 all-gather.2.cloned.1.call-update
  14.2 0.0 copy-start.17
  14.2 0.0 copy-start.16
  14.2 5.9 %all-to-all-start = ((bf16[8,3,2,256,128]{4,3,2,1,0:T(8,128)(2,1)}), bf16[8,3,2,256,128]{4,3,2,1,0:T(8,128)(2,1)S(1)}, u32[]{:S(2)}, u32[]{:S(2)}) async-start(bf16[8,3,2,256,128]{4,3,2,1,0:T(8,128)(2,1)} %pack_heads.1.after_ref), calls=%async_computation | async-start | bytes 6291456 | tf_op jit(solution)/shard_map/all_to_all | solution.py:542
  20.1 0.0 collective-permute-start.3
  20.1 0.7 reshape.17.counts_ref
  20.8 0.2 copy.14
  21.0 0.8 reshape.16.tiles_ref
  21.8 35.9 %all-to-all-done.qkv_ref = bf16[8,3,2,256,128]{4,3,2,1,0:T(8,128)(2,1)S(1)} async-done(((bf16[8,3,2,256,128]{4,3,2,1,0:T(8,128)(2,1)}), bf16[8,3,2,256,128]{4,3,2,1,0:T(8,128)(2,1)S(1)}, u32[]{:S(2)}, u32[]{:S(2)}) %all-to-all-start) | async-done | bytes 3145760 | tf_op jit(solution)/shard_map/all_to_all | solution.py:542
  57.7 1.8 copy-done
  59.5 10.6 %attention_forward.1 = (bf16[4,2,512,128]{3,2,1,0:T(8,128)(2,1)}, f32[32,8,128]{2,1,0:T(8,128)}, bf16[2,512,128]{2,1,0:T(8,128)(2,1)}, bf16[2,512,128]{2,1,0:T(8...) custom-call(s32[6]{0:T(128)} %stack.23.place_ref, s32[1792]{0:T(1024)} %reshape.16.tiles_ref, ...), custom_call_target="tpu_custom_call" | custom-call | flops 4294967296 | bytes 6291456 | tf_op jit(solution)/shard_map/attention_forward/pallas_call | solution.py:204
  70.1 0.4 collective-permute-start
  70.5 1.7 collective-permute-start.1
  72.2 0.7 collective-permute-start.2
  72.9 6.2 %grad_attn.1.refs_0_ = bf16[4,2,512,128]{3,2,1,0:T(8,128)(2,1)} custom-call(s32[6]{0:T(128)} %stack.23.place_ref, bf16[256,2048]{1,0:T(8,128)(2,1)} %bitcast.11, bf16[256,2048]{1,0:T(8,128)(2,1)} %collective-permute-done.3.other_ref, bf16[2048,1024]{1,0:T(8,128)(2,1)} %all-gather.2.cloned.1.call-done.w_ref.refs_4_, ...), custom_call_target="tpu_custom_call" | custom-call | flops 2147483648 | bytes 7340032 | tf_op jit(solution)/shard_map/grad_attn/pallas_call | solution.py:318
  79.1 4.4 %collective-permute-done.1.refs_3_.refs_2_ = bf16[2,512,128]{2,1,0:T(8,128)(2,1)S(1)} collective-permute-done((bf16[2,512,128]{2,1,0:T(8,128)(2,1)}, bf16[2,512,128]{2,1,0:T(8,128)(2,1)S(1)}, u32[]{:S(2)}, u32[]{:S(2)}) %collective-permute-start.1) | collective-permute-done | bytes 262176 | tf_op jit(solution)/shard_map/ppermute | solution.py:546
  83.5 1.1 collective-permute-done.2.refs_4_.refs_3_
  84.6 0.7 copy-done.4
  85.3 4.6 %all-to-all-start.1 = ((bf16[4,2,512,128]{3,2,1,0:T(8,128)(2,1)}), bf16[4,2,512,128]{3,2,1,0:T(8,128)(2,1)S(1)}, u32[]{:S(2)}, u32[]{:S(2)}) async-start(bf16[4,2,512,128]{3,2,1,0:T(8,128)(2,1)} %gate.2), calls=%async_computation.1 | async-start | bytes 2097152 | tf_op jit(solution)/shard_map/all_to_all | solution.py:538
  89.9 5.8 %grad_weight_parts.1 = (bf16[4,128,512]{2,1,0:T(8,128)(2,1)}, bf16[4,128,512]{2,1,0:T(8,128)(2,1)}, bf16[4,128,512]{2,1,0:T(8,128)(2,1)}, bf16[4,128,512]{2,1,0:...) custom-call(s32[6]{0:T(128)} %stack.23.place_ref, ...), custom_call_target="tpu_custom_call" | custom-call | flops 2147483648 | bytes 7340032 | tf_op jit(solution)/shard_map/grad_weight_parts/pallas_call | solution.py:408
  95.7 1.8 collective-permute-start.5
  97.5 3.2 %collective-permute-start.6 = (bf16[4,128,512]{2,1,0:T(8,128)(2,1)}, bf16[4,128,512]{2,1,0:T(8,128)(2,1)}, u32[]{:S(2)}, u32[]{:S(2)}) collective-permute-start(bf16[4,128,512]{2,1,0:T(8,128)(2,1)} %get-tuple-element.45), channel_id=1, source_target_pairs={{0,16},{8,24},{16,0},{24,8},{32,48},{40,56},{48,32},{56,40},{64,80... | collective-permute-start | bytes 1572872 | tf_op jit(solution)/shard_map/ppermute | solution.py:549
  100.6 0.7 collective-permute-start.7
  101.4 1.1 collective-permute-start.8
  102.5 1.7 collective-permute-start.9
  104.1 1.0 copy-done.5
  105.1 15.5 %attention_backward.1.refs_5_.refs_1_ = bf16[8,3,2,256,128]{4,3,2,1,0:T(8,128)(2,1)} custom-call(s32[6]{0:T(128)} %stack.23.place_ref, s32[1792]{0:T(1024)} %reshape.16.tiles_ref, s32[256]{0:T(256)} %reshape.17.counts_ref, bf16[8,3,2,256,128]{4,3,2,1,0:T(8,128)(2,1)} %copy-done, bf16[4,2,512,128]{3,2,1,0:T(8,128)(2,1)} %copy-done.5, ...), custom_call_target="tpu_custom_call" | custom-call | flops 299999985664 | bytes 1048576 | tf_op jit(solution)/shard_map/attention_backward/pallas_call | solution.py:283
  120.6 3.0 %collective-permute-start.10 = (bf16[4,128,512]{2,1,0:T(8,128)(2,1)}, bf16[4,128,512]{2,1,0:T(8,128)(2,1)S(1)}, u32[]{:S(2)}, u32[]{:S(2)}) collective-permute-start(bf16[4,128,512]{2,1,0:T(8,128)(2,1)} %gate.3), channel_id=1, source_target_pairs={{0,64},{8,72},{16,80},{24,88},{32,96},{40,104},{48,112},{56,120},{... | collective-permute-start | bytes 1572872 | tf_op jit(solution)/shard_map/ppermute | solution.py:553
  123.7 6.5 %all-to-all-start.2 = ((bf16[8,3,2,256,128]{4,3,2,1,0:T(8,128)(2,1)}), bf16[8,3,2,256,128]{4,3,2,1,0:T(8,128)(2,1)}, u32[]{:S(2)}, u32[]{:S(2)}) async-start(bf16[8,3,2,256,128]{4,3,2,1,0:T(8,128)(2,1)} %attention_backward.1.refs_5_.refs_1_), calls=%async_computation.2 | async-start | bytes 6291456 | tf_op jit(solution)/shard_map/all_to_all | solution.py:552
  130.1 8.3 %project.1 = (f32[256,2048]{1,0:T(8,128)}, bf16[256,2048]{1,0:T(8,128)(2,1)}) custom-call(s32[6]{0:T(128)} %stack.23.place_ref, bf16[2,512,128]{2,1,0:T(8,128)(2,1)} %get-tuple-element.32.refs_1_.refs_0_, bf16[2,512,128]{2,1,0:T(8,128)(2,1)} %copy-done.2, bf16[2,512,128]{2,1,0:T(8,128)(2,1)} %copy-done.3, bf16[2,512,128]{2,1,0:T(8,128)(2,1)} %copy-done.4, ...), custom_call_target="tpu_custom_call" | custom-call | flops 2147483648 | bytes 8388608 | tf_op jit(solution)/shard_map/project/pallas_call | solution.py:367
  138.5 0.4 collective-permute-start.4
  138.9 0.0 copy-start.18
  138.9 0.8 copy-done.18
  139.7 3.5 %summed.1 = (bf16[128,512]{1,0:T(8,128)(2,1)}, bf16[128,512]{1,0:T(8,128)(2,1)}, bf16[128,512]{1,0:T(8,128)(2,1)}, bf16[128,512]{1,0:T(8,128)(2,1)}, bf16[128,51...) custom-call(bf16[4,128,512]{2,1,0:T(8,128)(2,1)} %get-tuple-element.38.refs_0_, ...), custom_call_target="tpu_custom_call" | custom-call | flops 999999995904 | bytes 1048576 | tf_op jit(solution)/shard_map/summed/pallas_call | solution.py:453
  143.2 0.4 collective-permute-start.11
  143.6 1.5 collective-permute-start.12
  145.0 1.0 collective-permute-start.13
  146.0 1.6 collective-permute-start.14
  147.6 4.8 %collective-permute-done.11.refs_1_ = bf16[128,512]{1,0:T(8,128)(2,1)S(1)} collective-permute-done((bf16[128,512]{1,0:T(8,128)(2,1)}, bf16[128,512]{1,0:T(8,128)(2,1)S(1)}, u32[]{:S(2)}, u32[]{:S(2)}) %collective-permute-start.11) | collective-permute-done | bytes 131104 | tf_op jit(solution)/shard_map/ppermute | solution.py:559
  152.4 1.1 collective-permute-start.15
  153.5 1.9 collective-permute-start.16
  155.4 2.5 %collective-permute-done.15.refs_6_ = bf16[128,512]{1,0:T(8,128)(2,1)S(1)} collective-permute-done((bf16[128,512]{1,0:T(8,128)(2,1)}, bf16[128,512]{1,0:T(8,128)(2,1)S(1)}, u32[]{:S(2)}, u32[]{:S(2)}) %collective-permute-start.15) | collective-permute-done | bytes 131104 | tf_op jit(solution)/shard_map/ppermute | solution.py:560
  157.9 0.9 collective-permute-done.16.refs_7_
  158.9 0.6 copy-done.15
  159.5 2.1 %summed_side_by_side.1.a_ref = bf16[128,1024]{1,0:T(8,128)(2,1)} custom-call(bf16[128,512]{1,0:T(8,128)(2,1)} %get-tuple-element.51.refs_0_, bf16[128,512]{1,0:T(8,128)(2,1)} %copy-done.10, bf16[128,512]{1,0:T(8,128)(2,1)} %copy-done.11, bf16[128,512]{1,0:T(8,128)(2,1)} %copy-done.12, bf16[128,512]{1,0:T(8,128)(2,1)} %get-tuple-element.55.refs_4_, ...), custom_call_target="tpu_custom_call" | custom-call | bytes 1310720 | tf_op jit(solution)/shard_map/summed_side_by_side/pallas_call | solution.py:478
  161.6 6.4 %collective-permute-start.19 = (bf16[128,1024]{1,0:T(8,128)(2,1)}, bf16[128,1024]{1,0:T(8,128)(2,1)S(1)}, u32[]{:S(2)}, u32[]{:S(2)}) collective-permute-start(bf16[128,1024]{1,0:T(8,128)(2,1)} %summed_side_by_side.1.a_ref), channel_id=1, source_target_pairs={{0,6},{1,7},{2,4},{3,5},{4,2},{5,3},{6,0},{7,1},{8,14},{9,15},{10,... | collective-permute-start | bytes 786440 | tf_op jit(solution)/shard_map/ppermute | solution.py:563
  168.0 0.4 collective-permute-start.18
  168.4 0.2 collective-permute-start.17
  168.6 2.5 %add_convert_fusion.refs_1_ = bf16[256,2048]{1,0:T(8,128)(2,1)} fusion(f32[256,2048]{1,0:T(8,128)S(1)} %copy-done.1, bf16[256,2048]{1,0:T(8,128)(2,1)} %collective-permute-done.4), kind=kLoop, calls=%fused_computation | loop fusion | flops 1572864 | bytes 4194304 | tf_op jit(solution)/shard_map/convert_element_type | solution.py:557
  171.1 4.5 %unpack_heads.1 = (bf16[1,256,2048]{2,1,0:T(8,128)(2,1)}, bf16[1,256,2048]{2,1,0:T(8,128)(2,1)}, bf16[1,256,2048]{2,1,0:T(8,128)(2,1)}) custom-call(bf16[8,3,2,256,128]{4,3,2,1,0:T(8,128)(2,1)} %all-to-all-done.2.in_ref), custom_call_target="tpu_custom_call" | custom-call | bytes 6291456 | tf_op jit(solution)/shard_map/unpack_heads/pallas_call | solution.py:72
  175.6 4.0 %collective-permute-done.19.d_ref = bf16[128,1024]{1,0:T(8,128)(2,1)S(1)} collective-permute-done((bf16[128,1024]{1,0:T(8,128)(2,1)}, bf16[128,1024]{1,0:T(8,128)(2,1)S(1)}, u32[]{:S(2)}, u32[]{:S(2)}) %collective-permute-start.19) | collective-permute-done | bytes 262176 | tf_op jit(solution)/shard_map/ppermute | solution.py:563
  179.6 0.0 copy-start.9
  179.6 0.7 copy-done.7
  180.3 0.1 copy-done.8
  180.4 0.1 copy-done.9
  180.5 2.0 %summed_over_chips.1.own_ref = bf16[128,1024]{1,0:T(8,128)(2,1)} custom-call(bf16[128,1024]{1,0:T(8,128)(2,1)} %summed_side_by_side.1.a_ref, bf16[128,1024]{1,0:T(8,128)(2,1)} %copy-done.9, bf16[128,1024]{1,0:T(8,128)(2,1)} %copy-done.8, bf16[128,1024]{1,0:T(8,128)(2,1)} %copy-done.7, bf16[1,256,2048]{2,1,0:T(8,128)(2,1)} %get-tuple-element.28.refs_0_, ...), custom_call_target="tpu_custom_call" | custom-call | bytes 1310720 | tf_op jit(solution)/shard_map/summed_over_chips/pallas_call | solution.py:496
  182.5 1.9 collective-permute-start.20
  184.5 1.4 collective-permute-done.20.other_ref
  185.8 0.7 copy-done.6
  186.5 2.1 %unpack_weight.1 = f32[128,2048]{1,0:T(8,128)} custom-call(s32[6]{0:T(128)} %stack.23.place_ref, bf16[128,1024]{1,0:T(8,128)(2,1)} %summed_over_chips.1.own_ref, bf16[128,1024]{1,0:T(8,128)(2,1)} %copy-done.6), custom_call_target="tpu_custom_call" | custom-call | bytes 1572864 | tf_op jit(solution)/shard_map/unpack_weight/pallas_call | solution.py:114
  (44 shorter events, 0.1 us)
Async XLA Ops:
  7.2 65.7 %all-gather.2.cloned.1.call-start = ((), (), s32[]{:S(2)}) async-start(), calls=%async_computation.3 | async-start | bytes 4456448 | tf_op jit(solution)/shard_map/all_gather | solution.py:541
  14.2 6.0 %copy-start.17 = (s32[1,16,16]{2,1,0:T(8,128)S(1)}, s32[1,16,16]{2,1,0:T(8,128)}, u32[]{:S(2)}) copy-start(s32[1,16,16]{2,1,0:T(8,128)} %param.13) | copy-start | bytes 3076
  14.2 6.6 %copy-start.16 = (s32[1,16,16,7]{2,1,3,0:T(8,128)S(1)}, s32[1,16,16,7]{2,1,3,0:T(8,128)}, u32[]{:S(2)}) copy-start(s32[1,16,16,7]{2,1,3,0:T(8,128)} %param.12) | copy-start | bytes 21508
  14.2 43.5 %all-to-all-start = ((bf16[8,3,2,256,128]{4,3,2,1,0:T(8,128)(2,1)}), bf16[8,3,2,256,128]{4,3,2,1,0:T(8,128)(2,1)S(1)}, u32[]{:S(2)}, u32[]{:S(2)}) async-start(bf16[8,3,2,256,128]{4,3,2,1,0:T(8,128)(2,1)} %pack_heads.1.after_ref), calls=%async_computation | async-start | bytes 6291456 | tf_op jit(solution)/shard_map/all_to_all | solution.py:542
  20.1 52.7 %collective-permute-start.3 = (bf16[256,2048]{1,0:T(8,128)(2,1)}, bf16[256,2048]{1,0:T(8,128)(2,1)}, u32[]{:S(2)}, u32[]{:S(2)}) collective-permute-start(bf16[256,2048]{1,0:T(8,128)(2,1)} %bitcast.10), channel_id=1, source_target_pairs={{0,1},{1,0},{2,3},{3,2},{4,5},{5,4},{6,7},{7,6},{8,9},{9,8},{10,11... | collective-permute-start | bytes 3145736 | tf_op jit(solution)/shard_map/ppermute | solution.py:544
  57.7 1.8 copy-start
  70.1 9.0 %collective-permute-start = (bf16[2,512,128]{2,1,0:T(8,128)(2,1)}, bf16[2,512,128]{2,1,0:T(8,128)(2,1)S(1)}, u32[]{:S(2)}, u32[]{:S(2)}) collective-permute-start(bf16[2,512,128]{2,1,0:T(8,128)(2,1)} %get-tuple-element.33), channel_id=1, source_target_pairs={{0,2},{1,3},{2,4},{3,5},{4,6},{5,7},{6,0},{7,1},{8,10},{9,11},{10,... | collective-permute-start | bytes 786440 | tf_op jit(solution)/shard_map/ppermute | solution.py:546
  70.5 13.1 %collective-permute-start.1 = (bf16[2,512,128]{2,1,0:T(8,128)(2,1)}, bf16[2,512,128]{2,1,0:T(8,128)(2,1)S(1)}, u32[]{:S(2)}, u32[]{:S(2)}) collective-permute-start(bf16[2,512,128]{2,1,0:T(8,128)(2,1)} %get-tuple-element.34), channel_id=1, source_target_pairs={{0,4},{1,5},{2,6},{3,7},{4,0},{5,1},{6,2},{7,3},{8,12},{9,13},{10,... | collective-permute-start | bytes 786440 | tf_op jit(solution)/shard_map/ppermute | solution.py:546
  72.2 12.5 %collective-permute-start.2 = (bf16[2,512,128]{2,1,0:T(8,128)(2,1)}, bf16[2,512,128]{2,1,0:T(8,128)(2,1)S(1)}, u32[]{:S(2)}, u32[]{:S(2)}) collective-permute-start(bf16[2,512,128]{2,1,0:T(8,128)(2,1)} %get-tuple-element.35), channel_id=1, source_target_pairs={{0,6},{1,7},{2,0},{3,1},{4,2},{5,3},{6,4},{7,5},{8,14},{9,15},{10,... | collective-permute-start | bytes 786440 | tf_op jit(solution)/shard_map/ppermute | solution.py:546
  79.1 5.6 %copy-start.2 = (bf16[2,512,128]{2,1,0:T(8,128)(2,1)}, bf16[2,512,128]{2,1,0:T(8,128)(2,1)S(1)}, u32[]{:S(2)}) copy-start(bf16[2,512,128]{2,1,0:T(8,128)(2,1)S(1)} %collective-permute-done.refs_2_.refs_1_) | copy-start | bytes 786436
  83.5 1.1 copy-start.3
  84.6 0.7 copy-start.4
  85.3 18.8 %all-to-all-start.1 = ((bf16[4,2,512,128]{3,2,1,0:T(8,128)(2,1)}), bf16[4,2,512,128]{3,2,1,0:T(8,128)(2,1)S(1)}, u32[]{:S(2)}, u32[]{:S(2)}) async-start(bf16[4,2,512,128]{3,2,1,0:T(8,128)(2,1)} %gate.2), calls=%async_computation.1 | async-start | bytes 2097152 | tf_op jit(solution)/shard_map/all_to_all | solution.py:538
  95.7 25.0 %collective-permute-start.5 = (bf16[4,128,512]{2,1,0:T(8,128)(2,1)}, bf16[4,128,512]{2,1,0:T(8,128)(2,1)}, u32[]{:S(2)}, u32[]{:S(2)}) collective-permute-start(bf16[4,128,512]{2,1,0:T(8,128)(2,1)} %get-tuple-element.44), channel_id=1, source_target_pairs={{0,8},{8,16},{16,24},{24,0},{32,40},{40,48},{48,56},{56,32},{64,72... | collective-permute-start | bytes 1572872 | tf_op jit(solution)/shard_map/ppermute | solution.py:549
  97.5 41.0 %collective-permute-start.6 = (bf16[4,128,512]{2,1,0:T(8,128)(2,1)}, bf16[4,128,512]{2,1,0:T(8,128)(2,1)}, u32[]{:S(2)}, u32[]{:S(2)}) collective-permute-start(bf16[4,128,512]{2,1,0:T(8,128)(2,1)} %get-tuple-element.45), channel_id=1, source_target_pairs={{0,16},{8,24},{16,0},{24,8},{32,48},{40,56},{48,32},{56,40},{64,80... | collective-permute-start | bytes 1572872 | tf_op jit(solution)/shard_map/ppermute | solution.py:549
  100.6 38.2 %collective-permute-start.7 = (bf16[4,128,512]{2,1,0:T(8,128)(2,1)}, bf16[4,128,512]{2,1,0:T(8,128)(2,1)}, u32[]{:S(2)}, u32[]{:S(2)}) collective-permute-start(bf16[4,128,512]{2,1,0:T(8,128)(2,1)} %get-tuple-element.46), channel_id=1, source_target_pairs={{0,24},{8,0},{16,8},{24,16},{32,56},{40,32},{48,40},{56,48},{64,88... | collective-permute-start | bytes 1572872 | tf_op jit(solution)/shard_map/ppermute | solution.py:549
  101.4 37.5 %collective-permute-start.8 = (bf16[4,128,512]{2,1,0:T(8,128)(2,1)}, bf16[4,128,512]{2,1,0:T(8,128)(2,1)}, u32[]{:S(2)}, u32[]{:S(2)}) collective-permute-start(bf16[4,128,512]{2,1,0:T(8,128)(2,1)} %get-tuple-element.48), channel_id=1, source_target_pairs={{0,32},{8,40},{16,48},{24,56},{32,64},{40,72},{48,80},{56,88},{64,... | collective-permute-start | bytes 1572872 | tf_op jit(solution)/shard_map/ppermute | solution.py:550
  102.5 36.4 %collective-permute-start.9 = (bf16[4,128,512]{2,1,0:T(8,128)(2,1)}, bf16[4,128,512]{2,1,0:T(8,128)(2,1)}, u32[]{:S(2)}, u32[]{:S(2)}) collective-permute-start(bf16[4,128,512]{2,1,0:T(8,128)(2,1)} %get-tuple-element.49), channel_id=1, source_target_pairs={{0,96},{8,104},{16,112},{24,120},{32,0},{40,8},{48,16},{56,24},{64... | collective-permute-start | bytes 1572872 | tf_op jit(solution)/shard_map/ppermute | solution.py:550
  104.1 1.0 copy-start.5
  120.6 18.2 %collective-permute-start.10 = (bf16[4,128,512]{2,1,0:T(8,128)(2,1)}, bf16[4,128,512]{2,1,0:T(8,128)(2,1)S(1)}, u32[]{:S(2)}, u32[]{:S(2)}) collective-permute-start(bf16[4,128,512]{2,1,0:T(8,128)(2,1)} %gate.3), channel_id=1, source_target_pairs={{0,64},{8,72},{16,80},{24,88},{32,96},{40,104},{48,112},{56,120},{... | collective-permute-start | bytes 1572872 | tf_op jit(solution)/shard_map/ppermute | solution.py:553
  123.7 47.4 %all-to-all-start.2 = ((bf16[8,3,2,256,128]{4,3,2,1,0:T(8,128)(2,1)}), bf16[8,3,2,256,128]{4,3,2,1,0:T(8,128)(2,1)}, u32[]{:S(2)}, u32[]{:S(2)}) async-start(bf16[8,3,2,256,128]{4,3,2,1,0:T(8,128)(2,1)} %attention_backward.1.refs_5_.refs_1_), calls=%async_computation.2 | async-start | bytes 6291456 | tf_op jit(solution)/shard_map/all_to_all | solution.py:552
  138.5 30.1 %collective-permute-start.4 = (bf16[256,2048]{1,0:T(8,128)(2,1)}, bf16[256,2048]{1,0:T(8,128)(2,1)}, u32[]{:S(2)}, u32[]{:S(2)}) collective-permute-start(bf16[256,2048]{1,0:T(8,128)(2,1)} %get-tuple-element.40), channel_id=1, source_target_pairs={{0,1},{1,0},{2,3},{3,2},{4,5},{5,4},{6,7},{7,6},{8,9},{9,8},{10,11... | collective-permute-start | bytes 3145736 | tf_op jit(solution)/shard_map/ppermute | solution.py:557
  138.9 0.8 copy-start.18
  139.7 28.9 %copy-start.1 = (f32[256,2048]{1,0:T(8,128)S(1)}, f32[256,2048]{1,0:T(8,128)}, u32[]{:S(2)}) copy-start(f32[256,2048]{1,0:T(8,128)} %get-tuple-element.39) | copy-start | bytes 6291460
  143.2 9.2 %collective-permute-start.11 = (bf16[128,512]{1,0:T(8,128)(2,1)}, bf16[128,512]{1,0:T(8,128)(2,1)S(1)}, u32[]{:S(2)}, u32[]{:S(2)}) collective-permute-start(bf16[128,512]{1,0:T(8,128)(2,1)} %get-tuple-element.52), channel_id=1, source_target_pairs={{0,32},{8,40},{16,48},{24,56},{32,64},{40,72},{48,80},{56,88},{64,... | collective-permute-start | bytes 393224 | tf_op jit(solution)/shard_map/ppermute | solution.py:559
  143.6 9.9 %collective-permute-start.12 = (bf16[128,512]{1,0:T(8,128)(2,1)}, bf16[128,512]{1,0:T(8,128)(2,1)S(1)}, u32[]{:S(2)}, u32[]{:S(2)}) collective-permute-start(bf16[128,512]{1,0:T(8,128)(2,1)} %get-tuple-element.53), channel_id=1, source_target_pairs={{0,64},{8,72},{16,80},{24,88},{32,96},{40,104},{48,112},{56,120},{... | collective-permute-start | bytes 393224 | tf_op jit(solution)/shard_map/ppermute | solution.py:559
  145.0 10.3 %collective-permute-start.13 = (bf16[128,512]{1,0:T(8,128)(2,1)}, bf16[128,512]{1,0:T(8,128)(2,1)S(1)}, u32[]{:S(2)}, u32[]{:S(2)}) collective-permute-start(bf16[128,512]{1,0:T(8,128)(2,1)} %get-tuple-element.54), channel_id=1, source_target_pairs={{0,96},{8,104},{16,112},{24,120},{32,0},{40,8},{48,16},{56,24},{64... | collective-permute-start | bytes 393224 | tf_op jit(solution)/shard_map/ppermute | solution.py:559
  146.0 9.3 %collective-permute-start.14 = (bf16[128,512]{1,0:T(8,128)(2,1)}, bf16[128,512]{1,0:T(8,128)(2,1)S(1)}, u32[]{:S(2)}, u32[]{:S(2)}) collective-permute-start(bf16[128,512]{1,0:T(8,128)(2,1)} %get-tuple-element.56), channel_id=1, source_target_pairs={{0,8},{8,16},{16,24},{24,0},{32,40},{40,48},{48,56},{56,32},{64,72... | collective-permute-start | bytes 393224 | tf_op jit(solution)/shard_map/ppermute | solution.py:560
  152.4 6.5 %copy-start.10 = (bf16[128,512]{1,0:T(8,128)(2,1)}, bf16[128,512]{1,0:T(8,128)(2,1)S(1)}, u32[]{:S(2)}) copy-start(bf16[128,512]{1,0:T(8,128)(2,1)S(1)} %collective-permute-done.11.refs_1_) | copy-start | bytes 393220
  152.4 5.5 %collective-permute-start.15 = (bf16[128,512]{1,0:T(8,128)(2,1)}, bf16[128,512]{1,0:T(8,128)(2,1)S(1)}, u32[]{:S(2)}, u32[]{:S(2)}) collective-permute-start(bf16[128,512]{1,0:T(8,128)(2,1)} %get-tuple-element.57), channel_id=1, source_target_pairs={{0,16},{8,24},{16,0},{24,8},{32,48},{40,56},{48,32},{56,40},{64,80... | collective-permute-start | bytes 393224 | tf_op jit(solution)/shard_map/ppermute | solution.py:560
  153.4 5.4 %copy-start.11 = (bf16[128,512]{1,0:T(8,128)(2,1)}, bf16[128,512]{1,0:T(8,128)(2,1)S(1)}, u32[]{:S(2)}) copy-start(bf16[128,512]{1,0:T(8,128)(2,1)S(1)} %collective-permute-done.12.refs_2_) | copy-start | bytes 393220
  153.5 5.4 %collective-permute-start.16 = (bf16[128,512]{1,0:T(8,128)(2,1)}, bf16[128,512]{1,0:T(8,128)(2,1)S(1)}, u32[]{:S(2)}, u32[]{:S(2)}) collective-permute-start(bf16[128,512]{1,0:T(8,128)(2,1)} %get-tuple-element.58), channel_id=1, source_target_pairs={{0,24},{8,0},{16,8},{24,16},{32,56},{40,32},{48,40},{56,48},{64,88... | collective-permute-start | bytes 393224 | tf_op jit(solution)/shard_map/ppermute | solution.py:560
  155.4 3.5 %copy-start.12 = (bf16[128,512]{1,0:T(8,128)(2,1)}, bf16[128,512]{1,0:T(8,128)(2,1)S(1)}, u32[]{:S(2)}) copy-start(bf16[128,512]{1,0:T(8,128)(2,1)S(1)} %collective-permute-done.13.refs_3_) | copy-start | bytes 393220
  155.4 3.5 %copy-start.13 = (bf16[128,512]{1,0:T(8,128)(2,1)}, bf16[128,512]{1,0:T(8,128)(2,1)S(1)}, u32[]{:S(2)}) copy-start(bf16[128,512]{1,0:T(8,128)(2,1)S(1)} %collective-permute-done.14.refs_5_) | copy-start | bytes 393220
  157.9 1.0 copy-start.14
  158.8 0.6 copy-start.15
  161.6 18.0 %collective-permute-start.19 = (bf16[128,1024]{1,0:T(8,128)(2,1)}, bf16[128,1024]{1,0:T(8,128)(2,1)S(1)}, u32[]{:S(2)}, u32[]{:S(2)}) collective-permute-start(bf16[128,1024]{1,0:T(8,128)(2,1)} %summed_side_by_side.1.a_ref), channel_id=1, source_target_pairs={{0,6},{1,7},{2,4},{3,5},{4,2},{5,3},{6,0},{7,1},{8,14},{9,15},{10,... | collective-permute-start | bytes 786440 | tf_op jit(solution)/shard_map/ppermute | solution.py:563
  168.0 11.6 %collective-permute-start.18 = (bf16[128,1024]{1,0:T(8,128)(2,1)}, bf16[128,1024]{1,0:T(8,128)(2,1)S(1)}, u32[]{:S(2)}, u32[]{:S(2)}) collective-permute-start(bf16[128,1024]{1,0:T(8,128)(2,1)} %summed_side_by_side.1.a_ref), channel_id=1, source_target_pairs={{0,4},{1,5},{2,6},{3,7},{4,0},{5,1},{6,2},{7,3},{8,12},{9,13},{10,... | collective-permute-start | bytes 786440 | tf_op jit(solution)/shard_map/ppermute | solution.py:563
  168.4 11.2 %collective-permute-start.17 = (bf16[128,1024]{1,0:T(8,128)(2,1)}, bf16[128,1024]{1,0:T(8,128)(2,1)S(1)}, u32[]{:S(2)}, u32[]{:S(2)}) collective-permute-start(bf16[128,1024]{1,0:T(8,128)(2,1)} %summed_side_by_side.1.a_ref), channel_id=1, source_target_pairs={{0,2},{1,3},{2,0},{3,1},{4,6},{5,7},{6,4},{7,5},{8,10},{9,11},{10,... | collective-permute-start | bytes 786440 | tf_op jit(solution)/shard_map/ppermute | solution.py:563
  179.6 0.7 copy-start.7
  179.6 0.8 copy-start.8
  179.6 0.9 copy-start.9
  182.5 3.3 %collective-permute-start.20 = (bf16[128,1024]{1,0:T(8,128)(2,1)}, bf16[128,1024]{1,0:T(8,128)(2,1)S(1)}, u32[]{:S(2)}, u32[]{:S(2)}) collective-permute-start(bf16[128,1024]{1,0:T(8,128)(2,1)} %summed_over_chips.1.own_ref), channel_id=1, source_target_pairs={{0,1},{1,0},{2,3},{3,2},{4,5},{5,4},{6,7},{7,6},{8,9},{9,8},{10,11... | collective-permute-start | bytes 786440 | tf_op jit(solution)/shard_map/ppermute | solution.py:565
  185.8 0.7 copy-start.6
Sparse Core Ops, SparseCore 0:
  14.3 54.8 all-gather.1

commit v3 on v2

--- a/solution.py
+++ b/solution.py
@@ -31,25 +31,36 @@
     return pl.CostEstimate(flops=flops, bytes_accessed=moved, transcendentals=exps)
 
 
-def pack_kernel(q_ref, k_ref, v_ref, out_ref):
+def pack_kernel(q_ref, k_ref, v_ref, out_ref, rows_ref, in_sems, out_sems):
     seq, _, halves, _, width = out_ref.shape
-    for n, ref in enumerate((q_ref, k_ref, v_ref)):
+    loads = [pltpu.make_async_copy(ref.at[0], rows_ref.at[n], in_sems.at[n]) for n, ref in enumerate((q_ref, k_ref, v_ref))]
+    for load in loads:
+        load.start()
+    stores = []
+    for n, load in enumerate(loads):
+        load.wait()
         for s in range(seq):
             for half in range(halves):
-                column = (s + seq * half) * width
-                out_ref[s, n, half] = ref[0, :, column : column + width]
+                source = rows_ref.at[n, :, pl.ds((s + seq * half) * width, width)]
+                stores.append(pltpu.make_async_copy(source, out_ref.at[s, n, half], out_sems.at[len(stores)]))
+                stores[-1].start()
+    for store in stores:
+        store.wait()
 
 
 def pack(q, k, v, seq, head_dim):
     _, tokens, columns = q.shape
     halves = columns // (seq * head_dim)
-    rows = tokens // 4
     return pl.pallas_call(
         pack_kernel,
-        grid=(tokens // rows,),
         out_shape=jax.ShapeDtypeStruct((seq, 3, halves, tokens, head_dim), q.dtype),
-        in_specs=[pl.BlockSpec((1, rows, columns), lambda i: (0, i, 0))] * 3,
-        out_specs=pl.BlockSpec((seq, 3, halves, rows, head_dim), lambda i: (0, 0, 0, i, 0)),
+        in_specs=[HBM] * 3,
+        out_specs=HBM,
+        scratch_shapes=[
+            pltpu.VMEM((3, tokens, columns), q.dtype),
+            pltpu.SemaphoreType.DMA((3,)),
+            pltpu.SemaphoreType.DMA((3 * seq * halves,)),
+        ],
         compiler_params=pltpu.CompilerParams(vmem_limit_bytes=VMEM_LIMIT),
         cost_estimate=cost(0, 12 * tokens * columns),
         name="pack_heads",
@@ -85,22 +96,42 @@
     return [pl.multiple_of((2 * x + core + 2 * chips * half) * TILE, TILE) for x in range(chips) for half in range(2)]
 
 
-def pack_weight_kernel(chips, place_ref, in_ref, after_ref, out_ref):
+def pack_weight_kernel(chips, place_ref, in_ref, *out_refs):
     for i, column in enumerate(core_columns(place_ref[2], chips)):
-        out_ref[:, pl.ds(i * TILE, TILE)] = in_ref[:, pl.ds(column, TILE)]
-
-
-def pack_weight(place, shard, after, chips):
+        out_refs[i // chips][:, pl.ds(i % chips * TILE, TILE)] = in_ref[:, pl.ds(column, TILE)]
+
+
+def pack_weight(place, shard, chips):
     rows, columns = shard.shape
     return pl.pallas_call(
         functools.partial(pack_weight_kernel, chips),
-        out_shape=jax.ShapeDtypeStruct((rows, columns // 2), shard.dtype),
-        in_specs=[SMEM, VMEM, HBM],
-        out_specs=VMEM,
+        out_shape=(jax.ShapeDtypeStruct((rows, columns // 4), shard.dtype),) * 2,
+        in_specs=[SMEM, VMEM],
+        out_specs=(VMEM,) * 2,
         compiler_params=pltpu.CompilerParams(vmem_limit_bytes=VMEM_LIMIT),
         cost_estimate=cost(0, 3 * rows * columns),
         name="pack_weight",
-    )(place, shard, after)
+    )(place, shard)
+
+
+def stack_kernel(*refs):
+    count = len(refs) // 2 - 1
+    for n in range(2):
+        for k in range(count):
+            refs[2 * count + n][k] = refs[n * count + k][...]
+
+
+def stack_lines(first, second):
+    shape = (len(first), *first[0].shape)
+    return pl.pallas_call(
+        stack_kernel,
+        out_shape=(jax.ShapeDtypeStruct(shape, first[0].dtype),) * 2,
+        in_specs=[VMEM] * (2 * len(first)),
+        out_specs=(VMEM,) * 2,
+        compiler_params=pltpu.CompilerParams(vmem_limit_bytes=VMEM_LIMIT),
+        cost_estimate=cost(0, 8 * math.prod(shape)),
+        name="stack_lines",
+    )(*first, *second)
 
 
 def unpack_weight_kernel(chips, place_ref, own_ref, other_ref, out_ref):
@@ -215,14 +246,18 @@
             pltpu.VMEM((UNITS_AT_ONCE * slots, TILE, TILE), F32),
             pltpu.VMEM((UNITS_AT_ONCE, slots * TILE, 2 * TILE), BF16),
         ],
-        compiler_params=pltpu.CompilerParams(vmem_limit_bytes=VMEM_LIMIT),
-        cost_estimate=cost(16 * units * slots * TILE**3, 6 * MIB, units * slots * TILE * TILE),
+        compiler_params=pltpu.CompilerParams(vmem_limit_bytes=20 * MIB),
+        cost_estimate=cost(3*10**11, MIB),
         name="attention_forward",
     )(place, tiles, counts, qkv)
 
 
 def backward_kernel(multi, slots, units, width, scale, place_ref, tiles_ref, counts_ref, qkv_ref, g_ref, a_ref, lse_ref, *refs):
-    out_ref, kt_ref, dk_acc, dv_acc, s_ref, dp_ref, p_ref, d_ref = refs[-8:]
+    out_ref, kt_ref, dk_acc, dv_acc, s_ref, dp_ref, p_ref, d_ref = refs[-12:-4]
+    loads = [pltpu.make_async_copy(ref, refs[n - 4], refs[-1].at[n]) for n, ref in enumerate((g_ref, a_ref, lse_ref))]
+    for load in loads:
+        load.start()
+    g_ref, a_ref, lse_ref = refs[-4:-1]
     scale2 = scale * math.log2(math.e)
     q_ref, k_ref, v_ref = (qkv_ref.at[:, n] for n in range(3))
     dq_ref, dk_ref, dv_ref = (out_ref.at[:, n] for n in range(3))
@@ -233,6 +268,9 @@
             kt_ref[half * units + t] = rows_of(k_ref, half, t)[...].T
             dk_acc[half * units + t] = jnp.zeros((TILE, TILE), F32)
             dv_acc[half * units + t] = jnp.zeros((TILE, TILE), F32)
+
+    for load in loads:
+        load.wait()
 
     @pl.loop(0, units // multi)
     def _(step):
@@ -283,7 +321,7 @@
     return pl.pallas_call(
         functools.partial(backward_kernel, UNITS_AT_ONCE, slots, units, width, 1.0 / math.sqrt(head_dim)),
         out_shape=jax.ShapeDtypeStruct(qkv.shape, BF16),
-        in_specs=[SMEM] * 3 + [VMEM] * 4 + [HBM] * len(after),
+        in_specs=[SMEM] * 3 + [VMEM] + [HBM] * (3 + len(after)),
         out_specs=VMEM,
         scratch_shapes=[
             pltpu.VMEM((halves * units, head_dim, TILE), BF16),
@@ -293,6 +331,10 @@
             pltpu.VMEM((UNITS_AT_ONCE * slots, TILE, TILE), F32),
             pltpu.VMEM((UNITS_AT_ONCE * slots, TILE, TILE), BF16),
             pltpu.VMEM((UNITS_AT_ONCE, slots * TILE, 2 * TILE), BF16),
+            pltpu.VMEM(g.shape, g.dtype),
+            pltpu.VMEM(a.shape, a.dtype),
+            pltpu.VMEM(lse.shape, lse.dtype),
+            pltpu.SemaphoreType.DMA((3,)),
         ],
         compiler_params=pltpu.CompilerParams(vmem_limit_bytes=VMEM_LIMIT),
         cost_estimate=cost(3*10**11, MIB),
@@ -300,88 +342,110 @@
     )(place, tiles, counts, qkv, g, a, lse, *after)
 
 
-def grad_attn_kernel(place_ref, own_ref, other_ref, w_ref, after_ref, g_ref):
+def block_row(place_ref, side, ky, kz):
+    y = lax.rem(place_ref[3] + side - ky, side)
+    z = lax.rem(place_ref[4] + side - kz, side)
+    return pl.multiple_of((y * side + z) * TILE, TILE)
+
+
+def grad_attn_kernel(side, chips, place_ref, own_ref, other_ref, *refs):
+    w_refs, g_ref = refs[: 2 * side], refs[-1]
     tokens = own_ref.shape[0]
     core = place_ref[2]
-    rows = jnp.concatenate([own_ref[...], other_ref[...]], axis=0)
-    g = mm(rows, w_ref[...]).astype(BF16)
-    for slot, first in ((core, 0), (1 - core, tokens)):
-        target = pl.ds(pl.multiple_of(slot * tokens, tokens), tokens)
-        for half in range(2):
-            g_ref[0, half, target, :] = g[first : first + tokens, half * TILE : (half + 1) * TILE]
-
-
-def grad_attn(place, own, other, weights, after, chips):
+    for part in range(2):
+        total = None
+        for i in range(side):
+            starts = [block_row(place_ref, side, *((i, j) if part == 0 else (j, i))) for j in range(side)]
+            rows = [jnp.concatenate([ref[:, pl.ds(start, TILE)] for start in starts], axis=1) for ref in (own_ref, other_ref)]
+            w = w_refs[part * side + i][...]
+            step = mm(jnp.concatenate(rows, axis=0), w.reshape(side * TILE, w.shape[2]))
+            total = step if total is None else total + step
+        g = total.astype(BF16)
+        for n in range(chips):
+            x, half = divmod(part * chips + n, 2)
+            for slot, first in ((core, 0), (1 - core, tokens)):
+                target = pl.ds(pl.multiple_of(slot * tokens, tokens), tokens)
+                g_ref[x, half, target, :] = g[first : first + tokens, n * TILE : (n + 1) * TILE]
+
+
+def grad_attn(place, own, other, weights, after, side, chips):
     tokens, depth = own.shape
-    columns = weights.shape[1]
-    block = columns // chips
-    return pl.pallas_call(
-        grad_attn_kernel,
-        grid=(chips,),
+    columns = 2 * weights[0].shape[2]
+    return pl.pallas_call(
+        functools.partial(grad_attn_kernel, side, chips),
         out_shape=jax.ShapeDtypeStruct((chips, 2, 2 * tokens, TILE), BF16),
-        in_specs=[
-            SMEM,
-            pl.BlockSpec((tokens, depth), lambda i: (0, 0)),
-            pl.BlockSpec((tokens, depth), lambda i: (0, 0)),
-            pl.BlockSpec((depth, block), lambda i: (0, i)),
-            HBM,
-        ],
-        out_specs=pl.BlockSpec((1, 2, 2 * tokens, TILE), lambda i: (i, 0, 0, 0)),
+        in_specs=[SMEM] + [VMEM] * (2 + len(weights)) + [HBM],
+        out_specs=VMEM,
         compiler_params=pltpu.CompilerParams(vmem_limit_bytes=VMEM_LIMIT),
         cost_estimate=cost(4 * tokens * depth * columns, 7 * MIB),
         name="grad_attn",
-    )(place, own, other, weights, after)
-
-
-def gather_rows(place_ref, block_refs, rows_ref):
+    )(place, own, other, *weights, after)
+
+
+def row_copies(place_ref, block_refs, rows_ref, sems):
     chips = len(block_refs)
     halves, rows, width = block_refs[0].shape
     tokens = rows // 2
     core = place_ref[2]
+    copies = []
     for k, ref in enumerate(block_refs):
         chip = lax.rem(place_ref[5] + chips - k, chips)
         for half in range(halves):
             target = pl.ds(pl.multiple_of((chip * halves + half) * width, width), width)
             for slot, first in ((core, 0), (1 - core, tokens)):
-                source = pl.ds(pl.multiple_of(slot * tokens, tokens), tokens)
-                rows_ref[first : first + tokens, target] = ref[half, source, :]
-
-
-def project_kernel(place_ref, *refs):
-    block_refs, w_ref, own_ref, other_ref, rows_ref = refs[:-5], refs[-5], refs[-3], refs[-2], refs[-1]
-
-    @pl.when(pl.program_id(0) == 0)
-    def _():
-        gather_rows(place_ref, block_refs, rows_ref)
-
+                source = ref.at[half, pl.ds(pl.multiple_of(slot * tokens, tokens), tokens), :]
+                copies.append(pltpu.make_async_copy(source, rows_ref.at[pl.ds(first, tokens), target], sems.at[len(copies)]))
+    return copies
+
+
+def project_kernel(side, place_ref, *refs):
+    block_refs, w_refs, (own_ref, other_ref, rows_ref, sems) = refs[: -5 - 2 * side], refs[-5 - 2 * side : -5], refs[-4:]
+    copies = row_copies(place_ref, block_refs, rows_ref, sems)
+    for copy in copies:
+        copy.start()
+    for copy in copies:
+        copy.wait()
     tokens = own_ref.shape[0]
-    out = mm(rows_ref[...], w_ref[...], NT)
-    own_ref[...] = out[:tokens]
-    other_ref[...] = out[tokens:].astype(BF16)
-
-
-def project(place, blocks, weights, after):
-    features, columns = weights.shape
+    for ky in range(side):
+        for kz in range(0, side, 2):
+            first = w_refs[ky][kz : kz + 2]
+            second = jnp.concatenate([w_refs[side + kz][ky], w_refs[side + kz + 1][ky]], axis=0)
+            w = jnp.concatenate([first.reshape(second.shape), second], axis=1)
+            out = mm(rows_ref[...], w, NT)
+            for n in range(2):
+                target = pl.ds(block_row(place_ref, side, ky, kz + n), TILE)
+                block = out[:, n * TILE : (n + 1) * TILE]
+                own_ref[:, target] = block[:tokens]
+                other_ref[:, target] = block[tokens:].astype(BF16)
+
+
+def project(place, blocks, weights, after, side):
+    features = side * side * weights[0].shape[1]
+    columns = 2 * weights[0].shape[2]
     tokens = blocks[0].shape[1] // 2
-    step = 2 * TILE
-    return pl.pallas_call(
-        project_kernel,
-        grid=(features // step,),
+    return pl.pallas_call(
+        functools.partial(project_kernel, side),
         out_shape=(jax.ShapeDtypeStruct((tokens, features), F32), jax.ShapeDtypeStruct((tokens, features), BF16)),
-        in_specs=[SMEM]
-        + [pl.BlockSpec(block.shape, lambda i: (0, 0, 0)) for block in blocks]
-        + [pl.BlockSpec((step, columns), lambda i: (i, 0)), HBM],
-        out_specs=(pl.BlockSpec((tokens, step), lambda i: (0, i)),) * 2,
-        scratch_shapes=[pltpu.VMEM((2 * tokens, columns), BF16)],
+        in_specs=[SMEM] + [HBM] * len(blocks) + [VMEM] * len(weights) + [HBM],
+        out_specs=(VMEM, VMEM),
+        scratch_shapes=[pltpu.VMEM((2 * tokens, columns), BF16), pltpu.SemaphoreType.DMA((4 * len(blocks),))],
         compiler_params=pltpu.CompilerParams(vmem_limit_bytes=VMEM_LIMIT),
         cost_estimate=cost(4 * tokens * features * columns, 8 * MIB),
         name="project",
-    )(place, *blocks, weights, after)
+    )(place, *blocks, *weights, after)
 
 
 def grad_weight_kernel(side, chips, place_ref, own_ref, other_ref, *refs):
-    block_refs, out_refs, (rows_ref, part_ref, sems) = refs[:chips], refs[chips:-3], refs[-3:]
-    gather_rows(place_ref, block_refs, rows_ref)
+    block_refs, out_refs, (rows_ref, grad_ref, part_ref, sems, load_sems) = refs[:chips], refs[chips:-5], refs[-5:]
+    tokens = own_ref.shape[0]
+    loads = row_copies(place_ref, block_refs, rows_ref, load_sems)
+    for n, ref in enumerate((own_ref, other_ref)):
+        target = grad_ref.at[pl.ds(n * tokens, tokens), :]
+        loads.append(pltpu.make_async_copy(ref, target, load_sems.at[len(loads)]))
+    for load in loads:
+        load.start()
+    for load in loads:
+        load.wait()
     rows = part_ref.shape[2]
     half = part_ref.shape[3]
     copies = [pltpu.make_async_copy(part_ref.at[n], out_refs[n], sems.at[n]) for n in range(2 * side)]
@@ -389,8 +453,7 @@
         for kz in range(side):
             row = lax.rem(place_ref[3] + ky, side) * side + lax.rem(place_ref[4] + kz, side)
             columns = pl.ds(pl.multiple_of(row * rows, rows), rows)
-            left = jnp.concatenate([own_ref[:, columns], other_ref[:, columns]], axis=0)
-            part = mm(left, rows_ref[...], TN)
+            part = mm(grad_ref[:, columns], rows_ref[...], TN)
             part_ref[kz, ky] = part[:, :half].astype(BF16)
             part_ref[side + ky, kz] = part[:, half:].astype(BF16)
             if ky == side - 1:
@@ -408,12 +471,14 @@
     return pl.pallas_call(
         functools.partial(grad_weight_kernel, side, chips),
         out_shape=(jax.ShapeDtypeStruct((side, rows, columns // 2), BF16),) * (2 * side),
-        in_specs=[SMEM] + [VMEM] * (2 + chips),
+        in_specs=[SMEM] + [HBM] * (2 + chips),
         out_specs=(HBM,) * (2 * side),
         scratch_shapes=[
             pltpu.VMEM((2 * tokens, columns), BF16),
+            pltpu.VMEM((2 * tokens, features), BF16),
             pltpu.VMEM((2 * side, side, rows, columns // 2), BF16),
             pltpu.SemaphoreType.DMA((2 * side,)),
+            pltpu.SemaphoreType.DMA((4 * chips + 2,)),
         ],
         compiler_params=pltpu.CompilerParams(vmem_limit_bytes=VMEM_LIMIT),
         cost_estimate=cost(4 * tokens * features * columns, 7 * MIB),
@@ -429,8 +494,8 @@
     return pl.pallas_call(
         gate_kernel,
         out_shape=jax.ShapeDtypeStruct(values.shape, values.dtype),
-        in_specs=[ANY] * (1 + len(after)),
-        out_specs=ANY,
+        in_specs=[HBM] * (1 + len(after)),
+        out_specs=HBM,
         input_output_aliases={0: 0},
         compiler_params=pltpu.CompilerParams(vmem_limit_bytes=VMEM_LIMIT),
         name="gate",
@@ -537,14 +602,20 @@
     def over_chips(values):
         return lax.all_to_all(values, "seq", split_axis=0, concat_axis=0, tiled=True, axis_index_groups=same_core)
 
+    shard_z, shard_y = pack_weight(place, out_weight, chips)
+    lines_z, lines_y = stack_lines(
+        [shard_z] + [lax.ppermute(shard_z, "dp", z_shift(k)) for k in range(1, side)],
+        [shard_y] + [lax.ppermute(shard_y, "dp", y_shift(k)) for k in range(1, side)],
+    )
+    weights = [lines_z] + [lax.ppermute(lines_z, "dp", y_shift(k)) for k in range(1, side)]
+    weights += [lines_y] + [lax.ppermute(lines_y, "dp", z_shift(k)) for k in range(1, side)]
     packed = pack(queries, key_states, value_states, seq, head_dim)
-    weights = lax.all_gather(pack_weight(place, out_weight, packed, chips), "dp", axis=0, tiled=True)
     qkv = lax.all_to_all(packed, "seq", split_axis=0, concat_axis=0, tiled=True)
     own_rows = grad_output[0]
     other_rows = lax.ppermute(own_rows, "seq", across)
     a, lse, *a_blocks = attention_forward(place, lists, counts, qkv, chips, width)
     a_home = [a_blocks[0]] + [lax.ppermute(a_blocks[k], "seq", x_shift(k)) for k in range(1, chips)]
-    g = over_chips(gate(grad_attn(place, own_rows, other_rows, weights, lse, chips), *a_home))
+    g = over_chips(gate(grad_attn(place, own_rows, other_rows, weights, lse, side, chips), *a_home))
     parts = grad_weight_parts(place, own_rows, other_rows, a_home, side)
     z_first = [parts[0]] + [lax.ppermute(parts[k], "dp", z_shift(k)) for k in range(1, side)]
     y_first = [parts[side]] + [lax.ppermute(parts[side + k], "dp", y_shift(k)) for k in (1, side - 1)]
@@ -553,7 +624,7 @@
     y_first += [lax.ppermute(gate(parts[side + k], grads), "dp", y_shift(k)) for k in range(2, side - 1)]
 
     z_sum, y_sum = summed(z_first, y_first)
-    out_own, out_other = project(place, a_home, weights, grads)
+    out_own, out_other = project(place, a_home, weights, grads, side)
     output = (out_own + lax.ppermute(out_other, "seq", across).astype(F32)).astype(BF16)
     chip_share = summed_side_by_side(
         [z_sum[0]] + [lax.ppermute(z_sum[k], "dp", y_shift(k)) for k in range(1, side)],

time: 196 us -> 184 us (0.939)
  starting transfers between devices: 48.1 us -> 71 us
  waiting for transfers between devices: 55.1 us -> 33.2 us
  between operations: 14.2 us -> 1 us
    all_to_all x1, waiting for transfers between devices: 35.9 us -> 0.01 us  [per_device(): qkv = lax.all_to_all(packed, 'seq', split_axis=0, concat_axis=0, tiled=True)]
    ppermute x0 -> x12, waiting for transfers between devices: none -> 20.8 us  [the longest x3 7.05 us: per_device(): lax.ppermute(lines_y, 'dp', z_shift(k))]
    ppermute x0 -> x12, starting transfers between devices: none -> 16.6 us  [the longest x3 6.47 us: per_device(): lax.ppermute(lines_y, 'dp', z_shift(k))]
    ppermute x3, waiting for transfers between devices: 5.55 us -> 0.01 us  [per_device(): lax.ppermute(a_blocks[k], 'seq', x_shift(k))]
    ppermute x3, waiting for transfers between devices: 4.76 us -> 0.91 us  [per_device(): lax.ppermute(z_sum[k], 'dp', y_shift(k))]
    ppermute x2, starting transfers between devices: 2.77 us -> 6.37 us  [per_device(): lax.ppermute(parts[side + k], 'dp', y_shift(k))]
    ppermute x3, starting transfers between devices: 2.78 us -> 5.61 us  [per_device(): lax.ppermute(a_blocks[k], 'seq', x_shift(k))]
    pallas_call x1, Pallas kernels: 10.6 us -> 7.86 us  [attention_forward(): pl.pallas_call(functools.partial(forward_kernel, UNITS_AT_ONCE, slots, un...]
  transfers between devices with their start and end apart: 25 -> 36, of which waited for: 8 -> 13; matrix products, arithmetic and copies ran while one was open for 2% -> 2% of each run, Pallas kernels for 29% -> 32%
where the time goes in v3:
time: 184 us; the launch traced here: 183 us
  starting transfers between devices  71 us (39%)
  Pallas kernels  65.9 us (36%)
  waiting for transfers between devices  33.2 us (18%)
  local copies, waits for them, and re-layouts  9.6 us (5%)
  other arithmetic  2.48 us (1%)
    pallas_call x1, Pallas kernels, attention_backward(): pl.pallas_call(functools.partial(backward_kernel, UNITS_AT_ONCE, slots, u...  15.8 us
    unnamed x63, local copies, waits for them, and re-layouts  8.67 us
    all_to_all x1, starting transfers between devices, per_device(): lax.all_to_all(grads, 'seq', split_axis=0, concat_axis=0, tiled=True)  7.94 us
    pallas_call x1, Pallas kernels, attention_forward(): pl.pallas_call(functools.partial(forward_kernel, UNITS_AT_ONCE, slots, un...  7.86 us
    pallas_call x1, Pallas kernels, project(): pl.pallas_call(functools.partial(project_kernel, side), out_shape=(jax.Sh...  7.84 us
    ppermute x3, waiting for transfers between devices, per_device(): lax.ppermute(lines_y, 'dp', z_shift(k))  7.05 us
    ppermute x3, waiting for transfers between devices, per_device(): lax.ppermute(chip_share, 'seq', x_swap(k))  6.5 us
    pallas_call x1, Pallas kernels, grad_weight_parts(): pl.pallas_call(functools.partial(grad_weight_kernel, side, chips), out_sh...  6.47 us
  transfers between devices with their start and end apart: 36, of which 13 were waited for; matrix products, arithmetic and copies ran while one was open for 2% of the time, Pallas kernels for 32%

profile of v3, /device:TPU:1, one launch (start us, length us, event | category | flops | bytes accessed | tf_op | source)
XLA Modules:
  0.0 183.2 jit_solution(10659849069931837815)
XLA Ops:
  0.6 3.4 %pack_heads.1 = bf16[8,3,2,256,128]{4,3,2,1,0:T(8,128)(2,1)} custom-call(bf16[1,256,2048]{2,1,0:T(8,128)(2,1)} %q_ref.1, bf16[1,256,2048]{2,1,0:T(8,128)(2,1)} %k_ref.1, bf16[1,256,2048]{2,1,0:T(8,128)(2,1)} %v_ref.1), custom_call_target="tpu_custom_call" | custom-call | bytes 6291456 | tf_op jit(solution)/shard_map/pack_heads/pallas_call | solution.py:54
  4.0 5.9 %all-to-all-start = ((bf16[8,3,2,256,128]{4,3,2,1,0:T(8,128)(2,1)}), bf16[8,3,2,256,128]{4,3,2,1,0:T(8,128)(2,1)S(1)}, u32[]{:S(2)}, u32[]{:S(2)}) async-start(bf16[8,3,2,256,128]{4,3,2,1,0:T(8,128)(2,1)} %pack_heads.1), calls=%async_computation | async-start | bytes 6291456 | tf_op jit(solution)/shard_map/all_to_all | solution.py:613
  10.0 0.7 stack.23.place_ref
  10.6 1.8 pack_weight.1
  12.4 3.8 %collective-permute-start.5 = (bf16[128,512]{1,0:T(8,128)(2,1)}, bf16[128,512]{1,0:T(8,128)(2,1)S(1)}, u32[]{:S(2)}, u32[]{:S(2)}) collective-permute-start(bf16[128,512]{1,0:T(8,128)(2,1)} %get-tuple-element.40.refs_0_), channel_id=1, source_target_pairs={{0,24},{8,0},{16,8},{24,16},{32,56},{40,32},{48,40},{56,48},{64,88... | collective-permute-start | bytes 393224 | tf_op jit(solution)/shard_map/ppermute | solution.py:607
  16.2 0.7 collective-permute-start.3
  16.9 2.7 %collective-permute-start.8 = (bf16[128,512]{1,0:T(8,128)(2,1)}, bf16[128,512]{1,0:T(8,128)(2,1)S(1)}, u32[]{:S(2)}, u32[]{:S(2)}) collective-permute-start(bf16[128,512]{1,0:T(8,128)(2,1)} %get-tuple-element.41.refs_4_), channel_id=1, source_target_pairs={{0,96},{8,104},{16,112},{24,120},{32,0},{40,8},{48,16},{56,24},{64... | collective-permute-start | bytes 393224 | tf_op jit(solution)/shard_map/ppermute | solution.py:608
  20.0 2.3 %collective-permute-done.5.refs_3_ = bf16[128,512]{1,0:T(8,128)(2,1)S(1)} collective-permute-done((bf16[128,512]{1,0:T(8,128)(2,1)}, bf16[128,512]{1,0:T(8,128)(2,1)S(1)}, u32[]{:S(2)}, u32[]{:S(2)}) %collective-permute-start.5) | collective-permute-done | bytes 131104 | tf_op jit(solution)/shard_map/ppermute | solution.py:607
  22.3 1.3 collective-permute-start.6
  23.6 2.0 %collective-permute-done.3.refs_1_ = bf16[128,512]{1,0:T(8,128)(2,1)S(1)} collective-permute-done((bf16[128,512]{1,0:T(8,128)(2,1)}, bf16[128,512]{1,0:T(8,128)(2,1)S(1)}, u32[]{:S(2)}, u32[]{:S(2)}) %collective-permute-start.3) | collective-permute-done | bytes 131104 | tf_op jit(solution)/shard_map/ppermute | solution.py:607
  25.6 3.6 %collective-permute-done.6.refs_5_ = bf16[128,512]{1,0:T(8,128)(2,1)S(1)} collective-permute-done((bf16[128,512]{1,0:T(8,128)(2,1)}, bf16[128,512]{1,0:T(8,128)(2,1)S(1)}, u32[]{:S(2)}, u32[]{:S(2)}) %collective-permute-start.6) | collective-permute-done | bytes 131104 | tf_op jit(solution)/shard_map/ppermute | solution.py:608
  29.3 0.6 copy-done.27
  29.9 2.3 %stack_lines.1 = (bf16[4,128,512]{2,1,0:T(8,128)(2,1)}, bf16[4,128,512]{2,1,0:T(8,128)(2,1)}) custom-call(bf16[128,512]{1,0:T(8,128)(2,1)} %get-tuple-element.40.refs_0_, bf16[128,512]{1,0:T(8,128)(2,1)} %copy-done.24, bf16[128,512]{1,0:T(8,128)(2,1)} %copy-done.23, bf16[128,512]{1,0:T(8,128)(2,1)} %copy-done.22, ...), custom_call_target="tpu_custom_call" | custom-call | bytes 2097152 | tf_op jit(solution)/shard_map/stack_lines/pallas_call | solution.py:126
  32.8 2.2 %collective-permute-start.15 = (bf16[256,2048]{1,0:T(8,128)(2,1)}, bf16[256,2048]{1,0:T(8,128)(2,1)}, u32[]{:S(2)}, u32[]{:S(2)}) collective-permute-start(bf16[256,2048]{1,0:T(8,128)(2,1)} %bitcast.10), channel_id=1, source_target_pairs={{0,1},{1,0},{2,3},{3,2},{4,5},{5,4},{6,7},{7,6},{8,9},{9,8},{10,11... | collective-permute-start | bytes 3145736 | tf_op jit(solution)/shard_map/ppermute | solution.py:615
  35.5 0.8 collective-permute-start.9
  36.2 3.3 %collective-permute-start.14 = (bf16[4,128,512]{2,1,0:T(8,128)(2,1)}, bf16[4,128,512]{2,1,0:T(8,128)(2,1)}, u32[]{:S(2)}, u32[]{:S(2)}) collective-permute-start(bf16[4,128,512]{2,1,0:T(8,128)(2,1)} %get-tuple-element.43.refs_4_.refs_8_), channel_id=1, source_target_pairs={{0,24},{8,0},{16,8},{24,16},{32,56},{40,32},{48,40},{56,48},{64,88... | collective-permute-start | bytes 1572872 | tf_op jit(solution)/shard_map/ppermute | solution.py:611
  39.5 5.4 %collective-permute-done.11.refs_3_.refs_7_ = bf16[4,128,512]{2,1,0:T(8,128)(2,1)} collective-permute-done((bf16[4,128,512]{2,1,0:T(8,128)(2,1)}, bf16[4,128,512]{2,1,0:T(8,128)(2,1)}, u32[]{:S(2)}, u32[]{:S(2)}) %collective-permute-start.11) | collective-permute-done | bytes 524320 | tf_op jit(solution)/shard_map/ppermute | solution.py:610
  45.0 3.2 %collective-permute-start.13 = (bf16[4,128,512]{2,1,0:T(8,128)(2,1)}, bf16[4,128,512]{2,1,0:T(8,128)(2,1)}, u32[]{:S(2)}, u32[]{:S(2)}) collective-permute-start(bf16[4,128,512]{2,1,0:T(8,128)(2,1)} %get-tuple-element.43.refs_4_.refs_8_), channel_id=1, source_target_pairs={{0,16},{8,24},{16,0},{24,8},{32,48},{40,56},{48,32},{56,40},{64,80... | collective-permute-start | bytes 1572872 | tf_op jit(solution)/shard_map/ppermute | solution.py:611
  48.1 0.7 copy-done.2
  48.8 7.9 %attention_forward.1 = (bf16[4,2,512,128]{3,2,1,0:T(8,128)(2,1)S(1)}, f32[32,8,128]{2,1,0:T(8,128)S(1)}, bf16[2,512,128]{2,1,0:T(8,128)(2,1)S(1)}, bf16[2,512,12...) custom-call(s32[6]{0:T(128)S(1)} %copy-done.2, ...), custom_call_target="tpu_custom_call" | custom-call | flops 299999985664 | bytes 1048576 | tf_op jit(solution)/shard_map/attention_forward/pallas_call | solution.py:235
  56.7 0.7 copy-done.1
  57.4 0.7 copy-done.5
  58.1 1.0 copy-done.6
  59.4 1.9 %collective-permute-start = (bf16[2,512,128]{2,1,0:T(8,128)(2,1)S(1)}, bf16[2,512,128]{2,1,0:T(8,128)(2,1)S(1)}, u32[]{:S(2)}, u32[]{:S(2)}) collective-permute-start(bf16[2,512,128]{2,1,0:T(8,128)(2,1)S(1)} %get-tuple-element.37), channel_id=1, source_target_pairs={{0,2},{1,3},{2,4},{3,5},{4,6},{5,7},{6,0},{7,1},{8,10},{9,11},{10,... | collective-permute-start | bytes 786440 | tf_op jit(solution)/shard_map/ppermute | solution.py:617
  61.3 0.7 collective-permute-done.14.refs_7_.refs_11_
  62.0 2.8 %collective-permute-start.1 = (bf16[2,512,128]{2,1,0:T(8,128)(2,1)S(1)}, bf16[2,512,128]{2,1,0:T(8,128)(2,1)S(1)}, u32[]{:S(2)}, u32[]{:S(2)}) collective-permute-start(bf16[2,512,128]{2,1,0:T(8,128)(2,1)S(1)} %get-tuple-element.38), channel_id=1, source_target_pairs={{0,4},{1,5},{2,6},{3,7},{4,0},{5,1},{6,2},{7,3},{8,12},{9,13},{10,... | collective-permute-start | bytes 786440 | tf_op jit(solution)/shard_map/ppermute | solution.py:617
  64.8 0.9 collective-permute-start.2
  65.7 6.4 %collective-permute-done.12.refs_5_.refs_9_ = bf16[4,128,512]{2,1,0:T(8,128)(2,1)} collective-permute-done((bf16[4,128,512]{2,1,0:T(8,128)(2,1)}, bf16[4,128,512]{2,1,0:T(8,128)(2,1)}, u32[]{:S(2)}, u32[]{:S(2)}) %collective-permute-start.12) | collective-permute-done | bytes 524320 | tf_op jit(solution)/shard_map/ppermute | solution.py:611
  72.0 6.2 %grad_attn.1.refs_0_ = bf16[4,2,512,128]{3,2,1,0:T(8,128)(2,1)} custom-call(s32[6]{0:T(128)} %stack.23.place_ref, bf16[256,2048]{1,0:T(8,128)(2,1)} %bitcast.11, bf16[256,2048]{1,0:T(8,128)(2,1)} %collective-permute-done.15.other_ref, bf16[4,128,512]{2,1,0:T(8,128)(2,1)} %get-tuple-element.42.refs_0_.refs_4_, ...), custom_call_target="tpu_custom_call" | custom-call | flops 2147483648 | bytes 7340032 | tf_op jit(solution)/shard_map/grad_attn/pallas_call | solution.py:374
  78.3 0.7 copy-done.8
  79.2 5.1 %all-to-all-start.1 = ((bf16[4,2,512,128]{3,2,1,0:T(8,128)(2,1)}), bf16[4,2,512,128]{3,2,1,0:T(8,128)(2,1)S(1)}, u32[]{:S(2)}, u32[]{:S(2)}) async-start(bf16[4,2,512,128]{3,2,1,0:T(8,128)(2,1)} %gate.2), calls=%async_computation.1 | async-start | bytes 2097152 | tf_op jit(solution)/shard_map/all_to_all | solution.py:603
  84.3 6.5 %grad_weight_parts.1 = (bf16[4,128,512]{2,1,0:T(8,128)(2,1)}, bf16[4,128,512]{2,1,0:T(8,128)(2,1)}, bf16[4,128,512]{2,1,0:T(8,128)(2,1)}, bf16[4,128,512]{2,1,0:...) custom-call(s32[6]{0:T(128)} %stack.23.place_ref, ...), custom_call_target="tpu_custom_call" | custom-call | flops 2147483648 | bytes 7340032 | tf_op jit(solution)/shard_map/grad_weight_parts/pallas_call | solution.py:471
  90.9 2.2 %collective-permute-start.18 = (bf16[4,128,512]{2,1,0:T(8,128)(2,1)}, bf16[4,128,512]{2,1,0:T(8,128)(2,1)}, u32[]{:S(2)}, u32[]{:S(2)}) collective-permute-start(bf16[4,128,512]{2,1,0:T(8,128)(2,1)} %get-tuple-element.53), channel_id=1, source_target_pairs={{0,16},{8,24},{16,0},{24,8},{32,48},{40,56},{48,32},{56,40},{64,80... | collective-permute-start | bytes 1572872 | tf_op jit(solution)/shard_map/ppermute | solution.py:620
  93.1 0.9 collective-permute-start.19
  94.0 3.7 %collective-permute-start.20 = (bf16[4,128,512]{2,1,0:T(8,128)(2,1)}, bf16[4,128,512]{2,1,0:T(8,128)(2,1)}, u32[]{:S(2)}, u32[]{:S(2)}) collective-permute-start(bf16[4,128,512]{2,1,0:T(8,128)(2,1)} %get-tuple-element.56), channel_id=1, source_target_pairs={{0,32},{8,40},{16,48},{24,56},{32,64},{40,72},{48,80},{56,88},{64,... | collective-permute-start | bytes 1572872 | tf_op jit(solution)/shard_map/ppermute | solution.py:621
  97.7 2.7 %collective-permute-start.21 = (bf16[4,128,512]{2,1,0:T(8,128)(2,1)}, bf16[4,128,512]{2,1,0:T(8,128)(2,1)}, u32[]{:S(2)}, u32[]{:S(2)}) collective-permute-start(bf16[4,128,512]{2,1,0:T(8,128)(2,1)} %get-tuple-element.57), channel_id=1, source_target_pairs={{0,96},{8,104},{16,112},{24,120},{32,0},{40,8},{48,16},{56,24},{64... | collective-permute-start | bytes 1572872 | tf_op jit(solution)/shard_map/ppermute | solution.py:621
  100.4 1.0 copy-done.11
  101.4 15.8 %attention_backward.1.refs_12_.refs_1_ = bf16[8,3,2,256,128]{4,3,2,1,0:T(8,128)(2,1)} custom-call(s32[6]{0:T(128)} %stack.23.place_ref, s32[1792]{0:T(1024)} %copy-done.3, s32[256]{0:T(256)} %copy-done.4, bf16[8,3,2,256,128]{4,3,2,1,0:T(8,128)(2,1)} %copy-done, bf16[4,2,512,128]{3,2,1,0:T(8,128)(2,1)} %copy-done.11, bf16[4,2,512,128]{3,2,1,0:T(8,128)(2,1)} %copy-done.6, ...), custom_call_target="tpu_custom_call" | custom-call | flops 299999985664 | bytes 1048576 | tf_op jit(solution)/shard_map/attention_backward/pallas_call | solution.py:321
  117.2 1.2 collective-permute-start.22
  118.4 7.9 %all-to-all-start.2 = ((bf16[8,3,2,256,128]{4,3,2,1,0:T(8,128)(2,1)}), bf16[8,3,2,256,128]{4,3,2,1,0:T(8,128)(2,1)}, u32[]{:S(2)}, u32[]{:S(2)}) async-start(bf16[8,3,2,256,128]{4,3,2,1,0:T(8,128)(2,1)} %attention_backward.1.refs_12_.refs_1_), calls=%async_computation.2 | async-start | bytes 6291456 | tf_op jit(solution)/shard_map/all_to_all | solution.py:623
  126.4 7.8 %project.1 = (f32[256,2048]{1,0:T(8,128)}, bf16[256,2048]{1,0:T(8,128)(2,1)}) custom-call(s32[6]{0:T(128)} %stack.23.place_ref, bf16[2,512,128]{2,1,0:T(8,128)(2,1)} %copy-done.1, bf16[2,512,128]{2,1,0:T(8,128)(2,1)} %copy-done.8, bf16[2,512,128]{2,1,0:T(8,128)(2,1)} %copy-done.9, bf16[2,512,128]{2,1,0:T(8,128)(2,1)} %copy-done.10, ...), custom_call_target="tpu_custom_call" | custom-call | flops 2147483648 | bytes 8388608 | tf_op jit(solution)/shard_map/project/pallas_call | solution.py:426
  134.4 0.8 copy-done.30
  135.2 3.5 %summed.1 = (bf16[128,512]{1,0:T(8,128)(2,1)}, bf16[128,512]{1,0:T(8,128)(2,1)}, bf16[128,512]{1,0:T(8,128)(2,1)}, bf16[128,512]{1,0:T(8,128)(2,1)}, bf16[128,51...) custom-call(bf16[4,128,512]{2,1,0:T(8,128)(2,1)} %get-tuple-element.46.refs_0_, ...), custom_call_target="tpu_custom_call" | custom-call | flops 999999995904 | bytes 1048576 | tf_op jit(solution)/shard_map/summed/pallas_call | solution.py:518
  138.6 1.2 collective-permute-start.23
  139.8 1.4 collective-permute-start.24
  141.2 1.3 collective-permute-start.25
  142.5 1.8 collective-permute-start.26
  144.3 0.6 collective-permute-done.23.refs_1_
  144.9 2.2 %collective-permute-start.27 = (bf16[128,512]{1,0:T(8,128)(2,1)}, bf16[128,512]{1,0:T(8,128)(2,1)S(1)}, u32[]{:S(2)}, u32[]{:S(2)}) collective-permute-start(bf16[128,512]{1,0:T(8,128)(2,1)} %get-tuple-element.65), channel_id=1, source_target_pairs={{0,16},{8,24},{16,0},{24,8},{32,48},{40,56},{48,32},{56,40},{64,80... | collective-permute-start | bytes 393224 | tf_op jit(solution)/shard_map/ppermute | solution.py:631
  147.3 2.3 %collective-permute-start.28 = (bf16[128,512]{1,0:T(8,128)(2,1)}, bf16[128,512]{1,0:T(8,128)(2,1)S(1)}, u32[]{:S(2)}, u32[]{:S(2)}) collective-permute-start(bf16[128,512]{1,0:T(8,128)(2,1)} %get-tuple-element.66), channel_id=1, source_target_pairs={{0,24},{8,0},{16,8},{24,16},{32,56},{40,32},{48,40},{56,48},{64,88... | collective-permute-start | bytes 393224 | tf_op jit(solution)/shard_map/ppermute | solution.py:631
  149.7 2.5 %collective-permute-done.27.refs_6_ = bf16[128,512]{1,0:T(8,128)(2,1)S(1)} collective-permute-done((bf16[128,512]{1,0:T(8,128)(2,1)}, bf16[128,512]{1,0:T(8,128)(2,1)S(1)}, u32[]{:S(2)}, u32[]{:S(2)}) %collective-permute-start.27) | collective-permute-done | bytes 131104 | tf_op jit(solution)/shard_map/ppermute | solution.py:631
  152.2 1.2 collective-permute-done.28.refs_7_
  153.4 0.6 copy-done.21
  154.0 2.1 %summed_side_by_side.1.a_ref = bf16[128,1024]{1,0:T(8,128)(2,1)} custom-call(bf16[128,512]{1,0:T(8,128)(2,1)} %get-tuple-element.59.refs_0_, bf16[128,512]{1,0:T(8,128)(2,1)} %copy-done.16, bf16[128,512]{1,0:T(8,128)(2,1)} %copy-done.17, bf16[128,512]{1,0:T(8,128)(2,1)} %copy-done.18, bf16[128,512]{1,0:T(8,128)(2,1)} %get-tuple-element.63.refs_4_, ...), custom_call_target="tpu_custom_call" | custom-call | bytes 1310720 | tf_op jit(solution)/shard_map/summed_side_by_side/pallas_call | solution.py:543
  156.1 5.4 %collective-permute-start.31 = (bf16[128,1024]{1,0:T(8,128)(2,1)}, bf16[128,1024]{1,0:T(8,128)(2,1)S(1)}, u32[]{:S(2)}, u32[]{:S(2)}) collective-permute-start(bf16[128,1024]{1,0:T(8,128)(2,1)} %summed_side_by_side.1.a_ref), channel_id=1, source_target_pairs={{0,6},{1,7},{2,4},{3,5},{4,2},{5,3},{6,0},{7,1},{8,14},{9,15},{10,... | collective-permute-start | bytes 786440 | tf_op jit(solution)/shard_map/ppermute | solution.py:634
  162.1 2.5 %add_convert_fusion.refs_1_ = bf16[256,2048]{1,0:T(8,128)(2,1)} fusion(f32[256,2048]{1,0:T(8,128)S(1)} %copy-done.7, bf16[256,2048]{1,0:T(8,128)(2,1)} %collective-permute-done.16), kind=kLoop, calls=%fused_computation | loop fusion | flops 1572864 | bytes 4194304 | tf_op jit(solution)/shard_map/convert_element_type | solution.py:628
  164.6 4.5 %unpack_heads.1 = (bf16[1,256,2048]{2,1,0:T(8,128)(2,1)}, bf16[1,256,2048]{2,1,0:T(8,128)(2,1)}, bf16[1,256,2048]{2,1,0:T(8,128)(2,1)}) custom-call(bf16[8,3,2,256,128]{4,3,2,1,0:T(8,128)(2,1)} %all-to-all-done.2.in_ref), custom_call_target="tpu_custom_call" | custom-call | bytes 6291456 | tf_op jit(solution)/shard_map/unpack_heads/pallas_call | solution.py:83
  169.1 6.5 %collective-permute-done.31.d_ref = bf16[128,1024]{1,0:T(8,128)(2,1)S(1)} collective-permute-done((bf16[128,1024]{1,0:T(8,128)(2,1)}, bf16[128,1024]{1,0:T(8,128)(2,1)S(1)}, u32[]{:S(2)}, u32[]{:S(2)}) %collective-permute-start.31) | collective-permute-done | bytes 262176 | tf_op jit(solution)/shard_map/ppermute | solution.py:634
  175.6 0.7 copy-done.13
  176.4 2.0 %summed_over_chips.1.own_ref = bf16[128,1024]{1,0:T(8,128)(2,1)} custom-call(bf16[128,1024]{1,0:T(8,128)(2,1)} %summed_side_by_side.1.a_ref, bf16[128,1024]{1,0:T(8,128)(2,1)} %copy-done.15, bf16[128,1024]{1,0:T(8,128)(2,1)} %copy-done.14, bf16[128,1024]{1,0:T(8,128)(2,1)} %copy-done.13, bf16[1,256,2048]{2,1,0:T(8,128)(2,1)} %get-tuple-element.32.refs_0_, ...), custom_call_target="tpu_custom_call" | custom-call | bytes 1310720 | tf_op jit(solution)/shard_map/summed_over_chips/pallas_call | solution.py:561
  178.5 0.5 collective-permute-start.32
  179.0 1.4 collective-permute-done.32.other_ref
  180.3 0.7 copy-done.12
  181.0 2.1 %unpack_weight.1 = f32[128,2048]{1,0:T(8,128)} custom-call(s32[6]{0:T(128)} %stack.23.place_ref, bf16[128,1024]{1,0:T(8,128)(2,1)} %summed_over_chips.1.own_ref, bf16[128,1024]{1,0:T(8,128)(2,1)} %copy-done.12), custom_call_target="tpu_custom_call" | custom-call | bytes 1572864 | tf_op jit(solution)/shard_map/unpack_weight/pallas_call | solution.py:145
  (90 shorter events, 3.3 us)
Async XLA Ops:
  4.0 31.0 %copy-start.29 = (s32[1,16,16]{2,1,0:T(8,128)S(1)}, s32[1,16,16]{2,1,0:T(8,128)}, u32[]{:S(2)}) copy-start(s32[1,16,16]{2,1,0:T(8,128)} %param.13) | copy-start | bytes 3076
  4.0 31.1 %copy-start.28 = (s32[1,16,16,7]{2,1,3,0:T(8,128)S(1)}, s32[1,16,16,7]{2,1,3,0:T(8,128)}, u32[]{:S(2)}) copy-start(s32[1,16,16,7]{2,1,3,0:T(8,128)} %param.12) | copy-start | bytes 21508
  4.0 44.1 %all-to-all-start = ((bf16[8,3,2,256,128]{4,3,2,1,0:T(8,128)(2,1)}), bf16[8,3,2,256,128]{4,3,2,1,0:T(8,128)(2,1)S(1)}, u32[]{:S(2)}, u32[]{:S(2)}) async-start(bf16[8,3,2,256,128]{4,3,2,1,0:T(8,128)(2,1)} %pack_heads.1), calls=%async_computation | async-start | bytes 6291456 | tf_op jit(solution)/shard_map/all_to_all | solution.py:613
  12.4 9.8 %collective-permute-start.5 = (bf16[128,512]{1,0:T(8,128)(2,1)}, bf16[128,512]{1,0:T(8,128)(2,1)S(1)}, u32[]{:S(2)}, u32[]{:S(2)}) collective-permute-start(bf16[128,512]{1,0:T(8,128)(2,1)} %get-tuple-element.40.refs_0_), channel_id=1, source_target_pairs={{0,24},{8,0},{16,8},{24,16},{32,56},{40,32},{48,40},{56,48},{64,88... | collective-permute-start | bytes 393224 | tf_op jit(solution)/shard_map/ppermute | solution.py:607
  16.2 7.4 %collective-permute-start.4 = (bf16[128,512]{1,0:T(8,128)(2,1)}, bf16[128,512]{1,0:T(8,128)(2,1)S(1)}, u32[]{:S(2)}, u32[]{:S(2)}) collective-permute-start(bf16[128,512]{1,0:T(8,128)(2,1)} %get-tuple-element.40.refs_0_), channel_id=1, source_target_pairs={{0,16},{8,24},{16,0},{24,8},{32,48},{40,56},{48,32},{56,40},{64,80... | collective-permute-start | bytes 393224 | tf_op jit(solution)/shard_map/ppermute | solution.py:607
  16.2 9.4 %collective-permute-start.3 = (bf16[128,512]{1,0:T(8,128)(2,1)}, bf16[128,512]{1,0:T(8,128)(2,1)S(1)}, u32[]{:S(2)}, u32[]{:S(2)}) collective-permute-start(bf16[128,512]{1,0:T(8,128)(2,1)} %get-tuple-element.40.refs_0_), channel_id=1, source_target_pairs={{0,8},{8,16},{16,24},{24,0},{32,40},{40,48},{48,56},{56,32},{64,72... | collective-permute-start | bytes 393224 | tf_op jit(solution)/shard_map/ppermute | solution.py:607
  16.9 8.7 %collective-permute-start.8 = (bf16[128,512]{1,0:T(8,128)(2,1)}, bf16[128,512]{1,0:T(8,128)(2,1)S(1)}, u32[]{:S(2)}, u32[]{:S(2)}) collective-permute-start(bf16[128,512]{1,0:T(8,128)(2,1)} %get-tuple-element.41.refs_4_), channel_id=1, source_target_pairs={{0,96},{8,104},{16,112},{24,120},{32,0},{40,8},{48,16},{56,24},{64... | collective-permute-start | bytes 393224 | tf_op jit(solution)/shard_map/ppermute | solution.py:608
  19.6 6.0 %collective-permute-start.7 = (bf16[128,512]{1,0:T(8,128)(2,1)}, bf16[128,512]{1,0:T(8,128)(2,1)S(1)}, u32[]{:S(2)}, u32[]{:S(2)}) collective-permute-start(bf16[128,512]{1,0:T(8,128)(2,1)} %get-tuple-element.41.refs_4_), channel_id=1, source_target_pairs={{0,64},{8,72},{16,80},{24,88},{32,96},{40,104},{48,112},{56,120},{... | collective-permute-start | bytes 393224 | tf_op jit(solution)/shard_map/ppermute | solution.py:608
  22.3 7.0 %copy-start.22 = (bf16[128,512]{1,0:T(8,128)(2,1)}, bf16[128,512]{1,0:T(8,128)(2,1)S(1)}, u32[]{:S(2)}) copy-start(bf16[128,512]{1,0:T(8,128)(2,1)S(1)} %collective-permute-done.5.refs_3_) | copy-start | bytes 393220
  22.3 7.0 %collective-permute-start.6 = (bf16[128,512]{1,0:T(8,128)(2,1)}, bf16[128,512]{1,0:T(8,128)(2,1)S(1)}, u32[]{:S(2)}, u32[]{:S(2)}) collective-permute-start(bf16[128,512]{1,0:T(8,128)(2,1)} %get-tuple-element.41.refs_4_), channel_id=1, source_target_pairs={{0,32},{8,40},{16,48},{24,56},{32,64},{40,72},{48,80},{56,88},{64,... | collective-permute-start | bytes 393224 | tf_op jit(solution)/shard_map/ppermute | solution.py:608
  23.6 5.7 %copy-start.23 = (bf16[128,512]{1,0:T(8,128)(2,1)}, bf16[128,512]{1,0:T(8,128)(2,1)S(1)}, u32[]{:S(2)}) copy-start(bf16[128,512]{1,0:T(8,128)(2,1)S(1)} %collective-permute-done.4.refs_2_) | copy-start | bytes 393220
  25.6 3.7 %copy-start.24 = (bf16[128,512]{1,0:T(8,128)(2,1)}, bf16[128,512]{1,0:T(8,128)(2,1)S(1)}, u32[]{:S(2)}) copy-start(bf16[128,512]{1,0:T(8,128)(2,1)S(1)} %collective-permute-done.3.refs_1_) | copy-start | bytes 393220
  25.6 3.7 %copy-start.25 = (bf16[128,512]{1,0:T(8,128)(2,1)}, bf16[128,512]{1,0:T(8,128)(2,1)S(1)}, u32[]{:S(2)}) copy-start(bf16[128,512]{1,0:T(8,128)(2,1)S(1)} %collective-permute-done.8.refs_7_) | copy-start | bytes 393220
  25.6 3.7 %copy-start.26 = (bf16[128,512]{1,0:T(8,128)(2,1)}, bf16[128,512]{1,0:T(8,128)(2,1)S(1)}, u32[]{:S(2)}) copy-start(bf16[128,512]{1,0:T(8,128)(2,1)S(1)} %collective-permute-done.7.refs_6_) | copy-start | bytes 393220
  32.2 12.7 %collective-permute-start.11 = (bf16[4,128,512]{2,1,0:T(8,128)(2,1)}, bf16[4,128,512]{2,1,0:T(8,128)(2,1)}, u32[]{:S(2)}, u32[]{:S(2)}) collective-permute-start(bf16[4,128,512]{2,1,0:T(8,128)(2,1)} %get-tuple-element.42.refs_0_.refs_4_), channel_id=1, source_target_pairs={{0,96},{8,104},{16,112},{24,120},{32,0},{40,8},{48,16},{56,24},{64... | collective-permute-start | bytes 1572872 | tf_op jit(solution)/shard_map/ppermute | solution.py:610
  32.4 15.7 %collective-permute-start.10 = (bf16[4,128,512]{2,1,0:T(8,128)(2,1)}, bf16[4,128,512]{2,1,0:T(8,128)(2,1)}, u32[]{:S(2)}, u32[]{:S(2)}) collective-permute-start(bf16[4,128,512]{2,1,0:T(8,128)(2,1)} %get-tuple-element.42.refs_0_.refs_4_), channel_id=1, source_target_pairs={{0,64},{8,72},{16,80},{24,88},{32,96},{40,104},{48,112},{56,120},{... | collective-permute-start | bytes 1572872 | tf_op jit(solution)/shard_map/ppermute | solution.py:610
  32.8 39.3 %collective-permute-start.15 = (bf16[256,2048]{1,0:T(8,128)(2,1)}, bf16[256,2048]{1,0:T(8,128)(2,1)}, u32[]{:S(2)}, u32[]{:S(2)}) collective-permute-start(bf16[256,2048]{1,0:T(8,128)(2,1)} %bitcast.10), channel_id=1, source_target_pairs={{0,1},{1,0},{2,3},{3,2},{4,5},{5,4},{6,7},{7,6},{8,9},{9,8},{10,11... | collective-permute-start | bytes 3145736 | tf_op jit(solution)/shard_map/ppermute | solution.py:615
  35.1 21.6 %copy-start.4 = (s32[256]{0:T(256)}, s32[256]{0:T(256)S(1)}, u32[]{:S(2)}) copy-start(s32[256]{0:T(256)S(1)} %reshape.17.counts_ref) | copy-start | bytes 3076
  35.5 21.2 %copy-start.3 = (s32[1792]{0:T(1024)}, s32[1792]{0:T(1024)S(1)}, u32[]{:S(2)}) copy-start(s32[1792]{0:T(1024)S(1)} %reshape.16.tiles_ref) | copy-start | bytes 21508
  35.5 23.9 %collective-permute-start.9 = (bf16[4,128,512]{2,1,0:T(8,128)(2,1)}, bf16[4,128,512]{2,1,0:T(8,128)(2,1)}, u32[]{:S(2)}, u32[]{:S(2)}) collective-permute-start(bf16[4,128,512]{2,1,0:T(8,128)(2,1)} %get-tuple-element.42.refs_0_.refs_4_), channel_id=1, source_target_pairs={{0,32},{8,40},{16,48},{24,56},{32,64},{40,72},{48,80},{56,88},{64,... | collective-permute-start | bytes 1572872 | tf_op jit(solution)/shard_map/ppermute | solution.py:610
  36.2 25.8 %collective-permute-start.14 = (bf16[4,128,512]{2,1,0:T(8,128)(2,1)}, bf16[4,128,512]{2,1,0:T(8,128)(2,1)}, u32[]{:S(2)}, u32[]{:S(2)}) collective-permute-start(bf16[4,128,512]{2,1,0:T(8,128)(2,1)} %get-tuple-element.43.refs_4_.refs_8_), channel_id=1, source_target_pairs={{0,24},{8,0},{16,8},{24,16},{32,56},{40,32},{48,40},{56,48},{64,88... | collective-permute-start | bytes 1572872 | tf_op jit(solution)/shard_map/ppermute | solution.py:611
  45.0 19.8 %collective-permute-start.13 = (bf16[4,128,512]{2,1,0:T(8,128)(2,1)}, bf16[4,128,512]{2,1,0:T(8,128)(2,1)}, u32[]{:S(2)}, u32[]{:S(2)}) collective-permute-start(bf16[4,128,512]{2,1,0:T(8,128)(2,1)} %get-tuple-element.43.refs_4_.refs_8_), channel_id=1, source_target_pairs={{0,16},{8,24},{16,0},{24,8},{32,48},{40,56},{48,32},{56,40},{64,80... | collective-permute-start | bytes 1572872 | tf_op jit(solution)/shard_map/ppermute | solution.py:611
  48.1 23.9 %collective-permute-start.12 = (bf16[4,128,512]{2,1,0:T(8,128)(2,1)}, bf16[4,128,512]{2,1,0:T(8,128)(2,1)}, u32[]{:S(2)}, u32[]{:S(2)}) collective-permute-start(bf16[4,128,512]{2,1,0:T(8,128)(2,1)} %get-tuple-element.43.refs_4_.refs_8_), channel_id=1, source_target_pairs={{0,8},{8,16},{16,24},{24,0},{32,40},{40,48},{48,56},{56,32},{64,72... | collective-permute-start | bytes 1572872 | tf_op jit(solution)/shard_map/ppermute | solution.py:611
  48.1 0.7 copy-start.2
  48.8 7.9 %copy-start = (bf16[8,3,2,256,128]{4,3,2,1,0:T(8,128)(2,1)}, bf16[8,3,2,256,128]{4,3,2,1,0:T(8,128)(2,1)S(1)}, u32[]{:S(2)}) copy-start(bf16[8,3,2,256,128]{4,3,2,1,0:T(8,128)(2,1)S(1)} %all-to-all-done.qkv_ref) | copy-start | bytes 9437188
  56.7 0.7 copy-start.1
  58.1 1.0 copy-start.6
  59.4 18.9 %collective-permute-start = (bf16[2,512,128]{2,1,0:T(8,128)(2,1)S(1)}, bf16[2,512,128]{2,1,0:T(8,128)(2,1)S(1)}, u32[]{:S(2)}, u32[]{:S(2)}) collective-permute-start(bf16[2,512,128]{2,1,0:T(8,128)(2,1)S(1)} %get-tuple-element.37), channel_id=1, source_target_pairs={{0,2},{1,3},{2,4},{3,5},{4,6},{5,7},{6,0},{7,1},{8,10},{9,11},{10,... | collective-permute-start | bytes 786440 | tf_op jit(solution)/shard_map/ppermute | solution.py:617
  62.0 16.3 %collective-permute-start.1 = (bf16[2,512,128]{2,1,0:T(8,128)(2,1)S(1)}, bf16[2,512,128]{2,1,0:T(8,128)(2,1)S(1)}, u32[]{:S(2)}, u32[]{:S(2)}) collective-permute-start(bf16[2,512,128]{2,1,0:T(8,128)(2,1)S(1)} %get-tuple-element.38), channel_id=1, source_target_pairs={{0,4},{1,5},{2,6},{3,7},{4,0},{5,1},{6,2},{7,3},{8,12},{9,13},{10,... | collective-permute-start | bytes 786440 | tf_op jit(solution)/shard_map/ppermute | solution.py:617
  64.8 13.5 %collective-permute-start.2 = (bf16[2,512,128]{2,1,0:T(8,128)(2,1)S(1)}, bf16[2,512,128]{2,1,0:T(8,128)(2,1)S(1)}, u32[]{:S(2)}, u32[]{:S(2)}) collective-permute-start(bf16[2,512,128]{2,1,0:T(8,128)(2,1)S(1)} %get-tuple-element.39), channel_id=1, source_target_pairs={{0,6},{1,7},{2,0},{3,1},{4,2},{5,3},{6,4},{7,5},{8,14},{9,15},{10,... | collective-permute-start | bytes 786440 | tf_op jit(solution)/shard_map/ppermute | solution.py:617
  78.3 0.7 copy-start.8
  78.3 0.8 copy-start.9
  78.3 0.9 copy-start.10
  79.2 21.2 %all-to-all-start.1 = ((bf16[4,2,512,128]{3,2,1,0:T(8,128)(2,1)}), bf16[4,2,512,128]{3,2,1,0:T(8,128)(2,1)S(1)}, u32[]{:S(2)}, u32[]{:S(2)}) async-start(bf16[4,2,512,128]{3,2,1,0:T(8,128)(2,1)} %gate.2), calls=%async_computation.1 | async-start | bytes 2097152 | tf_op jit(solution)/shard_map/all_to_all | solution.py:603
  90.8 26.4 %collective-permute-start.17 = (bf16[4,128,512]{2,1,0:T(8,128)(2,1)}, bf16[4,128,512]{2,1,0:T(8,128)(2,1)}, u32[]{:S(2)}, u32[]{:S(2)}) collective-permute-start(bf16[4,128,512]{2,1,0:T(8,128)(2,1)} %get-tuple-element.52), channel_id=1, source_target_pairs={{0,8},{8,16},{16,24},{24,0},{32,40},{40,48},{48,56},{56,32},{64,72... | collective-permute-start | bytes 1572872 | tf_op jit(solution)/shard_map/ppermute | solution.py:620
  90.9 43.4 %collective-permute-start.18 = (bf16[4,128,512]{2,1,0:T(8,128)(2,1)}, bf16[4,128,512]{2,1,0:T(8,128)(2,1)}, u32[]{:S(2)}, u32[]{:S(2)}) collective-permute-start(bf16[4,128,512]{2,1,0:T(8,128)(2,1)} %get-tuple-element.53), channel_id=1, source_target_pairs={{0,16},{8,24},{16,0},{24,8},{32,48},{40,56},{48,32},{56,40},{64,80... | collective-permute-start | bytes 1572872 | tf_op jit(solution)/shard_map/ppermute | solution.py:620
  93.1 41.2 %collective-permute-start.19 = (bf16[4,128,512]{2,1,0:T(8,128)(2,1)}, bf16[4,128,512]{2,1,0:T(8,128)(2,1)}, u32[]{:S(2)}, u32[]{:S(2)}) collective-permute-start(bf16[4,128,512]{2,1,0:T(8,128)(2,1)} %get-tuple-element.54), channel_id=1, source_target_pairs={{0,24},{8,0},{16,8},{24,16},{32,56},{40,32},{48,40},{56,48},{64,88... | collective-permute-start | bytes 1572872 | tf_op jit(solution)/shard_map/ppermute | solution.py:620
  94.0 40.3 %collective-permute-start.20 = (bf16[4,128,512]{2,1,0:T(8,128)(2,1)}, bf16[4,128,512]{2,1,0:T(8,128)(2,1)}, u32[]{:S(2)}, u32[]{:S(2)}) collective-permute-start(bf16[4,128,512]{2,1,0:T(8,128)(2,1)} %get-tuple-element.56), channel_id=1, source_target_pairs={{0,32},{8,40},{16,48},{24,56},{32,64},{40,72},{48,80},{56,88},{64,... | collective-permute-start | bytes 1572872 | tf_op jit(solution)/shard_map/ppermute | solution.py:621
  97.7 36.6 %collective-permute-start.21 = (bf16[4,128,512]{2,1,0:T(8,128)(2,1)}, bf16[4,128,512]{2,1,0:T(8,128)(2,1)}, u32[]{:S(2)}, u32[]{:S(2)}) collective-permute-start(bf16[4,128,512]{2,1,0:T(8,128)(2,1)} %get-tuple-element.57), channel_id=1, source_target_pairs={{0,96},{8,104},{16,112},{24,120},{32,0},{40,8},{48,16},{56,24},{64... | collective-permute-start | bytes 1572872 | tf_op jit(solution)/shard_map/ppermute | solution.py:621
  100.4 1.0 copy-start.11
  117.2 17.2 %collective-permute-start.22 = (bf16[4,128,512]{2,1,0:T(8,128)(2,1)}, bf16[4,128,512]{2,1,0:T(8,128)(2,1)S(1)}, u32[]{:S(2)}, u32[]{:S(2)}) collective-permute-start(bf16[4,128,512]{2,1,0:T(8,128)(2,1)} %gate.3), channel_id=1, source_target_pairs={{0,64},{8,72},{16,80},{24,88},{32,96},{40,104},{48,112},{56,120},{... | collective-permute-start | bytes 1572872 | tf_op jit(solution)/shard_map/ppermute | solution.py:624
  118.4 46.1 %all-to-all-start.2 = ((bf16[8,3,2,256,128]{4,3,2,1,0:T(8,128)(2,1)}), bf16[8,3,2,256,128]{4,3,2,1,0:T(8,128)(2,1)}, u32[]{:S(2)}, u32[]{:S(2)}) async-start(bf16[8,3,2,256,128]{4,3,2,1,0:T(8,128)(2,1)} %attention_backward.1.refs_12_.refs_1_), calls=%async_computation.2 | async-start | bytes 6291456 | tf_op jit(solution)/shard_map/all_to_all | solution.py:623
  134.2 27.8 %collective-permute-start.16 = (bf16[256,2048]{1,0:T(8,128)(2,1)}, bf16[256,2048]{1,0:T(8,128)(2,1)}, u32[]{:S(2)}, u32[]{:S(2)}) collective-permute-start(bf16[256,2048]{1,0:T(8,128)(2,1)} %get-tuple-element.48), channel_id=1, source_target_pairs={{0,1},{1,0},{2,3},{3,2},{4,5},{5,4},{6,7},{7,6},{8,9},{9,8},{10,11... | collective-permute-start | bytes 3145736 | tf_op jit(solution)/shard_map/ppermute | solution.py:628
  134.4 0.8 copy-start.30
  135.2 26.9 %copy-start.7 = (f32[256,2048]{1,0:T(8,128)S(1)}, f32[256,2048]{1,0:T(8,128)}, u32[]{:S(2)}) copy-start(f32[256,2048]{1,0:T(8,128)} %get-tuple-element.47) | copy-start | bytes 6291460
  138.6 6.2 %collective-permute-start.23 = (bf16[128,512]{1,0:T(8,128)(2,1)}, bf16[128,512]{1,0:T(8,128)(2,1)S(1)}, u32[]{:S(2)}, u32[]{:S(2)}) collective-permute-start(bf16[128,512]{1,0:T(8,128)(2,1)} %get-tuple-element.60), channel_id=1, source_target_pairs={{0,32},{8,40},{16,48},{24,56},{32,64},{40,72},{48,80},{56,88},{64,... | collective-permute-start | bytes 393224 | tf_op jit(solution)/shard_map/ppermute | solution.py:630
  139.8 7.5 %collective-permute-start.24 = (bf16[128,512]{1,0:T(8,128)(2,1)}, bf16[128,512]{1,0:T(8,128)(2,1)S(1)}, u32[]{:S(2)}, u32[]{:S(2)}) collective-permute-start(bf16[128,512]{1,0:T(8,128)(2,1)} %get-tuple-element.61), channel_id=1, source_target_pairs={{0,64},{8,72},{16,80},{24,88},{32,96},{40,104},{48,112},{56,120},{... | collective-permute-start | bytes 393224 | tf_op jit(solution)/shard_map/ppermute | solution.py:630
  141.2 8.5 %collective-permute-start.25 = (bf16[128,512]{1,0:T(8,128)(2,1)}, bf16[128,512]{1,0:T(8,128)(2,1)S(1)}, u32[]{:S(2)}, u32[]{:S(2)}) collective-permute-start(bf16[128,512]{1,0:T(8,128)(2,1)} %get-tuple-element.62), channel_id=1, source_target_pairs={{0,96},{8,104},{16,112},{24,120},{32,0},{40,8},{48,16},{56,24},{64... | collective-permute-start | bytes 393224 | tf_op jit(solution)/shard_map/ppermute | solution.py:630
  142.5 7.2 %collective-permute-start.26 = (bf16[128,512]{1,0:T(8,128)(2,1)}, bf16[128,512]{1,0:T(8,128)(2,1)S(1)}, u32[]{:S(2)}, u32[]{:S(2)}) collective-permute-start(bf16[128,512]{1,0:T(8,128)(2,1)} %get-tuple-element.64), channel_id=1, source_target_pairs={{0,8},{8,16},{16,24},{24,0},{32,40},{40,48},{48,56},{56,32},{64,72... | collective-permute-start | bytes 393224 | tf_op jit(solution)/shard_map/ppermute | solution.py:631
  144.9 8.5 %copy-start.16 = (bf16[128,512]{1,0:T(8,128)(2,1)}, bf16[128,512]{1,0:T(8,128)(2,1)S(1)}, u32[]{:S(2)}) copy-start(bf16[128,512]{1,0:T(8,128)(2,1)S(1)} %collective-permute-done.23.refs_1_) | copy-start | bytes 393220
  144.9 7.3 %collective-permute-start.27 = (bf16[128,512]{1,0:T(8,128)(2,1)}, bf16[128,512]{1,0:T(8,128)(2,1)S(1)}, u32[]{:S(2)}, u32[]{:S(2)}) collective-permute-start(bf16[128,512]{1,0:T(8,128)(2,1)} %get-tuple-element.65), channel_id=1, source_target_pairs={{0,16},{8,24},{16,0},{24,8},{32,48},{40,56},{48,32},{56,40},{64,80... | collective-permute-start | bytes 393224 | tf_op jit(solution)/shard_map/ppermute | solution.py:631
  147.3 6.0 %copy-start.17 = (bf16[128,512]{1,0:T(8,128)(2,1)}, bf16[128,512]{1,0:T(8,128)(2,1)S(1)}, u32[]{:S(2)}) copy-start(bf16[128,512]{1,0:T(8,128)(2,1)S(1)} %collective-permute-done.24.refs_2_) | copy-start | bytes 393220
  147.3 6.0 %collective-permute-start.28 = (bf16[128,512]{1,0:T(8,128)(2,1)}, bf16[128,512]{1,0:T(8,128)(2,1)S(1)}, u32[]{:S(2)}, u32[]{:S(2)}) collective-permute-start(bf16[128,512]{1,0:T(8,128)(2,1)} %get-tuple-element.66), channel_id=1, source_target_pairs={{0,24},{8,0},{16,8},{24,16},{32,56},{40,32},{48,40},{56,48},{64,88... | collective-permute-start | bytes 393224 | tf_op jit(solution)/shard_map/ppermute | solution.py:631
  149.7 3.7 %copy-start.18 = (bf16[128,512]{1,0:T(8,128)(2,1)}, bf16[128,512]{1,0:T(8,128)(2,1)S(1)}, u32[]{:S(2)}) copy-start(bf16[128,512]{1,0:T(8,128)(2,1)S(1)} %collective-permute-done.25.refs_3_) | copy-start | bytes 393220
  149.7 3.7 %copy-start.19 = (bf16[128,512]{1,0:T(8,128)(2,1)}, bf16[128,512]{1,0:T(8,128)(2,1)S(1)}, u32[]{:S(2)}) copy-start(bf16[128,512]{1,0:T(8,128)(2,1)S(1)} %collective-permute-done.26.refs_5_) | copy-start | bytes 393220
  152.2 1.2 copy-start.20
  156.1 19.4 %collective-permute-start.31 = (bf16[128,1024]{1,0:T(8,128)(2,1)}, bf16[128,1024]{1,0:T(8,128)(2,1)S(1)}, u32[]{:S(2)}, u32[]{:S(2)}) collective-permute-start(bf16[128,1024]{1,0:T(8,128)(2,1)} %summed_side_by_side.1.a_ref), channel_id=1, source_target_pairs={{0,6},{1,7},{2,4},{3,5},{4,2},{5,3},{6,0},{7,1},{8,14},{9,15},{10,... | collective-permute-start | bytes 786440 | tf_op jit(solution)/shard_map/ppermute | solution.py:634
  161.5 14.1 %collective-permute-start.30 = (bf16[128,1024]{1,0:T(8,128)(2,1)}, bf16[128,1024]{1,0:T(8,128)(2,1)S(1)}, u32[]{:S(2)}, u32[]{:S(2)}) collective-permute-start(bf16[128,1024]{1,0:T(8,128)(2,1)} %summed_side_by_side.1.a_ref), channel_id=1, source_target_pairs={{0,4},{1,5},{2,6},{3,7},{4,0},{5,1},{6,2},{7,3},{8,12},{9,13},{10,... | collective-permute-start | bytes 786440 | tf_op jit(solution)/shard_map/ppermute | solution.py:634
  161.8 13.7 %collective-permute-start.29 = (bf16[128,1024]{1,0:T(8,128)(2,1)}, bf16[128,1024]{1,0:T(8,128)(2,1)S(1)}, u32[]{:S(2)}, u32[]{:S(2)}) collective-permute-start(bf16[128,1024]{1,0:T(8,128)(2,1)} %summed_side_by_side.1.a_ref), channel_id=1, source_target_pairs={{0,2},{1,3},{2,0},{3,1},{4,6},{5,7},{6,4},{7,5},{8,10},{9,11},{10,... | collective-permute-start | bytes 786440 | tf_op jit(solution)/shard_map/ppermute | solution.py:634
  175.6 0.7 copy-start.13
  175.6 0.8 copy-start.14
  175.6 0.9 copy-start.15
  178.5 1.9 %collective-permute-start.32 = (bf16[128,1024]{1,0:T(8,128)(2,1)}, bf16[128,1024]{1,0:T(8,128)(2,1)S(1)}, u32[]{:S(2)}, u32[]{:S(2)}) collective-permute-start(bf16[128,1024]{1,0:T(8,128)(2,1)} %summed_over_chips.1.own_ref), channel_id=1, source_target_pairs={{0,1},{1,0},{2,3},{3,2},{4,5},{5,4},{6,7},{7,6},{8,9},{9,8},{10,11... | collective-permute-start | bytes 786440 | tf_op jit(solution)/shard_map/ppermute | solution.py:636
  180.3 0.7 copy-start.12
  (3 other events, 2.0 us)

commit v4 on v3

--- a/solution.py
+++ b/solution.py
@@ -19,7 +19,7 @@
 ANY = pl.BlockSpec(memory_space=pl.ANY)
 HBM = pl.BlockSpec(memory_space=pltpu.HBM)
 TILE = 128
-UNITS_AT_ONCE = 4
+UNITS_AT_ONCE = 8
 VMEM_LIMIT = 60 * MIB
 
 
@@ -222,8 +222,8 @@
                 rows_of(a_ref, half, unit)[...] = a_t.T.astype(BF16)
                 lse_ref[half * units + unit] = jnp.broadcast_to(top[half] + jnp.log2(total), (8, TILE))
 
-    chips = len(block_refs)
-    for k, ref in enumerate(block_refs):
+    chips = len(block_refs) + 1
+    for k, ref in enumerate(block_refs, 1):
         ref[...] = a_ref[lax.rem(place_ref[5] + k, chips)]
 
 
@@ -238,15 +238,15 @@
             jax.ShapeDtypeStruct((chips, halves, rows, head_dim), BF16),
             jax.ShapeDtypeStruct((halves * units, 8, TILE), F32),
         )
-        + (jax.ShapeDtypeStruct((halves, rows, head_dim), BF16),) * chips,
+        + (jax.ShapeDtypeStruct((halves, rows, head_dim), BF16),) * (chips - 1),
         in_specs=[SMEM] * 3 + [VMEM],
-        out_specs=(VMEM,) * (2 + chips),
+        out_specs=(VMEM,) * (1 + chips),
         scratch_shapes=[
             pltpu.VMEM((halves * units, head_dim, TILE), BF16),
             pltpu.VMEM((UNITS_AT_ONCE * slots, TILE, TILE), F32),
             pltpu.VMEM((UNITS_AT_ONCE, slots * TILE, 2 * TILE), BF16),
         ],
-        compiler_params=pltpu.CompilerParams(vmem_limit_bytes=20 * MIB),
+        compiler_params=pltpu.CompilerParams(vmem_limit_bytes=28 * MIB),
         cost_estimate=cost(3*10**11, MIB),
         name="attention_forward",
     )(place, tiles, counts, qkv)
@@ -384,12 +384,14 @@
 
 def row_copies(place_ref, block_refs, rows_ref, sems):
     chips = len(block_refs)
-    halves, rows, width = block_refs[0].shape
+    halves, rows, width = block_refs[-1].shape
     tokens = rows // 2
     core = place_ref[2]
     copies = []
     for k, ref in enumerate(block_refs):
         chip = lax.rem(place_ref[5] + chips - k, chips)
+        if k == 0:
+            ref = ref.at[chip]
         for half in range(halves):
             target = pl.ds(pl.multiple_of((chip * halves + half) * width, width), width)
             for slot, first in ((core, 0), (1 - core, tokens)):
@@ -422,7 +424,7 @@
 def project(place, blocks, weights, after, side):
     features = side * side * weights[0].shape[1]
     columns = 2 * weights[0].shape[2]
-    tokens = blocks[0].shape[1] // 2
+    tokens = blocks[-1].shape[1] // 2
     return pl.pallas_call(
         functools.partial(project_kernel, side),
         out_shape=(jax.ShapeDtypeStruct((tokens, features), F32), jax.ShapeDtypeStruct((tokens, features), BF16)),
@@ -466,7 +468,7 @@
 def grad_weight_parts(place, own, other, blocks, side):
     tokens, features = own.shape
     chips = len(blocks)
-    columns = chips * blocks[0].shape[0] * blocks[0].shape[2]
+    columns = chips * blocks[-1].shape[0] * blocks[-1].shape[2]
     rows = features // side**2
     return pl.pallas_call(
         functools.partial(grad_weight_kernel, side, chips),
@@ -614,8 +616,8 @@
     own_rows = grad_output[0]
     other_rows = lax.ppermute(own_rows, "seq", across)
     a, lse, *a_blocks = attention_forward(place, lists, counts, qkv, chips, width)
-    a_home = [a_blocks[0]] + [lax.ppermute(a_blocks[k], "seq", x_shift(k)) for k in range(1, chips)]
-    g = over_chips(gate(grad_attn(place, own_rows, other_rows, weights, lse, side, chips), *a_home))
+    a_home = [a] + [lax.ppermute(a_blocks[k - 1], "seq", x_shift(k)) for k in range(1, chips)]
+    g = over_chips(gate(grad_attn(place, own_rows, other_rows, weights, lse, side, chips), *a_home[1:]))
     parts = grad_weight_parts(place, own_rows, other_rows, a_home, side)
     z_first = [parts[0]] + [lax.ppermute(parts[k], "dp", z_shift(k)) for k in range(1, side)]
     y_first = [parts[side]] + [lax.ppermute(parts[side + k], "dp", y_shift(k)) for k in (1, side - 1)]

time: 184 us -> 182 us (0.989)
  starting transfers between devices: 71 us -> 68.4 us
  waiting for transfers between devices: 33.2 us -> 35.5 us
    ppermute x2, starting transfers between devices: 6.37 us -> 4.19 us  [per_device(): lax.ppermute(parts[side + k], 'dp', y_shift(k))]
    unnamed x63 -> x61, local copies, waits for them, and re-layouts: 8.67 us -> 8.5 us
  transfers between devices with their start and end apart: 36 -> 36, of which waited for: 13 -> 14; matrix products, arithmetic and copies ran while one was open for 2% -> 2% of each run, Pallas kernels for 32% -> 31%
where the time goes in v4:
time: 182 us; the launch traced here: 181 us
  starting transfers between devices  68.4 us (38%)
  Pallas kernels  64.6 us (35%)
  waiting for transfers between devices  35.5 us (20%)
  local copies, waits for them, and re-layouts  9.39 us (5%)
  other arithmetic  2.48 us (1%)
    pallas_call x1, Pallas kernels, attention_backward(): pl.pallas_call(functools.partial(backward_kernel, UNITS_AT_ONCE, slots, u...  15.4 us
    unnamed x61, local copies, waits for them, and re-layouts  8.5 us
    all_to_all x1, starting transfers between devices, per_device(): lax.all_to_all(grads, 'seq', split_axis=0, concat_axis=0, tiled=True)  8.17 us
    pallas_call x1, Pallas kernels, project(): pl.pallas_call(functools.partial(project_kernel, side), out_shape=(jax.Sh...  7.85 us
    ppermute x3, waiting for transfers between devices, per_device(): lax.ppermute(lines_z, 'dp', y_shift(k))  7.36 us
    ppermute x3, waiting for transfers between devices, per_device(): lax.ppermute(lines_y, 'dp', z_shift(k))  7.05 us
    pallas_call x1, Pallas kernels, attention_forward(): pl.pallas_call(functools.partial(forward_kernel, UNITS_AT_ONCE, slots, un...  7.04 us
    ppermute x3, starting transfers between devices, per_device(): lax.ppermute(lines_y, 'dp', z_shift(k))  6.47 us
  transfers between devices with their start and end apart: 36, of which 14 were waited for; matrix products, arithmetic and copies ran while one was open for 2% of the time, Pallas kernels for 31%

profile of v4, /device:TPU:1, one launch (start us, length us, event | category | flops | bytes accessed | tf_op | source)
XLA Modules:
  0.0 181.3 jit_solution(6878334181802903709)
XLA Ops:
  0.6 3.3 %pack_heads.1 = bf16[8,3,2,256,128]{4,3,2,1,0:T(8,128)(2,1)} custom-call(bf16[1,256,2048]{2,1,0:T(8,128)(2,1)} %q_ref.1, bf16[1,256,2048]{2,1,0:T(8,128)(2,1)} %k_ref.1, bf16[1,256,2048]{2,1,0:T(8,128)(2,1)} %v_ref.1), custom_call_target="tpu_custom_call" | custom-call | bytes 6291456 | tf_op jit(solution)/shard_map/pack_heads/pallas_call | solution.py:54
  4.0 5.9 %all-to-all-start = ((bf16[8,3,2,256,128]{4,3,2,1,0:T(8,128)(2,1)}), bf16[8,3,2,256,128]{4,3,2,1,0:T(8,128)(2,1)S(1)}, u32[]{:S(2)}, u32[]{:S(2)}) async-start(bf16[8,3,2,256,128]{4,3,2,1,0:T(8,128)(2,1)} %pack_heads.1), calls=%async_computation | async-start | bytes 6291456 | tf_op jit(solution)/shard_map/all_to_all | solution.py:615
  10.0 0.6 stack.23.place_ref
  10.6 1.8 %pack_weight.1 = (bf16[128,512]{1,0:T(8,128)(2,1)}, bf16[128,512]{1,0:T(8,128)(2,1)}) custom-call(s32[6]{0:T(128)} %stack.23.place_ref, bf16[128,2048]{1,0:T(8,128)(2,1)} %in_ref.1), custom_call_target="tpu_custom_call" | custom-call | bytes 786432 | tf_op jit(solution)/shard_map/pack_weight/pallas_call | solution.py:106
  12.4 3.8 %collective-permute-start.5 = (bf16[128,512]{1,0:T(8,128)(2,1)}, bf16[128,512]{1,0:T(8,128)(2,1)S(1)}, u32[]{:S(2)}, u32[]{:S(2)}) collective-permute-start(bf16[128,512]{1,0:T(8,128)(2,1)} %get-tuple-element.39.refs_0_), channel_id=1, source_target_pairs={{0,24},{8,0},{16,8},{24,16},{32,56},{40,32},{48,40},{56,48},{64,88... | collective-permute-start | bytes 393224 | tf_op jit(solution)/shard_map/ppermute | solution.py:609
  16.1 0.7 collective-permute-start.3
  16.8 2.7 %collective-permute-start.8 = (bf16[128,512]{1,0:T(8,128)(2,1)}, bf16[128,512]{1,0:T(8,128)(2,1)S(1)}, u32[]{:S(2)}, u32[]{:S(2)}) collective-permute-start(bf16[128,512]{1,0:T(8,128)(2,1)} %get-tuple-element.40.refs_4_), channel_id=1, source_target_pairs={{0,96},{8,104},{16,112},{24,120},{32,0},{40,8},{48,16},{56,24},{64... | collective-permute-start | bytes 393224 | tf_op jit(solution)/shard_map/ppermute | solution.py:610
  19.9 2.3 %collective-permute-done.5.refs_3_ = bf16[128,512]{1,0:T(8,128)(2,1)S(1)} collective-permute-done((bf16[128,512]{1,0:T(8,128)(2,1)}, bf16[128,512]{1,0:T(8,128)(2,1)S(1)}, u32[]{:S(2)}, u32[]{:S(2)}) %collective-permute-start.5) | collective-permute-done | bytes 131104 | tf_op jit(solution)/shard_map/ppermute | solution.py:609
  22.2 1.3 collective-permute-start.6
  23.5 2.0 %collective-permute-done.3.refs_1_ = bf16[128,512]{1,0:T(8,128)(2,1)S(1)} collective-permute-done((bf16[128,512]{1,0:T(8,128)(2,1)}, bf16[128,512]{1,0:T(8,128)(2,1)S(1)}, u32[]{:S(2)}, u32[]{:S(2)}) %collective-permute-start.3) | collective-permute-done | bytes 131104 | tf_op jit(solution)/shard_map/ppermute | solution.py:609
  25.6 3.6 %collective-permute-done.6.refs_5_ = bf16[128,512]{1,0:T(8,128)(2,1)S(1)} collective-permute-done((bf16[128,512]{1,0:T(8,128)(2,1)}, bf16[128,512]{1,0:T(8,128)(2,1)S(1)}, u32[]{:S(2)}, u32[]{:S(2)}) %collective-permute-start.6) | collective-permute-done | bytes 131104 | tf_op jit(solution)/shard_map/ppermute | solution.py:610
  29.2 0.6 copy-done.26
  29.9 2.3 %stack_lines.1 = (bf16[4,128,512]{2,1,0:T(8,128)(2,1)}, bf16[4,128,512]{2,1,0:T(8,128)(2,1)}) custom-call(bf16[128,512]{1,0:T(8,128)(2,1)} %get-tuple-element.39.refs_0_, bf16[128,512]{1,0:T(8,128)(2,1)} %copy-done.23, bf16[128,512]{1,0:T(8,128)(2,1)} %copy-done.22, bf16[128,512]{1,0:T(8,128)(2,1)} %copy-done.21, ...), custom_call_target="tpu_custom_call" | custom-call | bytes 2097152 | tf_op jit(solution)/shard_map/stack_lines/pallas_call | solution.py:126
  32.7 2.2 %collective-permute-start.15 = (bf16[256,2048]{1,0:T(8,128)(2,1)}, bf16[256,2048]{1,0:T(8,128)(2,1)}, u32[]{:S(2)}, u32[]{:S(2)}) collective-permute-start(bf16[256,2048]{1,0:T(8,128)(2,1)} %bitcast.10), channel_id=1, source_target_pairs={{0,1},{1,0},{2,3},{3,2},{4,5},{5,4},{6,7},{7,6},{8,9},{9,8},{10,11... | collective-permute-start | bytes 3145736 | tf_op jit(solution)/shard_map/ppermute | solution.py:617
  35.4 0.8 collective-permute-start.9
  36.2 3.3 %collective-permute-start.14 = (bf16[4,128,512]{2,1,0:T(8,128)(2,1)}, bf16[4,128,512]{2,1,0:T(8,128)(2,1)}, u32[]{:S(2)}, u32[]{:S(2)}) collective-permute-start(bf16[4,128,512]{2,1,0:T(8,128)(2,1)} %get-tuple-element.42.refs_4_.refs_8_), channel_id=1, source_target_pairs={{0,24},{8,0},{16,8},{24,16},{32,56},{40,32},{48,40},{56,48},{64,88... | collective-permute-start | bytes 1572872 | tf_op jit(solution)/shard_map/ppermute | solution.py:613
  39.5 5.4 %collective-permute-done.11.refs_3_.refs_7_ = bf16[4,128,512]{2,1,0:T(8,128)(2,1)} collective-permute-done((bf16[4,128,512]{2,1,0:T(8,128)(2,1)}, bf16[4,128,512]{2,1,0:T(8,128)(2,1)}, u32[]{:S(2)}, u32[]{:S(2)}) %collective-permute-start.11) | collective-permute-done | bytes 524320 | tf_op jit(solution)/shard_map/ppermute | solution.py:612
  44.9 3.2 %collective-permute-start.13 = (bf16[4,128,512]{2,1,0:T(8,128)(2,1)}, bf16[4,128,512]{2,1,0:T(8,128)(2,1)}, u32[]{:S(2)}, u32[]{:S(2)}) collective-permute-start(bf16[4,128,512]{2,1,0:T(8,128)(2,1)} %get-tuple-element.42.refs_4_.refs_8_), channel_id=1, source_target_pairs={{0,16},{8,24},{16,0},{24,8},{32,48},{40,56},{48,32},{56,40},{64,80... | collective-permute-start | bytes 1572872 | tf_op jit(solution)/shard_map/ppermute | solution.py:613
  48.1 0.6 copy-done.2
  48.7 7.0 %attention_forward.1 = (bf16[4,2,512,128]{3,2,1,0:T(8,128)(2,1)S(1)}, f32[32,8,128]{2,1,0:T(8,128)S(1)}, bf16[2,512,128]{2,1,0:T(8,128)(2,1)S(1)}, bf16[2,512,12...) custom-call(s32[6]{0:T(128)S(1)} %copy-done.2, s32[1792]{0:T(1024)S(1)} %reshape.16.tiles_ref, s32[256]{0:T(256)S(1)} %reshape.17.counts_ref, ...), custom_call_target="tpu_custom_call" | custom-call | flops 299999985664 | bytes 1048576 | tf_op jit(solution)/shard_map/attention_forward/pallas_call | solution.py:235
  55.8 1.0 copy-done.1
  56.7 0.6 copy-done.5
  57.4 1.9 %collective-permute-done.9.refs_1_.refs_5_ = bf16[4,128,512]{2,1,0:T(8,128)(2,1)} collective-permute-done((bf16[4,128,512]{2,1,0:T(8,128)(2,1)}, bf16[4,128,512]{2,1,0:T(8,128)(2,1)}, u32[]{:S(2)}, u32[]{:S(2)}) %collective-permute-start.9) | collective-permute-done | bytes 524320 | tf_op jit(solution)/shard_map/ppermute | solution.py:612
  59.3 1.9 %collective-permute-start = (bf16[2,512,128]{2,1,0:T(8,128)(2,1)S(1)}, bf16[2,512,128]{2,1,0:T(8,128)(2,1)S(1)}, u32[]{:S(2)}, u32[]{:S(2)}) collective-permute-start(bf16[2,512,128]{2,1,0:T(8,128)(2,1)S(1)} %get-tuple-element.36), channel_id=1, source_target_pairs={{0,2},{1,3},{2,4},{3,5},{4,6},{5,7},{6,0},{7,1},{8,10},{9,11},{10,... | collective-permute-start | bytes 786440 | tf_op jit(solution)/shard_map/ppermute | solution.py:619
  61.3 0.7 collective-permute-done.14.refs_7_.refs_11_
  61.9 2.8 %collective-permute-start.1 = (bf16[2,512,128]{2,1,0:T(8,128)(2,1)S(1)}, bf16[2,512,128]{2,1,0:T(8,128)(2,1)S(1)}, u32[]{:S(2)}, u32[]{:S(2)}) collective-permute-start(bf16[2,512,128]{2,1,0:T(8,128)(2,1)S(1)} %get-tuple-element.37), channel_id=1, source_target_pairs={{0,4},{1,5},{2,6},{3,7},{4,0},{5,1},{6,2},{7,3},{8,12},{9,13},{10,... | collective-permute-start | bytes 786440 | tf_op jit(solution)/shard_map/ppermute | solution.py:619
  64.7 0.9 collective-permute-start.2
  65.6 6.4 %collective-permute-done.12.refs_5_.refs_9_ = bf16[4,128,512]{2,1,0:T(8,128)(2,1)} collective-permute-done((bf16[4,128,512]{2,1,0:T(8,128)(2,1)}, bf16[4,128,512]{2,1,0:T(8,128)(2,1)}, u32[]{:S(2)}, u32[]{:S(2)}) %collective-permute-start.12) | collective-permute-done | bytes 524320 | tf_op jit(solution)/shard_map/ppermute | solution.py:613
  72.0 6.2 %grad_attn.1.refs_0_ = bf16[4,2,512,128]{3,2,1,0:T(8,128)(2,1)} custom-call(s32[6]{0:T(128)} %stack.23.place_ref, bf16[256,2048]{1,0:T(8,128)(2,1)} %bitcast.11, bf16[256,2048]{1,0:T(8,128)(2,1)} %collective-permute-done.15.other_ref, bf16[4,128,512]{2,1,0:T(8,128)(2,1)} %get-tuple-element.41.refs_0_.refs_4_, ...), custom_call_target="tpu_custom_call" | custom-call | flops 2147483648 | bytes 7340032 | tf_op jit(solution)/shard_map/grad_attn/pallas_call | solution.py:374
  78.2 0.7 copy-done.8
  79.0 0.7 copy-done.10
  79.7 5.1 %all-to-all-start.1 = ((bf16[4,2,512,128]{3,2,1,0:T(8,128)(2,1)}), bf16[4,2,512,128]{3,2,1,0:T(8,128)(2,1)S(1)}, u32[]{:S(2)}, u32[]{:S(2)}) async-start(bf16[4,2,512,128]{3,2,1,0:T(8,128)(2,1)} %gate.2), calls=%async_computation.1 | async-start | bytes 2097152 | tf_op jit(solution)/shard_map/all_to_all | solution.py:605
  84.8 6.4 %grad_weight_parts.1 = (bf16[4,128,512]{2,1,0:T(8,128)(2,1)}, bf16[4,128,512]{2,1,0:T(8,128)(2,1)}, bf16[4,128,512]{2,1,0:T(8,128)(2,1)}, bf16[4,128,512]{2,1,0:...) custom-call(s32[6]{0:T(128)} %stack.23.place_ref, ...), custom_call_target="tpu_custom_call" | custom-call | flops 2147483648 | bytes 7340032 | tf_op jit(solution)/shard_map/grad_weight_parts/pallas_call | solution.py:473
  91.4 1.7 collective-permute-start.18
  93.0 1.5 collective-permute-start.19
  94.5 1.5 collective-permute-start.20
  96.1 2.7 %collective-permute-start.21 = (bf16[4,128,512]{2,1,0:T(8,128)(2,1)}, bf16[4,128,512]{2,1,0:T(8,128)(2,1)}, u32[]{:S(2)}, u32[]{:S(2)}) collective-permute-start(bf16[4,128,512]{2,1,0:T(8,128)(2,1)} %get-tuple-element.55), channel_id=1, source_target_pairs={{0,96},{8,104},{16,112},{24,120},{32,0},{40,8},{48,16},{56,24},{64... | collective-permute-start | bytes 1572872 | tf_op jit(solution)/shard_map/ppermute | solution.py:623
  99.2 1.0 copy-done.7
  100.2 15.4 %attention_backward.1.refs_12_.refs_1_ = bf16[8,3,2,256,128]{4,3,2,1,0:T(8,128)(2,1)} custom-call(s32[6]{0:T(128)} %stack.23.place_ref, s32[1792]{0:T(1024)} %copy-done.3, s32[256]{0:T(256)} %copy-done.4, bf16[8,3,2,256,128]{4,3,2,1,0:T(8,128)(2,1)} %copy-done, bf16[4,2,512,128]{3,2,1,0:T(8,128)(2,1)} %copy-done.7, bf16[4,2,512,128]{3,2,1,0:T(8,128)(2,1)} %copy-done.1, ...), custom_call_target="tpu_custom_call" | custom-call | flops 299999985664 | bytes 1048576 | tf_op jit(solution)/shard_map/attention_backward/pallas_call | solution.py:321
  115.6 0.8 collective-permute-start.22
  116.3 8.2 %all-to-all-start.2 = ((bf16[8,3,2,256,128]{4,3,2,1,0:T(8,128)(2,1)}), bf16[8,3,2,256,128]{4,3,2,1,0:T(8,128)(2,1)}, u32[]{:S(2)}, u32[]{:S(2)}) async-start(bf16[8,3,2,256,128]{4,3,2,1,0:T(8,128)(2,1)} %attention_backward.1.refs_12_.refs_1_), calls=%async_computation.2 | async-start | bytes 6291456 | tf_op jit(solution)/shard_map/all_to_all | solution.py:625
  124.5 7.8 %project.1 = (f32[256,2048]{1,0:T(8,128)}, bf16[256,2048]{1,0:T(8,128)(2,1)}) custom-call(s32[6]{0:T(128)} %stack.23.place_ref, bf16[4,2,512,128]{3,2,1,0:T(8,128)(2,1)} %copy-done.1, bf16[2,512,128]{2,1,0:T(8,128)(2,1)} %copy-done.8, bf16[2,512,128]{2,1,0:T(8,128)(2,1)} %copy-done.9, bf16[2,512,128]{2,1,0:T(8,128)(2,1)} %copy-done.10, ...), custom_call_target="tpu_custom_call" | custom-call | flops 2147483648 | bytes 8388608 | tf_op jit(solution)/shard_map/project/pallas_call | solution.py:428
  132.5 0.8 copy-done.29
  133.3 3.4 %summed.1 = (bf16[128,512]{1,0:T(8,128)(2,1)}, bf16[128,512]{1,0:T(8,128)(2,1)}, bf16[128,512]{1,0:T(8,128)(2,1)}, bf16[128,512]{1,0:T(8,128)(2,1)}, bf16[128,51...) custom-call(bf16[4,128,512]{2,1,0:T(8,128)(2,1)} %get-tuple-element.44.refs_0_, ...), custom_call_target="tpu_custom_call" | custom-call | flops 999999995904 | bytes 1048576 | tf_op jit(solution)/shard_map/summed/pallas_call | solution.py:520
  136.7 1.3 collective-permute-start.23
  138.0 1.7 collective-permute-start.24
  139.7 1.1 collective-permute-start.25
  140.7 1.8 collective-permute-start.26
  143.0 2.0 %collective-permute-start.27 = (bf16[128,512]{1,0:T(8,128)(2,1)}, bf16[128,512]{1,0:T(8,128)(2,1)S(1)}, u32[]{:S(2)}, u32[]{:S(2)}) collective-permute-start(bf16[128,512]{1,0:T(8,128)(2,1)} %get-tuple-element.63), channel_id=1, source_target_pairs={{0,16},{8,24},{16,0},{24,8},{32,48},{40,56},{48,32},{56,40},{64,80... | collective-permute-start | bytes 393224 | tf_op jit(solution)/shard_map/ppermute | solution.py:633
  145.0 0.8 collective-permute-done.24.refs_2_
  145.8 1.9 %collective-permute-start.28 = (bf16[128,512]{1,0:T(8,128)(2,1)}, bf16[128,512]{1,0:T(8,128)(2,1)S(1)}, u32[]{:S(2)}, u32[]{:S(2)}) collective-permute-start(bf16[128,512]{1,0:T(8,128)(2,1)} %get-tuple-element.64), channel_id=1, source_target_pairs={{0,24},{8,0},{16,8},{24,16},{32,56},{40,32},{48,40},{56,48},{64,88... | collective-permute-start | bytes 393224 | tf_op jit(solution)/shard_map/ppermute | solution.py:633
  147.7 2.5 %collective-permute-done.27.refs_6_ = bf16[128,512]{1,0:T(8,128)(2,1)S(1)} collective-permute-done((bf16[128,512]{1,0:T(8,128)(2,1)}, bf16[128,512]{1,0:T(8,128)(2,1)S(1)}, u32[]{:S(2)}, u32[]{:S(2)}) %collective-permute-start.27) | collective-permute-done | bytes 131104 | tf_op jit(solution)/shard_map/ppermute | solution.py:633
  150.2 1.2 collective-permute-done.28.refs_7_
  151.4 0.6 copy-done.20
  152.0 2.1 %summed_side_by_side.1.a_ref = bf16[128,1024]{1,0:T(8,128)(2,1)} custom-call(bf16[128,512]{1,0:T(8,128)(2,1)} %get-tuple-element.57.refs_0_, bf16[128,512]{1,0:T(8,128)(2,1)} %copy-done.15, bf16[128,512]{1,0:T(8,128)(2,1)} %copy-done.16, bf16[128,512]{1,0:T(8,128)(2,1)} %copy-done.17, bf16[128,512]{1,0:T(8,128)(2,1)} %get-tuple-element.61.refs_4_, ...), custom_call_target="tpu_custom_call" | custom-call | bytes 1310720 | tf_op jit(solution)/shard_map/summed_side_by_side/pallas_call | solution.py:545
  154.2 5.6 %collective-permute-start.31 = (bf16[128,1024]{1,0:T(8,128)(2,1)}, bf16[128,1024]{1,0:T(8,128)(2,1)S(1)}, u32[]{:S(2)}, u32[]{:S(2)}) collective-permute-start(bf16[128,1024]{1,0:T(8,128)(2,1)} %summed_side_by_side.1.a_ref), channel_id=1, source_target_pairs={{0,6},{1,7},{2,4},{3,5},{4,2},{5,3},{6,0},{7,1},{8,14},{9,15},{10,... | collective-permute-start | bytes 786440 | tf_op jit(solution)/shard_map/ppermute | solution.py:636
  160.3 2.5 %add_convert_fusion.refs_1_ = bf16[256,2048]{1,0:T(8,128)(2,1)} fusion(f32[256,2048]{1,0:T(8,128)S(1)} %copy-done.6, bf16[256,2048]{1,0:T(8,128)(2,1)} %collective-permute-done.16), kind=kLoop, calls=%fused_computation | loop fusion | flops 1572864 | bytes 4194304 | tf_op jit(solution)/shard_map/convert_element_type | solution.py:630
  162.8 4.5 %unpack_heads.1 = (bf16[1,256,2048]{2,1,0:T(8,128)(2,1)}, bf16[1,256,2048]{2,1,0:T(8,128)(2,1)}, bf16[1,256,2048]{2,1,0:T(8,128)(2,1)}) custom-call(bf16[8,3,2,256,128]{4,3,2,1,0:T(8,128)(2,1)} %all-to-all-done.2.in_ref), custom_call_target="tpu_custom_call" | custom-call | bytes 6291456 | tf_op jit(solution)/shard_map/unpack_heads/pallas_call | solution.py:83
  167.3 6.3 %collective-permute-done.31.d_ref = bf16[128,1024]{1,0:T(8,128)(2,1)S(1)} collective-permute-done((bf16[128,1024]{1,0:T(8,128)(2,1)}, bf16[128,1024]{1,0:T(8,128)(2,1)S(1)}, u32[]{:S(2)}, u32[]{:S(2)}) %collective-permute-start.31) | collective-permute-done | bytes 262176 | tf_op jit(solution)/shard_map/ppermute | solution.py:636
  173.6 0.7 copy-done.12
  174.5 2.0 %summed_over_chips.1.own_ref = bf16[128,1024]{1,0:T(8,128)(2,1)} custom-call(bf16[128,1024]{1,0:T(8,128)(2,1)} %summed_side_by_side.1.a_ref, bf16[128,1024]{1,0:T(8,128)(2,1)} %copy-done.14, bf16[128,1024]{1,0:T(8,128)(2,1)} %copy-done.13, bf16[128,1024]{1,0:T(8,128)(2,1)} %copy-done.12, bf16[1,256,2048]{2,1,0:T(8,128)(2,1)} %get-tuple-element.31.refs_0_, ...), custom_call_target="tpu_custom_call" | custom-call | bytes 1310720 | tf_op jit(solution)/shard_map/summed_over_chips/pallas_call | solution.py:563
  177.1 1.4 collective-permute-done.32.other_ref
  178.5 0.7 copy-done.11
  179.1 2.1 %unpack_weight.1 = f32[128,2048]{1,0:T(8,128)} custom-call(s32[6]{0:T(128)} %stack.23.place_ref, bf16[128,1024]{1,0:T(8,128)(2,1)} %summed_over_chips.1.own_ref, bf16[128,1024]{1,0:T(8,128)(2,1)} %copy-done.11), custom_call_target="tpu_custom_call" | custom-call | bytes 1572864 | tf_op jit(solution)/shard_map/unpack_weight/pallas_call | solution.py:145
  (88 shorter events, 4.1 us)
Async XLA Ops:
  4.0 31.0 %copy-start.28 = (s32[1,16,16]{2,1,0:T(8,128)S(1)}, s32[1,16,16]{2,1,0:T(8,128)}, u32[]{:S(2)}) copy-start(s32[1,16,16]{2,1,0:T(8,128)} %param.13) | copy-start | bytes 3076
  4.0 31.0 %copy-start.27 = (s32[1,16,16,7]{2,1,3,0:T(8,128)S(1)}, s32[1,16,16,7]{2,1,3,0:T(8,128)}, u32[]{:S(2)}) copy-start(s32[1,16,16,7]{2,1,3,0:T(8,128)} %param.12) | copy-start | bytes 21508
  4.0 44.1 %all-to-all-start = ((bf16[8,3,2,256,128]{4,3,2,1,0:T(8,128)(2,1)}), bf16[8,3,2,256,128]{4,3,2,1,0:T(8,128)(2,1)S(1)}, u32[]{:S(2)}, u32[]{:S(2)}) async-start(bf16[8,3,2,256,128]{4,3,2,1,0:T(8,128)(2,1)} %pack_heads.1), calls=%async_computation | async-start | bytes 6291456 | tf_op jit(solution)/shard_map/all_to_all | solution.py:615
  12.4 9.8 %collective-permute-start.5 = (bf16[128,512]{1,0:T(8,128)(2,1)}, bf16[128,512]{1,0:T(8,128)(2,1)S(1)}, u32[]{:S(2)}, u32[]{:S(2)}) collective-permute-start(bf16[128,512]{1,0:T(8,128)(2,1)} %get-tuple-element.39.refs_0_), channel_id=1, source_target_pairs={{0,24},{8,0},{16,8},{24,16},{32,56},{40,32},{48,40},{56,48},{64,88... | collective-permute-start | bytes 393224 | tf_op jit(solution)/shard_map/ppermute | solution.py:609
  16.1 7.4 %collective-permute-start.4 = (bf16[128,512]{1,0:T(8,128)(2,1)}, bf16[128,512]{1,0:T(8,128)(2,1)S(1)}, u32[]{:S(2)}, u32[]{:S(2)}) collective-permute-start(bf16[128,512]{1,0:T(8,128)(2,1)} %get-tuple-element.39.refs_0_), channel_id=1, source_target_pairs={{0,16},{8,24},{16,0},{24,8},{32,48},{40,56},{48,32},{56,40},{64,80... | collective-permute-start | bytes 393224 | tf_op jit(solution)/shard_map/ppermute | solution.py:609
  16.1 9.4 %collective-permute-start.3 = (bf16[128,512]{1,0:T(8,128)(2,1)}, bf16[128,512]{1,0:T(8,128)(2,1)S(1)}, u32[]{:S(2)}, u32[]{:S(2)}) collective-permute-start(bf16[128,512]{1,0:T(8,128)(2,1)} %get-tuple-element.39.refs_0_), channel_id=1, source_target_pairs={{0,8},{8,16},{16,24},{24,0},{32,40},{40,48},{48,56},{56,32},{64,72... | collective-permute-start | bytes 393224 | tf_op jit(solution)/shard_map/ppermute | solution.py:609
  16.8 8.7 %collective-permute-start.8 = (bf16[128,512]{1,0:T(8,128)(2,1)}, bf16[128,512]{1,0:T(8,128)(2,1)S(1)}, u32[]{:S(2)}, u32[]{:S(2)}) collective-permute-start(bf16[128,512]{1,0:T(8,128)(2,1)} %get-tuple-element.40.refs_4_), channel_id=1, source_target_pairs={{0,96},{8,104},{16,112},{24,120},{32,0},{40,8},{48,16},{56,24},{64... | collective-permute-start | bytes 393224 | tf_op jit(solution)/shard_map/ppermute | solution.py:610
  19.6 6.0 %collective-permute-start.7 = (bf16[128,512]{1,0:T(8,128)(2,1)}, bf16[128,512]{1,0:T(8,128)(2,1)S(1)}, u32[]{:S(2)}, u32[]{:S(2)}) collective-permute-start(bf16[128,512]{1,0:T(8,128)(2,1)} %get-tuple-element.40.refs_4_), channel_id=1, source_target_pairs={{0,64},{8,72},{16,80},{24,88},{32,96},{40,104},{48,112},{56,120},{... | collective-permute-start | bytes 393224 | tf_op jit(solution)/shard_map/ppermute | solution.py:610
  22.2 7.0 %copy-start.21 = (bf16[128,512]{1,0:T(8,128)(2,1)}, bf16[128,512]{1,0:T(8,128)(2,1)S(1)}, u32[]{:S(2)}) copy-start(bf16[128,512]{1,0:T(8,128)(2,1)S(1)} %collective-permute-done.5.refs_3_) | copy-start | bytes 393220
  22.2 7.0 %collective-permute-start.6 = (bf16[128,512]{1,0:T(8,128)(2,1)}, bf16[128,512]{1,0:T(8,128)(2,1)S(1)}, u32[]{:S(2)}, u32[]{:S(2)}) collective-permute-start(bf16[128,512]{1,0:T(8,128)(2,1)} %get-tuple-element.40.refs_4_), channel_id=1, source_target_pairs={{0,32},{8,40},{16,48},{24,56},{32,64},{40,72},{48,80},{56,88},{64,... | collective-permute-start | bytes 393224 | tf_op jit(solution)/shard_map/ppermute | solution.py:610
  23.5 5.7 %copy-start.22 = (bf16[128,512]{1,0:T(8,128)(2,1)}, bf16[128,512]{1,0:T(8,128)(2,1)S(1)}, u32[]{:S(2)}) copy-start(bf16[128,512]{1,0:T(8,128)(2,1)S(1)} %collective-permute-done.4.refs_2_) | copy-start | bytes 393220
  25.5 3.7 %copy-start.23 = (bf16[128,512]{1,0:T(8,128)(2,1)}, bf16[128,512]{1,0:T(8,128)(2,1)S(1)}, u32[]{:S(2)}) copy-start(bf16[128,512]{1,0:T(8,128)(2,1)S(1)} %collective-permute-done.3.refs_1_) | copy-start | bytes 393220
  25.5 3.7 %copy-start.24 = (bf16[128,512]{1,0:T(8,128)(2,1)}, bf16[128,512]{1,0:T(8,128)(2,1)S(1)}, u32[]{:S(2)}) copy-start(bf16[128,512]{1,0:T(8,128)(2,1)S(1)} %collective-permute-done.8.refs_7_) | copy-start | bytes 393220
  25.6 3.7 %copy-start.25 = (bf16[128,512]{1,0:T(8,128)(2,1)}, bf16[128,512]{1,0:T(8,128)(2,1)S(1)}, u32[]{:S(2)}) copy-start(bf16[128,512]{1,0:T(8,128)(2,1)S(1)} %collective-permute-done.7.refs_6_) | copy-start | bytes 393220
  29.2 0.7 copy-start.26
  32.2 12.7 %collective-permute-start.11 = (bf16[4,128,512]{2,1,0:T(8,128)(2,1)}, bf16[4,128,512]{2,1,0:T(8,128)(2,1)}, u32[]{:S(2)}, u32[]{:S(2)}) collective-permute-start(bf16[4,128,512]{2,1,0:T(8,128)(2,1)} %get-tuple-element.41.refs_0_.refs_4_), channel_id=1, source_target_pairs={{0,96},{8,104},{16,112},{24,120},{32,0},{40,8},{48,16},{56,24},{64... | collective-permute-start | bytes 1572872 | tf_op jit(solution)/shard_map/ppermute | solution.py:612
  32.4 15.7 %collective-permute-start.10 = (bf16[4,128,512]{2,1,0:T(8,128)(2,1)}, bf16[4,128,512]{2,1,0:T(8,128)(2,1)}, u32[]{:S(2)}, u32[]{:S(2)}) collective-permute-start(bf16[4,128,512]{2,1,0:T(8,128)(2,1)} %get-tuple-element.41.refs_0_.refs_4_), channel_id=1, source_target_pairs={{0,64},{8,72},{16,80},{24,88},{32,96},{40,104},{48,112},{56,120},{... | collective-permute-start | bytes 1572872 | tf_op jit(solution)/shard_map/ppermute | solution.py:612
  32.7 39.3 %collective-permute-start.15 = (bf16[256,2048]{1,0:T(8,128)(2,1)}, bf16[256,2048]{1,0:T(8,128)(2,1)}, u32[]{:S(2)}, u32[]{:S(2)}) collective-permute-start(bf16[256,2048]{1,0:T(8,128)(2,1)} %bitcast.10), channel_id=1, source_target_pairs={{0,1},{1,0},{2,3},{3,2},{4,5},{5,4},{6,7},{7,6},{8,9},{9,8},{10,11... | collective-permute-start | bytes 3145736 | tf_op jit(solution)/shard_map/ppermute | solution.py:617
  35.0 20.7 %copy-start.4 = (s32[256]{0:T(256)}, s32[256]{0:T(256)S(1)}, u32[]{:S(2)}) copy-start(s32[256]{0:T(256)S(1)} %reshape.17.counts_ref) | copy-start | bytes 3076
  35.4 20.3 %copy-start.3 = (s32[1792]{0:T(1024)}, s32[1792]{0:T(1024)S(1)}, u32[]{:S(2)}) copy-start(s32[1792]{0:T(1024)S(1)} %reshape.16.tiles_ref) | copy-start | bytes 21508
  35.4 23.9 %collective-permute-start.9 = (bf16[4,128,512]{2,1,0:T(8,128)(2,1)}, bf16[4,128,512]{2,1,0:T(8,128)(2,1)}, u32[]{:S(2)}, u32[]{:S(2)}) collective-permute-start(bf16[4,128,512]{2,1,0:T(8,128)(2,1)} %get-tuple-element.41.refs_0_.refs_4_), channel_id=1, source_target_pairs={{0,32},{8,40},{16,48},{24,56},{32,64},{40,72},{48,80},{56,88},{64,... | collective-permute-start | bytes 1572872 | tf_op jit(solution)/shard_map/ppermute | solution.py:612
  36.2 25.8 %collective-permute-start.14 = (bf16[4,128,512]{2,1,0:T(8,128)(2,1)}, bf16[4,128,512]{2,1,0:T(8,128)(2,1)}, u32[]{:S(2)}, u32[]{:S(2)}) collective-permute-start(bf16[4,128,512]{2,1,0:T(8,128)(2,1)} %get-tuple-element.42.refs_4_.refs_8_), channel_id=1, source_target_pairs={{0,24},{8,0},{16,8},{24,16},{32,56},{40,32},{48,40},{56,48},{64,88... | collective-permute-start | bytes 1572872 | tf_op jit(solution)/shard_map/ppermute | solution.py:613
  44.9 19.8 %collective-permute-start.13 = (bf16[4,128,512]{2,1,0:T(8,128)(2,1)}, bf16[4,128,512]{2,1,0:T(8,128)(2,1)}, u32[]{:S(2)}, u32[]{:S(2)}) collective-permute-start(bf16[4,128,512]{2,1,0:T(8,128)(2,1)} %get-tuple-element.42.refs_4_.refs_8_), channel_id=1, source_target_pairs={{0,16},{8,24},{16,0},{24,8},{32,48},{40,56},{48,32},{56,40},{64,80... | collective-permute-start | bytes 1572872 | tf_op jit(solution)/shard_map/ppermute | solution.py:613
  48.1 23.9 %collective-permute-start.12 = (bf16[4,128,512]{2,1,0:T(8,128)(2,1)}, bf16[4,128,512]{2,1,0:T(8,128)(2,1)}, u32[]{:S(2)}, u32[]{:S(2)}) collective-permute-start(bf16[4,128,512]{2,1,0:T(8,128)(2,1)} %get-tuple-element.42.refs_4_.refs_8_), channel_id=1, source_target_pairs={{0,8},{8,16},{16,24},{24,0},{32,40},{40,48},{48,56},{56,32},{64,72... | collective-permute-start | bytes 1572872 | tf_op jit(solution)/shard_map/ppermute | solution.py:613
  48.7 7.1 %copy-start = (bf16[8,3,2,256,128]{4,3,2,1,0:T(8,128)(2,1)}, bf16[8,3,2,256,128]{4,3,2,1,0:T(8,128)(2,1)S(1)}, u32[]{:S(2)}) copy-start(bf16[8,3,2,256,128]{4,3,2,1,0:T(8,128)(2,1)S(1)} %all-to-all-done.qkv_ref) | copy-start | bytes 9437188
  55.8 1.0 copy-start.1
  59.3 18.9 %collective-permute-start = (bf16[2,512,128]{2,1,0:T(8,128)(2,1)S(1)}, bf16[2,512,128]{2,1,0:T(8,128)(2,1)S(1)}, u32[]{:S(2)}, u32[]{:S(2)}) collective-permute-start(bf16[2,512,128]{2,1,0:T(8,128)(2,1)S(1)} %get-tuple-element.36), channel_id=1, source_target_pairs={{0,2},{1,3},{2,4},{3,5},{4,6},{5,7},{6,0},{7,1},{8,10},{9,11},{10,... | collective-permute-start | bytes 786440 | tf_op jit(solution)/shard_map/ppermute | solution.py:619
  61.9 16.3 %collective-permute-start.1 = (bf16[2,512,128]{2,1,0:T(8,128)(2,1)S(1)}, bf16[2,512,128]{2,1,0:T(8,128)(2,1)S(1)}, u32[]{:S(2)}, u32[]{:S(2)}) collective-permute-start(bf16[2,512,128]{2,1,0:T(8,128)(2,1)S(1)} %get-tuple-element.37), channel_id=1, source_target_pairs={{0,4},{1,5},{2,6},{3,7},{4,0},{5,1},{6,2},{7,3},{8,12},{9,13},{10,... | collective-permute-start | bytes 786440 | tf_op jit(solution)/shard_map/ppermute | solution.py:619
  64.7 13.5 %collective-permute-start.2 = (bf16[2,512,128]{2,1,0:T(8,128)(2,1)S(1)}, bf16[2,512,128]{2,1,0:T(8,128)(2,1)S(1)}, u32[]{:S(2)}, u32[]{:S(2)}) collective-permute-start(bf16[2,512,128]{2,1,0:T(8,128)(2,1)S(1)} %get-tuple-element.38), channel_id=1, source_target_pairs={{0,6},{1,7},{2,0},{3,1},{4,2},{5,3},{6,4},{7,5},{8,14},{9,15},{10,... | collective-permute-start | bytes 786440 | tf_op jit(solution)/shard_map/ppermute | solution.py:619
  78.2 0.7 copy-start.8
  78.2 0.8 copy-start.9
  79.0 0.7 copy-start.10
  79.7 19.5 %all-to-all-start.1 = ((bf16[4,2,512,128]{3,2,1,0:T(8,128)(2,1)}), bf16[4,2,512,128]{3,2,1,0:T(8,128)(2,1)S(1)}, u32[]{:S(2)}, u32[]{:S(2)}) async-start(bf16[4,2,512,128]{3,2,1,0:T(8,128)(2,1)} %gate.2), calls=%async_computation.1 | async-start | bytes 2097152 | tf_op jit(solution)/shard_map/all_to_all | solution.py:605
  91.3 24.3 %collective-permute-start.17 = (bf16[4,128,512]{2,1,0:T(8,128)(2,1)}, bf16[4,128,512]{2,1,0:T(8,128)(2,1)}, u32[]{:S(2)}, u32[]{:S(2)}) collective-permute-start(bf16[4,128,512]{2,1,0:T(8,128)(2,1)} %get-tuple-element.50), channel_id=1, source_target_pairs={{0,8},{8,16},{16,24},{24,0},{32,40},{40,48},{48,56},{56,32},{64,72... | collective-permute-start | bytes 1572872 | tf_op jit(solution)/shard_map/ppermute | solution.py:622
  91.4 41.0 %collective-permute-start.18 = (bf16[4,128,512]{2,1,0:T(8,128)(2,1)}, bf16[4,128,512]{2,1,0:T(8,128)(2,1)}, u32[]{:S(2)}, u32[]{:S(2)}) collective-permute-start(bf16[4,128,512]{2,1,0:T(8,128)(2,1)} %get-tuple-element.51), channel_id=1, source_target_pairs={{0,16},{8,24},{16,0},{24,8},{32,48},{40,56},{48,32},{56,40},{64,80... | collective-permute-start | bytes 1572872 | tf_op jit(solution)/shard_map/ppermute | solution.py:622
  93.0 39.4 %collective-permute-start.19 = (bf16[4,128,512]{2,1,0:T(8,128)(2,1)}, bf16[4,128,512]{2,1,0:T(8,128)(2,1)}, u32[]{:S(2)}, u32[]{:S(2)}) collective-permute-start(bf16[4,128,512]{2,1,0:T(8,128)(2,1)} %get-tuple-element.52), channel_id=1, source_target_pairs={{0,24},{8,0},{16,8},{24,16},{32,56},{40,32},{48,40},{56,48},{64,88... | collective-permute-start | bytes 1572872 | tf_op jit(solution)/shard_map/ppermute | solution.py:622
  94.5 37.9 %collective-permute-start.20 = (bf16[4,128,512]{2,1,0:T(8,128)(2,1)}, bf16[4,128,512]{2,1,0:T(8,128)(2,1)}, u32[]{:S(2)}, u32[]{:S(2)}) collective-permute-start(bf16[4,128,512]{2,1,0:T(8,128)(2,1)} %get-tuple-element.54), channel_id=1, source_target_pairs={{0,32},{8,40},{16,48},{24,56},{32,64},{40,72},{48,80},{56,88},{64,... | collective-permute-start | bytes 1572872 | tf_op jit(solution)/shard_map/ppermute | solution.py:623
  96.1 36.4 %collective-permute-start.21 = (bf16[4,128,512]{2,1,0:T(8,128)(2,1)}, bf16[4,128,512]{2,1,0:T(8,128)(2,1)}, u32[]{:S(2)}, u32[]{:S(2)}) collective-permute-start(bf16[4,128,512]{2,1,0:T(8,128)(2,1)} %get-tuple-element.55), channel_id=1, source_target_pairs={{0,96},{8,104},{16,112},{24,120},{32,0},{40,8},{48,16},{56,24},{64... | collective-permute-start | bytes 1572872 | tf_op jit(solution)/shard_map/ppermute | solution.py:623
  99.2 1.0 copy-start.7
  115.6 16.9 %collective-permute-start.22 = (bf16[4,128,512]{2,1,0:T(8,128)(2,1)}, bf16[4,128,512]{2,1,0:T(8,128)(2,1)S(1)}, u32[]{:S(2)}, u32[]{:S(2)}) collective-permute-start(bf16[4,128,512]{2,1,0:T(8,128)(2,1)} %gate.3), channel_id=1, source_target_pairs={{0,64},{8,72},{16,80},{24,88},{32,96},{40,104},{48,112},{56,120},{... | collective-permute-start | bytes 1572872 | tf_op jit(solution)/shard_map/ppermute | solution.py:626
  116.3 46.5 %all-to-all-start.2 = ((bf16[8,3,2,256,128]{4,3,2,1,0:T(8,128)(2,1)}), bf16[8,3,2,256,128]{4,3,2,1,0:T(8,128)(2,1)}, u32[]{:S(2)}, u32[]{:S(2)}) async-start(bf16[8,3,2,256,128]{4,3,2,1,0:T(8,128)(2,1)} %attention_backward.1.refs_12_.refs_1_), calls=%async_computation.2 | async-start | bytes 6291456 | tf_op jit(solution)/shard_map/all_to_all | solution.py:625
  132.4 28.0 %collective-permute-start.16 = (bf16[256,2048]{1,0:T(8,128)(2,1)}, bf16[256,2048]{1,0:T(8,128)(2,1)}, u32[]{:S(2)}, u32[]{:S(2)}) collective-permute-start(bf16[256,2048]{1,0:T(8,128)(2,1)} %get-tuple-element.46), channel_id=1, source_target_pairs={{0,1},{1,0},{2,3},{3,2},{4,5},{5,4},{6,7},{7,6},{8,9},{9,8},{10,11... | collective-permute-start | bytes 3145736 | tf_op jit(solution)/shard_map/ppermute | solution.py:630
  132.5 0.8 copy-start.29
  133.3 27.0 %copy-start.6 = (f32[256,2048]{1,0:T(8,128)S(1)}, f32[256,2048]{1,0:T(8,128)}, u32[]{:S(2)}) copy-start(f32[256,2048]{1,0:T(8,128)} %get-tuple-element.45) | copy-start | bytes 6291460
  136.7 6.3 %collective-permute-start.23 = (bf16[128,512]{1,0:T(8,128)(2,1)}, bf16[128,512]{1,0:T(8,128)(2,1)S(1)}, u32[]{:S(2)}, u32[]{:S(2)}) collective-permute-start(bf16[128,512]{1,0:T(8,128)(2,1)} %get-tuple-element.58), channel_id=1, source_target_pairs={{0,32},{8,40},{16,48},{24,56},{32,64},{40,72},{48,80},{56,88},{64,... | collective-permute-start | bytes 393224 | tf_op jit(solution)/shard_map/ppermute | solution.py:632
  138.0 7.8 %collective-permute-start.24 = (bf16[128,512]{1,0:T(8,128)(2,1)}, bf16[128,512]{1,0:T(8,128)(2,1)S(1)}, u32[]{:S(2)}, u32[]{:S(2)}) collective-permute-start(bf16[128,512]{1,0:T(8,128)(2,1)} %get-tuple-element.59), channel_id=1, source_target_pairs={{0,64},{8,72},{16,80},{24,88},{32,96},{40,104},{48,112},{56,120},{... | collective-permute-start | bytes 393224 | tf_op jit(solution)/shard_map/ppermute | solution.py:632
  139.7 8.0 %collective-permute-start.25 = (bf16[128,512]{1,0:T(8,128)(2,1)}, bf16[128,512]{1,0:T(8,128)(2,1)S(1)}, u32[]{:S(2)}, u32[]{:S(2)}) collective-permute-start(bf16[128,512]{1,0:T(8,128)(2,1)} %get-tuple-element.60), channel_id=1, source_target_pairs={{0,96},{8,104},{16,112},{24,120},{32,0},{40,8},{48,16},{56,24},{64... | collective-permute-start | bytes 393224 | tf_op jit(solution)/shard_map/ppermute | solution.py:632
  140.7 7.0 %collective-permute-start.26 = (bf16[128,512]{1,0:T(8,128)(2,1)}, bf16[128,512]{1,0:T(8,128)(2,1)S(1)}, u32[]{:S(2)}, u32[]{:S(2)}) collective-permute-start(bf16[128,512]{1,0:T(8,128)(2,1)} %get-tuple-element.62), channel_id=1, source_target_pairs={{0,8},{8,16},{16,24},{24,0},{32,40},{40,48},{48,56},{56,32},{64,72... | collective-permute-start | bytes 393224 | tf_op jit(solution)/shard_map/ppermute | solution.py:633
  143.0 8.4 %copy-start.15 = (bf16[128,512]{1,0:T(8,128)(2,1)}, bf16[128,512]{1,0:T(8,128)(2,1)S(1)}, u32[]{:S(2)}) copy-start(bf16[128,512]{1,0:T(8,128)(2,1)S(1)} %collective-permute-done.23.refs_1_) | copy-start | bytes 393220
  143.0 7.2 %collective-permute-start.27 = (bf16[128,512]{1,0:T(8,128)(2,1)}, bf16[128,512]{1,0:T(8,128)(2,1)S(1)}, u32[]{:S(2)}, u32[]{:S(2)}) collective-permute-start(bf16[128,512]{1,0:T(8,128)(2,1)} %get-tuple-element.63), channel_id=1, source_target_pairs={{0,16},{8,24},{16,0},{24,8},{32,48},{40,56},{48,32},{56,40},{64,80... | collective-permute-start | bytes 393224 | tf_op jit(solution)/shard_map/ppermute | solution.py:633
  145.8 5.6 %copy-start.16 = (bf16[128,512]{1,0:T(8,128)(2,1)}, bf16[128,512]{1,0:T(8,128)(2,1)S(1)}, u32[]{:S(2)}) copy-start(bf16[128,512]{1,0:T(8,128)(2,1)S(1)} %collective-permute-done.24.refs_2_) | copy-start | bytes 393220
  145.8 5.6 %collective-permute-start.28 = (bf16[128,512]{1,0:T(8,128)(2,1)}, bf16[128,512]{1,0:T(8,128)(2,1)S(1)}, u32[]{:S(2)}, u32[]{:S(2)}) collective-permute-start(bf16[128,512]{1,0:T(8,128)(2,1)} %get-tuple-element.64), channel_id=1, source_target_pairs={{0,24},{8,0},{16,8},{24,16},{32,56},{40,32},{48,40},{56,48},{64,88... | collective-permute-start | bytes 393224 | tf_op jit(solution)/shard_map/ppermute | solution.py:633
  147.7 3.7 %copy-start.17 = (bf16[128,512]{1,0:T(8,128)(2,1)}, bf16[128,512]{1,0:T(8,128)(2,1)S(1)}, u32[]{:S(2)}) copy-start(bf16[128,512]{1,0:T(8,128)(2,1)S(1)} %collective-permute-done.25.refs_3_) | copy-start | bytes 393220
  147.7 3.7 %copy-start.18 = (bf16[128,512]{1,0:T(8,128)(2,1)}, bf16[128,512]{1,0:T(8,128)(2,1)S(1)}, u32[]{:S(2)}) copy-start(bf16[128,512]{1,0:T(8,128)(2,1)S(1)} %collective-permute-done.26.refs_5_) | copy-start | bytes 393220
  150.2 1.2 copy-start.19
  151.4 0.7 copy-start.20
  154.2 19.5 %collective-permute-start.31 = (bf16[128,1024]{1,0:T(8,128)(2,1)}, bf16[128,1024]{1,0:T(8,128)(2,1)S(1)}, u32[]{:S(2)}, u32[]{:S(2)}) collective-permute-start(bf16[128,1024]{1,0:T(8,128)(2,1)} %summed_side_by_side.1.a_ref), channel_id=1, source_target_pairs={{0,6},{1,7},{2,4},{3,5},{4,2},{5,3},{6,0},{7,1},{8,14},{9,15},{10,... | collective-permute-start | bytes 786440 | tf_op jit(solution)/shard_map/ppermute | solution.py:636
  159.7 13.9 %collective-permute-start.30 = (bf16[128,1024]{1,0:T(8,128)(2,1)}, bf16[128,1024]{1,0:T(8,128)(2,1)S(1)}, u32[]{:S(2)}, u32[]{:S(2)}) collective-permute-start(bf16[128,1024]{1,0:T(8,128)(2,1)} %summed_side_by_side.1.a_ref), channel_id=1, source_target_pairs={{0,4},{1,5},{2,6},{3,7},{4,0},{5,1},{6,2},{7,3},{8,12},{9,13},{10,... | collective-permute-start | bytes 786440 | tf_op jit(solution)/shard_map/ppermute | solution.py:636
  160.1 13.5 %collective-permute-start.29 = (bf16[128,1024]{1,0:T(8,128)(2,1)}, bf16[128,1024]{1,0:T(8,128)(2,1)S(1)}, u32[]{:S(2)}, u32[]{:S(2)}) collective-permute-start(bf16[128,1024]{1,0:T(8,128)(2,1)} %summed_side_by_side.1.a_ref), channel_id=1, source_target_pairs={{0,2},{1,3},{2,0},{3,1},{4,6},{5,7},{6,4},{7,5},{8,10},{9,11},{10,... | collective-permute-start | bytes 786440 | tf_op jit(solution)/shard_map/ppermute | solution.py:636
  173.6 0.7 copy-start.12
  173.6 0.8 copy-start.13
  173.6 0.9 copy-start.14
  176.5 1.9 %collective-permute-start.32 = (bf16[128,1024]{1,0:T(8,128)(2,1)}, bf16[128,1024]{1,0:T(8,128)(2,1)S(1)}, u32[]{:S(2)}, u32[]{:S(2)}) collective-permute-start(bf16[128,1024]{1,0:T(8,128)(2,1)} %summed_over_chips.1.own_ref), channel_id=1, source_target_pairs={{0,1},{1,0},{2,3},{3,2},{4,5},{5,4},{6,7},{7,6},{8,9},{9,8},{10,11... | collective-permute-start | bytes 786440 | tf_op jit(solution)/shard_map/ppermute | solution.py:638
  178.5 0.7 copy-start.11
  (2 other events, 1.3 us)

commit v5 on v4

--- a/solution.py
+++ b/solution.py
@@ -492,7 +492,7 @@
     del refs
 
 
-def gate(values, *after):
+def gate(values, *after, weight=0):
     return pl.pallas_call(
         gate_kernel,
         out_shape=jax.ShapeDtypeStruct(values.shape, values.dtype),
@@ -500,6 +500,7 @@
         out_specs=HBM,
         input_output_aliases={0: 0},
         compiler_params=pltpu.CompilerParams(vmem_limit_bytes=VMEM_LIMIT),
+        cost_estimate=cost(weight, 0),
         name="gate",
     )(values, *after)
 
@@ -623,7 +624,7 @@
     y_first = [parts[side]] + [lax.ppermute(parts[side + k], "dp", y_shift(k)) for k in (1, side - 1)]
     grads = attention_backward(place, lists, counts, qkv, g, a, lse, (parts[0],), width)
     grads_home = lax.all_to_all(grads, "seq", split_axis=0, concat_axis=0, tiled=True)
-    y_first += [lax.ppermute(gate(parts[side + k], grads), "dp", y_shift(k)) for k in range(2, side - 1)]
+    y_first += [lax.ppermute(gate(parts[side + k], grads, weight=10**12), "dp", y_shift(k)) for k in range(2, side - 1)]
 
     z_sum, y_sum = summed(z_first, y_first)
     out_own, out_other = project(place, a_home, weights, grads, side)

time: 182 us -> 182 us (level)
  no operation moved by 1% of the time
where the time goes in v5:
time: 182 us; the launch traced here: 181 us
  starting transfers between devices  68.4 us (38%)
  Pallas kernels  64.6 us (35%)
  waiting for transfers between devices  35.5 us (20%)
  local copies, waits for them, and re-layouts  9.39 us (5%)
  other arithmetic  2.48 us (1%)
    pallas_call x1, Pallas kernels, attention_backward(): pl.pallas_call(functools.partial(backward_kernel, UNITS_AT_ONCE, slots, u...  15.3 us
    unnamed x61, local copies, waits for them, and re-layouts  8.5 us
    all_to_all x1, starting transfers between devices, per_device(): lax.all_to_all(grads, 'seq', split_axis=0, concat_axis=0, tiled=True)  8.16 us
    pallas_call x1, Pallas kernels, project(): pl.pallas_call(functools.partial(project_kernel, side), out_shape=(jax.Sh...  7.85 us
    ppermute x3, waiting for transfers between devices, per_device(): lax.ppermute(lines_z, 'dp', y_shift(k))  7.36 us
    ppermute x3, waiting for transfers between devices, per_device(): lax.ppermute(lines_y, 'dp', z_shift(k))  7.05 us
    pallas_call x1, Pallas kernels, attention_forward(): pl.pallas_call(functools.partial(forward_kernel, UNITS_AT_ONCE, slots, un...  7.04 us
    ppermute x3, starting transfers between devices, per_device(): lax.ppermute(lines_y, 'dp', z_shift(k))  6.47 us
  transfers between devices with their start and end apart: 36, of which 14 were waited for; matrix products, arithmetic and copies ran while one was open for 2% of the time, Pallas kernels for 31%

profile of v5, /device:TPU:1, one launch (start us, length us, event | category | flops | bytes accessed | tf_op | source)
XLA Modules:
  0.0 181.3 jit_solution(6878334181802903709)
XLA Ops:
  0.6 3.3 %pack_heads.1 = bf16[8,3,2,256,128]{4,3,2,1,0:T(8,128)(2,1)} custom-call(bf16[1,256,2048]{2,1,0:T(8,128)(2,1)} %q_ref.1, bf16[1,256,2048]{2,1,0:T(8,128)(2,1)} %k_ref.1, bf16[1,256,2048]{2,1,0:T(8,128)(2,1)} %v_ref.1), custom_call_target="tpu_custom_call" | custom-call | bytes 6291456 | tf_op jit(solution)/shard_map/pack_heads/pallas_call | solution.py:54
  4.0 5.9 %all-to-all-start = ((bf16[8,3,2,256,128]{4,3,2,1,0:T(8,128)(2,1)}), bf16[8,3,2,256,128]{4,3,2,1,0:T(8,128)(2,1)S(1)}, u32[]{:S(2)}, u32[]{:S(2)}) async-start(bf16[8,3,2,256,128]{4,3,2,1,0:T(8,128)(2,1)} %pack_heads.1), calls=%async_computation | async-start | bytes 6291456 | tf_op jit(solution)/shard_map/all_to_all | solution.py:616
  10.0 0.6 stack.23.place_ref
  10.6 1.8 %pack_weight.1 = (bf16[128,512]{1,0:T(8,128)(2,1)}, bf16[128,512]{1,0:T(8,128)(2,1)}) custom-call(s32[6]{0:T(128)} %stack.23.place_ref, bf16[128,2048]{1,0:T(8,128)(2,1)} %in_ref.1), custom_call_target="tpu_custom_call" | custom-call | bytes 786432 | tf_op jit(solution)/shard_map/pack_weight/pallas_call | solution.py:106
  12.4 3.8 %collective-permute-start.5 = (bf16[128,512]{1,0:T(8,128)(2,1)}, bf16[128,512]{1,0:T(8,128)(2,1)S(1)}, u32[]{:S(2)}, u32[]{:S(2)}) collective-permute-start(bf16[128,512]{1,0:T(8,128)(2,1)} %get-tuple-element.39.refs_0_), channel_id=1, source_target_pairs={{0,24},{8,0},{16,8},{24,16},{32,56},{40,32},{48,40},{56,48},{64,88... | collective-permute-start | bytes 393224 | tf_op jit(solution)/shard_map/ppermute | solution.py:610
  16.1 0.7 collective-permute-start.3
  16.8 2.7 %collective-permute-start.8 = (bf16[128,512]{1,0:T(8,128)(2,1)}, bf16[128,512]{1,0:T(8,128)(2,1)S(1)}, u32[]{:S(2)}, u32[]{:S(2)}) collective-permute-start(bf16[128,512]{1,0:T(8,128)(2,1)} %get-tuple-element.40.refs_4_), channel_id=1, source_target_pairs={{0,96},{8,104},{16,112},{24,120},{32,0},{40,8},{48,16},{56,24},{64... | collective-permute-start | bytes 393224 | tf_op jit(solution)/shard_map/ppermute | solution.py:611
  19.9 2.3 %collective-permute-done.5.refs_3_ = bf16[128,512]{1,0:T(8,128)(2,1)S(1)} collective-permute-done((bf16[128,512]{1,0:T(8,128)(2,1)}, bf16[128,512]{1,0:T(8,128)(2,1)S(1)}, u32[]{:S(2)}, u32[]{:S(2)}) %collective-permute-start.5) | collective-permute-done | bytes 131104 | tf_op jit(solution)/shard_map/ppermute | solution.py:610
  22.2 1.3 collective-permute-start.6
  23.5 2.0 %collective-permute-done.3.refs_1_ = bf16[128,512]{1,0:T(8,128)(2,1)S(1)} collective-permute-done((bf16[128,512]{1,0:T(8,128)(2,1)}, bf16[128,512]{1,0:T(8,128)(2,1)S(1)}, u32[]{:S(2)}, u32[]{:S(2)}) %collective-permute-start.3) | collective-permute-done | bytes 131104 | tf_op jit(solution)/shard_map/ppermute | solution.py:610
  25.6 3.6 %collective-permute-done.6.refs_5_ = bf16[128,512]{1,0:T(8,128)(2,1)S(1)} collective-permute-done((bf16[128,512]{1,0:T(8,128)(2,1)}, bf16[128,512]{1,0:T(8,128)(2,1)S(1)}, u32[]{:S(2)}, u32[]{:S(2)}) %collective-permute-start.6) | collective-permute-done | bytes 131104 | tf_op jit(solution)/shard_map/ppermute | solution.py:611
  29.2 0.6 copy-done.26
  29.9 2.3 %stack_lines.1 = (bf16[4,128,512]{2,1,0:T(8,128)(2,1)}, bf16[4,128,512]{2,1,0:T(8,128)(2,1)}) custom-call(bf16[128,512]{1,0:T(8,128)(2,1)} %get-tuple-element.39.refs_0_, bf16[128,512]{1,0:T(8,128)(2,1)} %copy-done.23, bf16[128,512]{1,0:T(8,128)(2,1)} %copy-done.22, bf16[128,512]{1,0:T(8,128)(2,1)} %copy-done.21, ...), custom_call_target="tpu_custom_call" | custom-call | bytes 2097152 | tf_op jit(solution)/shard_map/stack_lines/pallas_call | solution.py:126
  32.7 2.2 %collective-permute-start.15 = (bf16[256,2048]{1,0:T(8,128)(2,1)}, bf16[256,2048]{1,0:T(8,128)(2,1)}, u32[]{:S(2)}, u32[]{:S(2)}) collective-permute-start(bf16[256,2048]{1,0:T(8,128)(2,1)} %bitcast.10), channel_id=1, source_target_pairs={{0,1},{1,0},{2,3},{3,2},{4,5},{5,4},{6,7},{7,6},{8,9},{9,8},{10,11... | collective-permute-start | bytes 3145736 | tf_op jit(solution)/shard_map/ppermute | solution.py:618
  35.4 0.8 collective-permute-start.9
  36.2 3.3 %collective-permute-start.14 = (bf16[4,128,512]{2,1,0:T(8,128)(2,1)}, bf16[4,128,512]{2,1,0:T(8,128)(2,1)}, u32[]{:S(2)}, u32[]{:S(2)}) collective-permute-start(bf16[4,128,512]{2,1,0:T(8,128)(2,1)} %get-tuple-element.42.refs_4_.refs_8_), channel_id=1, source_target_pairs={{0,24},{8,0},{16,8},{24,16},{32,56},{40,32},{48,40},{56,48},{64,88... | collective-permute-start | bytes 1572872 | tf_op jit(solution)/shard_map/ppermute | solution.py:614
  39.5 5.4 %collective-permute-done.11.refs_3_.refs_7_ = bf16[4,128,512]{2,1,0:T(8,128)(2,1)} collective-permute-done((bf16[4,128,512]{2,1,0:T(8,128)(2,1)}, bf16[4,128,512]{2,1,0:T(8,128)(2,1)}, u32[]{:S(2)}, u32[]{:S(2)}) %collective-permute-start.11) | collective-permute-done | bytes 524320 | tf_op jit(solution)/shard_map/ppermute | solution.py:613
  44.9 3.2 %collective-permute-start.13 = (bf16[4,128,512]{2,1,0:T(8,128)(2,1)}, bf16[4,128,512]{2,1,0:T(8,128)(2,1)}, u32[]{:S(2)}, u32[]{:S(2)}) collective-permute-start(bf16[4,128,512]{2,1,0:T(8,128)(2,1)} %get-tuple-element.42.refs_4_.refs_8_), channel_id=1, source_target_pairs={{0,16},{8,24},{16,0},{24,8},{32,48},{40,56},{48,32},{56,40},{64,80... | collective-permute-start | bytes 1572872 | tf_op jit(solution)/shard_map/ppermute | solution.py:614
  48.1 0.6 copy-done.2
  48.7 7.0 %attention_forward.1 = (bf16[4,2,512,128]{3,2,1,0:T(8,128)(2,1)S(1)}, f32[32,8,128]{2,1,0:T(8,128)S(1)}, bf16[2,512,128]{2,1,0:T(8,128)(2,1)S(1)}, bf16[2,512,12...) custom-call(s32[6]{0:T(128)S(1)} %copy-done.2, s32[1792]{0:T(1024)S(1)} %reshape.16.tiles_ref, s32[256]{0:T(256)S(1)} %reshape.17.counts_ref, ...), custom_call_target="tpu_custom_call" | custom-call | flops 299999985664 | bytes 1048576 | tf_op jit(solution)/shard_map/attention_forward/pallas_call | solution.py:235
  55.8 1.0 copy-done.1
  56.7 0.6 copy-done.5
  57.4 1.9 %collective-permute-done.9.refs_1_.refs_5_ = bf16[4,128,512]{2,1,0:T(8,128)(2,1)} collective-permute-done((bf16[4,128,512]{2,1,0:T(8,128)(2,1)}, bf16[4,128,512]{2,1,0:T(8,128)(2,1)}, u32[]{:S(2)}, u32[]{:S(2)}) %collective-permute-start.9) | collective-permute-done | bytes 524320 | tf_op jit(solution)/shard_map/ppermute | solution.py:613
  59.3 1.9 %collective-permute-start = (bf16[2,512,128]{2,1,0:T(8,128)(2,1)S(1)}, bf16[2,512,128]{2,1,0:T(8,128)(2,1)S(1)}, u32[]{:S(2)}, u32[]{:S(2)}) collective-permute-start(bf16[2,512,128]{2,1,0:T(8,128)(2,1)S(1)} %get-tuple-element.36), channel_id=1, source_target_pairs={{0,2},{1,3},{2,4},{3,5},{4,6},{5,7},{6,0},{7,1},{8,10},{9,11},{10,... | collective-permute-start | bytes 786440 | tf_op jit(solution)/shard_map/ppermute | solution.py:620
  61.3 0.7 collective-permute-done.14.refs_7_.refs_11_
  61.9 2.8 %collective-permute-start.1 = (bf16[2,512,128]{2,1,0:T(8,128)(2,1)S(1)}, bf16[2,512,128]{2,1,0:T(8,128)(2,1)S(1)}, u32[]{:S(2)}, u32[]{:S(2)}) collective-permute-start(bf16[2,512,128]{2,1,0:T(8,128)(2,1)S(1)} %get-tuple-element.37), channel_id=1, source_target_pairs={{0,4},{1,5},{2,6},{3,7},{4,0},{5,1},{6,2},{7,3},{8,12},{9,13},{10,... | collective-permute-start | bytes 786440 | tf_op jit(solution)/shard_map/ppermute | solution.py:620
  64.7 0.9 collective-permute-start.2
  65.6 6.4 %collective-permute-done.12.refs_5_.refs_9_ = bf16[4,128,512]{2,1,0:T(8,128)(2,1)} collective-permute-done((bf16[4,128,512]{2,1,0:T(8,128)(2,1)}, bf16[4,128,512]{2,1,0:T(8,128)(2,1)}, u32[]{:S(2)}, u32[]{:S(2)}) %collective-permute-start.12) | collective-permute-done | bytes 524320 | tf_op jit(solution)/shard_map/ppermute | solution.py:614
  72.0 6.2 %grad_attn.1.refs_0_ = bf16[4,2,512,128]{3,2,1,0:T(8,128)(2,1)} custom-call(s32[6]{0:T(128)} %stack.23.place_ref, bf16[256,2048]{1,0:T(8,128)(2,1)} %bitcast.11, bf16[256,2048]{1,0:T(8,128)(2,1)} %collective-permute-done.15.other_ref, bf16[4,128,512]{2,1,0:T(8,128)(2,1)} %get-tuple-element.41.refs_0_.refs_4_, ...), custom_call_target="tpu_custom_call" | custom-call | flops 2147483648 | bytes 7340032 | tf_op jit(solution)/shard_map/grad_attn/pallas_call | solution.py:374
  78.2 0.7 copy-done.8
  79.0 0.7 copy-done.10
  79.7 5.1 %all-to-all-start.1 = ((bf16[4,2,512,128]{3,2,1,0:T(8,128)(2,1)}), bf16[4,2,512,128]{3,2,1,0:T(8,128)(2,1)S(1)}, u32[]{:S(2)}, u32[]{:S(2)}) async-start(bf16[4,2,512,128]{3,2,1,0:T(8,128)(2,1)} %gate.2), calls=%async_computation.1 | async-start | bytes 2097152 | tf_op jit(solution)/shard_map/all_to_all | solution.py:606
  84.8 6.4 %grad_weight_parts.1 = (bf16[4,128,512]{2,1,0:T(8,128)(2,1)}, bf16[4,128,512]{2,1,0:T(8,128)(2,1)}, bf16[4,128,512]{2,1,0:T(8,128)(2,1)}, bf16[4,128,512]{2,1,0:...) custom-call(s32[6]{0:T(128)} %stack.23.place_ref, ...), custom_call_target="tpu_custom_call" | custom-call | flops 2147483648 | bytes 7340032 | tf_op jit(solution)/shard_map/grad_weight_parts/pallas_call | solution.py:473
  91.4 1.7 collective-permute-start.18
  93.0 1.5 collective-permute-start.19
  94.5 1.5 collective-permute-start.20
  96.1 2.7 %collective-permute-start.21 = (bf16[4,128,512]{2,1,0:T(8,128)(2,1)}, bf16[4,128,512]{2,1,0:T(8,128)(2,1)}, u32[]{:S(2)}, u32[]{:S(2)}) collective-permute-start(bf16[4,128,512]{2,1,0:T(8,128)(2,1)} %get-tuple-element.55), channel_id=1, source_target_pairs={{0,96},{8,104},{16,112},{24,120},{32,0},{40,8},{48,16},{56,24},{64... | collective-permute-start | bytes 1572872 | tf_op jit(solution)/shard_map/ppermute | solution.py:624
  99.2 1.0 copy-done.7
  100.2 15.3 %attention_backward.1.refs_12_.refs_1_ = bf16[8,3,2,256,128]{4,3,2,1,0:T(8,128)(2,1)} custom-call(s32[6]{0:T(128)} %stack.23.place_ref, s32[1792]{0:T(1024)} %copy-done.3, s32[256]{0:T(256)} %copy-done.4, bf16[8,3,2,256,128]{4,3,2,1,0:T(8,128)(2,1)} %copy-done, bf16[4,2,512,128]{3,2,1,0:T(8,128)(2,1)} %copy-done.7, bf16[4,2,512,128]{3,2,1,0:T(8,128)(2,1)} %copy-done.1, ...), custom_call_target="tpu_custom_call" | custom-call | flops 299999985664 | bytes 1048576 | tf_op jit(solution)/shard_map/attention_backward/pallas_call | solution.py:321
  115.6 0.8 collective-permute-start.22
  116.3 8.2 %all-to-all-start.2 = ((bf16[8,3,2,256,128]{4,3,2,1,0:T(8,128)(2,1)}), bf16[8,3,2,256,128]{4,3,2,1,0:T(8,128)(2,1)}, u32[]{:S(2)}, u32[]{:S(2)}) async-start(bf16[8,3,2,256,128]{4,3,2,1,0:T(8,128)(2,1)} %attention_backward.1.refs_12_.refs_1_), calls=%async_computation.2 | async-start | bytes 6291456 | tf_op jit(solution)/shard_map/all_to_all | solution.py:626
  124.5 7.8 %project.1 = (f32[256,2048]{1,0:T(8,128)}, bf16[256,2048]{1,0:T(8,128)(2,1)}) custom-call(s32[6]{0:T(128)} %stack.23.place_ref, bf16[4,2,512,128]{3,2,1,0:T(8,128)(2,1)} %copy-done.1, bf16[2,512,128]{2,1,0:T(8,128)(2,1)} %copy-done.8, bf16[2,512,128]{2,1,0:T(8,128)(2,1)} %copy-done.9, bf16[2,512,128]{2,1,0:T(8,128)(2,1)} %copy-done.10, ...), custom_call_target="tpu_custom_call" | custom-call | flops 2147483648 | bytes 8388608 | tf_op jit(solution)/shard_map/project/pallas_call | solution.py:428
  132.5 0.8 copy-done.29
  133.3 3.4 %summed.1 = (bf16[128,512]{1,0:T(8,128)(2,1)}, bf16[128,512]{1,0:T(8,128)(2,1)}, bf16[128,512]{1,0:T(8,128)(2,1)}, bf16[128,512]{1,0:T(8,128)(2,1)}, bf16[128,51...) custom-call(bf16[4,128,512]{2,1,0:T(8,128)(2,1)} %get-tuple-element.44.refs_0_, ...), custom_call_target="tpu_custom_call" | custom-call | flops 999999995904 | bytes 1048576 | tf_op jit(solution)/shard_map/summed/pallas_call | solution.py:521
  136.7 1.3 collective-permute-start.23
  138.0 1.7 collective-permute-start.24
  139.7 1.1 collective-permute-start.25
  140.7 1.8 collective-permute-start.26
  143.0 2.0 %collective-permute-start.27 = (bf16[128,512]{1,0:T(8,128)(2,1)}, bf16[128,512]{1,0:T(8,128)(2,1)S(1)}, u32[]{:S(2)}, u32[]{:S(2)}) collective-permute-start(bf16[128,512]{1,0:T(8,128)(2,1)} %get-tuple-element.63), channel_id=1, source_target_pairs={{0,16},{8,24},{16,0},{24,8},{32,48},{40,56},{48,32},{56,40},{64,80... | collective-permute-start | bytes 393224 | tf_op jit(solution)/shard_map/ppermute | solution.py:634
  145.0 0.8 collective-permute-done.24.refs_2_
  145.8 1.9 %collective-permute-start.28 = (bf16[128,512]{1,0:T(8,128)(2,1)}, bf16[128,512]{1,0:T(8,128)(2,1)S(1)}, u32[]{:S(2)}, u32[]{:S(2)}) collective-permute-start(bf16[128,512]{1,0:T(8,128)(2,1)} %get-tuple-element.64), channel_id=1, source_target_pairs={{0,24},{8,0},{16,8},{24,16},{32,56},{40,32},{48,40},{56,48},{64,88... | collective-permute-start | bytes 393224 | tf_op jit(solution)/shard_map/ppermute | solution.py:634
  147.7 2.5 %collective-permute-done.27.refs_6_ = bf16[128,512]{1,0:T(8,128)(2,1)S(1)} collective-permute-done((bf16[128,512]{1,0:T(8,128)(2,1)}, bf16[128,512]{1,0:T(8,128)(2,1)S(1)}, u32[]{:S(2)}, u32[]{:S(2)}) %collective-permute-start.27) | collective-permute-done | bytes 131104 | tf_op jit(solution)/shard_map/ppermute | solution.py:634
  150.2 1.2 collective-permute-done.28.refs_7_
  151.4 0.6 copy-done.20
  152.0 2.1 %summed_side_by_side.1.a_ref = bf16[128,1024]{1,0:T(8,128)(2,1)} custom-call(bf16[128,512]{1,0:T(8,128)(2,1)} %get-tuple-element.57.refs_0_, bf16[128,512]{1,0:T(8,128)(2,1)} %copy-done.15, bf16[128,512]{1,0:T(8,128)(2,1)} %copy-done.16, bf16[128,512]{1,0:T(8,128)(2,1)} %copy-done.17, bf16[128,512]{1,0:T(8,128)(2,1)} %get-tuple-element.61.refs_4_, ...), custom_call_target="tpu_custom_call" | custom-call | bytes 1310720 | tf_op jit(solution)/shard_map/summed_side_by_side/pallas_call | solution.py:546
  154.1 5.6 %collective-permute-start.31 = (bf16[128,1024]{1,0:T(8,128)(2,1)}, bf16[128,1024]{1,0:T(8,128)(2,1)S(1)}, u32[]{:S(2)}, u32[]{:S(2)}) collective-permute-start(bf16[128,1024]{1,0:T(8,128)(2,1)} %summed_side_by_side.1.a_ref), channel_id=1, source_target_pairs={{0,6},{1,7},{2,4},{3,5},{4,2},{5,3},{6,0},{7,1},{8,14},{9,15},{10,... | collective-permute-start | bytes 786440 | tf_op jit(solution)/shard_map/ppermute | solution.py:637
  160.3 2.5 %add_convert_fusion.refs_1_ = bf16[256,2048]{1,0:T(8,128)(2,1)} fusion(f32[256,2048]{1,0:T(8,128)S(1)} %copy-done.6, bf16[256,2048]{1,0:T(8,128)(2,1)} %collective-permute-done.16), kind=kLoop, calls=%fused_computation | loop fusion | flops 1572864 | bytes 4194304 | tf_op jit(solution)/shard_map/convert_element_type | solution.py:631
  162.8 4.5 %unpack_heads.1 = (bf16[1,256,2048]{2,1,0:T(8,128)(2,1)}, bf16[1,256,2048]{2,1,0:T(8,128)(2,1)}, bf16[1,256,2048]{2,1,0:T(8,128)(2,1)}) custom-call(bf16[8,3,2,256,128]{4,3,2,1,0:T(8,128)(2,1)} %all-to-all-done.2.in_ref), custom_call_target="tpu_custom_call" | custom-call | bytes 6291456 | tf_op jit(solution)/shard_map/unpack_heads/pallas_call | solution.py:83
  167.3 6.3 %collective-permute-done.31.d_ref = bf16[128,1024]{1,0:T(8,128)(2,1)S(1)} collective-permute-done((bf16[128,1024]{1,0:T(8,128)(2,1)}, bf16[128,1024]{1,0:T(8,128)(2,1)S(1)}, u32[]{:S(2)}, u32[]{:S(2)}) %collective-permute-start.31) | collective-permute-done | bytes 262176 | tf_op jit(solution)/shard_map/ppermute | solution.py:637
  173.6 0.7 copy-done.12
  174.5 2.0 %summed_over_chips.1.own_ref = bf16[128,1024]{1,0:T(8,128)(2,1)} custom-call(bf16[128,1024]{1,0:T(8,128)(2,1)} %summed_side_by_side.1.a_ref, bf16[128,1024]{1,0:T(8,128)(2,1)} %copy-done.14, bf16[128,1024]{1,0:T(8,128)(2,1)} %copy-done.13, bf16[128,1024]{1,0:T(8,128)(2,1)} %copy-done.12, bf16[1,256,2048]{2,1,0:T(8,128)(2,1)} %get-tuple-element.31.refs_0_, ...), custom_call_target="tpu_custom_call" | custom-call | bytes 1310720 | tf_op jit(solution)/shard_map/summed_over_chips/pallas_call | solution.py:564
  177.1 1.4 collective-permute-done.32.other_ref
  178.5 0.7 copy-done.11
  179.1 2.1 %unpack_weight.1 = f32[128,2048]{1,0:T(8,128)} custom-call(s32[6]{0:T(128)} %stack.23.place_ref, bf16[128,1024]{1,0:T(8,128)(2,1)} %summed_over_chips.1.own_ref, bf16[128,1024]{1,0:T(8,128)(2,1)} %copy-done.11), custom_call_target="tpu_custom_call" | custom-call | bytes 1572864 | tf_op jit(solution)/shard_map/unpack_weight/pallas_call | solution.py:145
  (88 shorter events, 4.1 us)
Async XLA Ops:
  4.0 31.0 %copy-start.28 = (s32[1,16,16]{2,1,0:T(8,128)S(1)}, s32[1,16,16]{2,1,0:T(8,128)}, u32[]{:S(2)}) copy-start(s32[1,16,16]{2,1,0:T(8,128)} %param.13) | copy-start | bytes 3076
  4.0 31.0 %copy-start.27 = (s32[1,16,16,7]{2,1,3,0:T(8,128)S(1)}, s32[1,16,16,7]{2,1,3,0:T(8,128)}, u32[]{:S(2)}) copy-start(s32[1,16,16,7]{2,1,3,0:T(8,128)} %param.12) | copy-start | bytes 21508
  4.0 44.1 %all-to-all-start = ((bf16[8,3,2,256,128]{4,3,2,1,0:T(8,128)(2,1)}), bf16[8,3,2,256,128]{4,3,2,1,0:T(8,128)(2,1)S(1)}, u32[]{:S(2)}, u32[]{:S(2)}) async-start(bf16[8,3,2,256,128]{4,3,2,1,0:T(8,128)(2,1)} %pack_heads.1), calls=%async_computation | async-start | bytes 6291456 | tf_op jit(solution)/shard_map/all_to_all | solution.py:616
  12.4 9.8 %collective-permute-start.5 = (bf16[128,512]{1,0:T(8,128)(2,1)}, bf16[128,512]{1,0:T(8,128)(2,1)S(1)}, u32[]{:S(2)}, u32[]{:S(2)}) collective-permute-start(bf16[128,512]{1,0:T(8,128)(2,1)} %get-tuple-element.39.refs_0_), channel_id=1, source_target_pairs={{0,24},{8,0},{16,8},{24,16},{32,56},{40,32},{48,40},{56,48},{64,88... | collective-permute-start | bytes 393224 | tf_op jit(solution)/shard_map/ppermute | solution.py:610
  16.1 7.4 %collective-permute-start.4 = (bf16[128,512]{1,0:T(8,128)(2,1)}, bf16[128,512]{1,0:T(8,128)(2,1)S(1)}, u32[]{:S(2)}, u32[]{:S(2)}) collective-permute-start(bf16[128,512]{1,0:T(8,128)(2,1)} %get-tuple-element.39.refs_0_), channel_id=1, source_target_pairs={{0,16},{8,24},{16,0},{24,8},{32,48},{40,56},{48,32},{56,40},{64,80... | collective-permute-start | bytes 393224 | tf_op jit(solution)/shard_map/ppermute | solution.py:610
  16.1 9.4 %collective-permute-start.3 = (bf16[128,512]{1,0:T(8,128)(2,1)}, bf16[128,512]{1,0:T(8,128)(2,1)S(1)}, u32[]{:S(2)}, u32[]{:S(2)}) collective-permute-start(bf16[128,512]{1,0:T(8,128)(2,1)} %get-tuple-element.39.refs_0_), channel_id=1, source_target_pairs={{0,8},{8,16},{16,24},{24,0},{32,40},{40,48},{48,56},{56,32},{64,72... | collective-permute-start | bytes 393224 | tf_op jit(solution)/shard_map/ppermute | solution.py:610
  16.8 8.7 %collective-permute-start.8 = (bf16[128,512]{1,0:T(8,128)(2,1)}, bf16[128,512]{1,0:T(8,128)(2,1)S(1)}, u32[]{:S(2)}, u32[]{:S(2)}) collective-permute-start(bf16[128,512]{1,0:T(8,128)(2,1)} %get-tuple-element.40.refs_4_), channel_id=1, source_target_pairs={{0,96},{8,104},{16,112},{24,120},{32,0},{40,8},{48,16},{56,24},{64... | collective-permute-start | bytes 393224 | tf_op jit(solution)/shard_map/ppermute | solution.py:611
  19.6 6.0 %collective-permute-start.7 = (bf16[128,512]{1,0:T(8,128)(2,1)}, bf16[128,512]{1,0:T(8,128)(2,1)S(1)}, u32[]{:S(2)}, u32[]{:S(2)}) collective-permute-start(bf16[128,512]{1,0:T(8,128)(2,1)} %get-tuple-element.40.refs_4_), channel_id=1, source_target_pairs={{0,64},{8,72},{16,80},{24,88},{32,96},{40,104},{48,112},{56,120},{... | collective-permute-start | bytes 393224 | tf_op jit(solution)/shard_map/ppermute | solution.py:611
  22.2 7.0 %copy-start.21 = (bf16[128,512]{1,0:T(8,128)(2,1)}, bf16[128,512]{1,0:T(8,128)(2,1)S(1)}, u32[]{:S(2)}) copy-start(bf16[128,512]{1,0:T(8,128)(2,1)S(1)} %collective-permute-done.5.refs_3_) | copy-start | bytes 393220
  22.2 7.0 %collective-permute-start.6 = (bf16[128,512]{1,0:T(8,128)(2,1)}, bf16[128,512]{1,0:T(8,128)(2,1)S(1)}, u32[]{:S(2)}, u32[]{:S(2)}) collective-permute-start(bf16[128,512]{1,0:T(8,128)(2,1)} %get-tuple-element.40.refs_4_), channel_id=1, source_target_pairs={{0,32},{8,40},{16,48},{24,56},{32,64},{40,72},{48,80},{56,88},{64,... | collective-permute-start | bytes 393224 | tf_op jit(solution)/shard_map/ppermute | solution.py:611
  23.5 5.7 %copy-start.22 = (bf16[128,512]{1,0:T(8,128)(2,1)}, bf16[128,512]{1,0:T(8,128)(2,1)S(1)}, u32[]{:S(2)}) copy-start(bf16[128,512]{1,0:T(8,128)(2,1)S(1)} %collective-permute-done.4.refs_2_) | copy-start | bytes 393220
  25.5 3.7 %copy-start.23 = (bf16[128,512]{1,0:T(8,128)(2,1)}, bf16[128,512]{1,0:T(8,128)(2,1)S(1)}, u32[]{:S(2)}) copy-start(bf16[128,512]{1,0:T(8,128)(2,1)S(1)} %collective-permute-done.3.refs_1_) | copy-start | bytes 393220
  25.5 3.7 %copy-start.24 = (bf16[128,512]{1,0:T(8,128)(2,1)}, bf16[128,512]{1,0:T(8,128)(2,1)S(1)}, u32[]{:S(2)}) copy-start(bf16[128,512]{1,0:T(8,128)(2,1)S(1)} %collective-permute-done.8.refs_7_) | copy-start | bytes 393220
  25.6 3.7 %copy-start.25 = (bf16[128,512]{1,0:T(8,128)(2,1)}, bf16[128,512]{1,0:T(8,128)(2,1)S(1)}, u32[]{:S(2)}) copy-start(bf16[128,512]{1,0:T(8,128)(2,1)S(1)} %collective-permute-done.7.refs_6_) | copy-start | bytes 393220
  29.2 0.7 copy-start.26
  32.2 12.7 %collective-permute-start.11 = (bf16[4,128,512]{2,1,0:T(8,128)(2,1)}, bf16[4,128,512]{2,1,0:T(8,128)(2,1)}, u32[]{:S(2)}, u32[]{:S(2)}) collective-permute-start(bf16[4,128,512]{2,1,0:T(8,128)(2,1)} %get-tuple-element.41.refs_0_.refs_4_), channel_id=1, source_target_pairs={{0,96},{8,104},{16,112},{24,120},{32,0},{40,8},{48,16},{56,24},{64... | collective-permute-start | bytes 1572872 | tf_op jit(solution)/shard_map/ppermute | solution.py:613
  32.4 15.7 %collective-permute-start.10 = (bf16[4,128,512]{2,1,0:T(8,128)(2,1)}, bf16[4,128,512]{2,1,0:T(8,128)(2,1)}, u32[]{:S(2)}, u32[]{:S(2)}) collective-permute-start(bf16[4,128,512]{2,1,0:T(8,128)(2,1)} %get-tuple-element.41.refs_0_.refs_4_), channel_id=1, source_target_pairs={{0,64},{8,72},{16,80},{24,88},{32,96},{40,104},{48,112},{56,120},{... | collective-permute-start | bytes 1572872 | tf_op jit(solution)/shard_map/ppermute | solution.py:613
  32.7 39.3 %collective-permute-start.15 = (bf16[256,2048]{1,0:T(8,128)(2,1)}, bf16[256,2048]{1,0:T(8,128)(2,1)}, u32[]{:S(2)}, u32[]{:S(2)}) collective-permute-start(bf16[256,2048]{1,0:T(8,128)(2,1)} %bitcast.10), channel_id=1, source_target_pairs={{0,1},{1,0},{2,3},{3,2},{4,5},{5,4},{6,7},{7,6},{8,9},{9,8},{10,11... | collective-permute-start | bytes 3145736 | tf_op jit(solution)/shard_map/ppermute | solution.py:618
  35.0 20.7 %copy-start.4 = (s32[256]{0:T(256)}, s32[256]{0:T(256)S(1)}, u32[]{:S(2)}) copy-start(s32[256]{0:T(256)S(1)} %reshape.17.counts_ref) | copy-start | bytes 3076
  35.4 20.3 %copy-start.3 = (s32[1792]{0:T(1024)}, s32[1792]{0:T(1024)S(1)}, u32[]{:S(2)}) copy-start(s32[1792]{0:T(1024)S(1)} %reshape.16.tiles_ref) | copy-start | bytes 21508
  35.4 23.9 %collective-permute-start.9 = (bf16[4,128,512]{2,1,0:T(8,128)(2,1)}, bf16[4,128,512]{2,1,0:T(8,128)(2,1)}, u32[]{:S(2)}, u32[]{:S(2)}) collective-permute-start(bf16[4,128,512]{2,1,0:T(8,128)(2,1)} %get-tuple-element.41.refs_0_.refs_4_), channel_id=1, source_target_pairs={{0,32},{8,40},{16,48},{24,56},{32,64},{40,72},{48,80},{56,88},{64,... | collective-permute-start | bytes 1572872 | tf_op jit(solution)/shard_map/ppermute | solution.py:613
  36.2 25.8 %collective-permute-start.14 = (bf16[4,128,512]{2,1,0:T(8,128)(2,1)}, bf16[4,128,512]{2,1,0:T(8,128)(2,1)}, u32[]{:S(2)}, u32[]{:S(2)}) collective-permute-start(bf16[4,128,512]{2,1,0:T(8,128)(2,1)} %get-tuple-element.42.refs_4_.refs_8_), channel_id=1, source_target_pairs={{0,24},{8,0},{16,8},{24,16},{32,56},{40,32},{48,40},{56,48},{64,88... | collective-permute-start | bytes 1572872 | tf_op jit(solution)/shard_map/ppermute | solution.py:614
  44.9 19.8 %collective-permute-start.13 = (bf16[4,128,512]{2,1,0:T(8,128)(2,1)}, bf16[4,128,512]{2,1,0:T(8,128)(2,1)}, u32[]{:S(2)}, u32[]{:S(2)}) collective-permute-start(bf16[4,128,512]{2,1,0:T(8,128)(2,1)} %get-tuple-element.42.refs_4_.refs_8_), channel_id=1, source_target_pairs={{0,16},{8,24},{16,0},{24,8},{32,48},{40,56},{48,32},{56,40},{64,80... | collective-permute-start | bytes 1572872 | tf_op jit(solution)/shard_map/ppermute | solution.py:614
  48.1 23.9 %collective-permute-start.12 = (bf16[4,128,512]{2,1,0:T(8,128)(2,1)}, bf16[4,128,512]{2,1,0:T(8,128)(2,1)}, u32[]{:S(2)}, u32[]{:S(2)}) collective-permute-start(bf16[4,128,512]{2,1,0:T(8,128)(2,1)} %get-tuple-element.42.refs_4_.refs_8_), channel_id=1, source_target_pairs={{0,8},{8,16},{16,24},{24,0},{32,40},{40,48},{48,56},{56,32},{64,72... | collective-permute-start | bytes 1572872 | tf_op jit(solution)/shard_map/ppermute | solution.py:614
  48.7 7.1 %copy-start = (bf16[8,3,2,256,128]{4,3,2,1,0:T(8,128)(2,1)}, bf16[8,3,2,256,128]{4,3,2,1,0:T(8,128)(2,1)S(1)}, u32[]{:S(2)}) copy-start(bf16[8,3,2,256,128]{4,3,2,1,0:T(8,128)(2,1)S(1)} %all-to-all-done.qkv_ref) | copy-start | bytes 9437188
  55.8 1.0 copy-start.1
  59.3 18.9 %collective-permute-start = (bf16[2,512,128]{2,1,0:T(8,128)(2,1)S(1)}, bf16[2,512,128]{2,1,0:T(8,128)(2,1)S(1)}, u32[]{:S(2)}, u32[]{:S(2)}) collective-permute-start(bf16[2,512,128]{2,1,0:T(8,128)(2,1)S(1)} %get-tuple-element.36), channel_id=1, source_target_pairs={{0,2},{1,3},{2,4},{3,5},{4,6},{5,7},{6,0},{7,1},{8,10},{9,11},{10,... | collective-permute-start | bytes 786440 | tf_op jit(solution)/shard_map/ppermute | solution.py:620
  61.9 16.3 %collective-permute-start.1 = (bf16[2,512,128]{2,1,0:T(8,128)(2,1)S(1)}, bf16[2,512,128]{2,1,0:T(8,128)(2,1)S(1)}, u32[]{:S(2)}, u32[]{:S(2)}) collective-permute-start(bf16[2,512,128]{2,1,0:T(8,128)(2,1)S(1)} %get-tuple-element.37), channel_id=1, source_target_pairs={{0,4},{1,5},{2,6},{3,7},{4,0},{5,1},{6,2},{7,3},{8,12},{9,13},{10,... | collective-permute-start | bytes 786440 | tf_op jit(solution)/shard_map/ppermute | solution.py:620
  64.7 13.5 %collective-permute-start.2 = (bf16[2,512,128]{2,1,0:T(8,128)(2,1)S(1)}, bf16[2,512,128]{2,1,0:T(8,128)(2,1)S(1)}, u32[]{:S(2)}, u32[]{:S(2)}) collective-permute-start(bf16[2,512,128]{2,1,0:T(8,128)(2,1)S(1)} %get-tuple-element.38), channel_id=1, source_target_pairs={{0,6},{1,7},{2,0},{3,1},{4,2},{5,3},{6,4},{7,5},{8,14},{9,15},{10,... | collective-permute-start | bytes 786440 | tf_op jit(solution)/shard_map/ppermute | solution.py:620
  78.2 0.7 copy-start.8
  78.2 0.8 copy-start.9
  79.0 0.7 copy-start.10
  79.7 19.5 %all-to-all-start.1 = ((bf16[4,2,512,128]{3,2,1,0:T(8,128)(2,1)}), bf16[4,2,512,128]{3,2,1,0:T(8,128)(2,1)S(1)}, u32[]{:S(2)}, u32[]{:S(2)}) async-start(bf16[4,2,512,128]{3,2,1,0:T(8,128)(2,1)} %gate.2), calls=%async_computation.1 | async-start | bytes 2097152 | tf_op jit(solution)/shard_map/all_to_all | solution.py:606
  91.3 24.3 %collective-permute-start.17 = (bf16[4,128,512]{2,1,0:T(8,128)(2,1)}, bf16[4,128,512]{2,1,0:T(8,128)(2,1)}, u32[]{:S(2)}, u32[]{:S(2)}) collective-permute-start(bf16[4,128,512]{2,1,0:T(8,128)(2,1)} %get-tuple-element.50), channel_id=1, source_target_pairs={{0,8},{8,16},{16,24},{24,0},{32,40},{40,48},{48,56},{56,32},{64,72... | collective-permute-start | bytes 1572872 | tf_op jit(solution)/shard_map/ppermute | solution.py:623
  91.4 41.0 %collective-permute-start.18 = (bf16[4,128,512]{2,1,0:T(8,128)(2,1)}, bf16[4,128,512]{2,1,0:T(8,128)(2,1)}, u32[]{:S(2)}, u32[]{:S(2)}) collective-permute-start(bf16[4,128,512]{2,1,0:T(8,128)(2,1)} %get-tuple-element.51), channel_id=1, source_target_pairs={{0,16},{8,24},{16,0},{24,8},{32,48},{40,56},{48,32},{56,40},{64,80... | collective-permute-start | bytes 1572872 | tf_op jit(solution)/shard_map/ppermute | solution.py:623
  93.0 39.4 %collective-permute-start.19 = (bf16[4,128,512]{2,1,0:T(8,128)(2,1)}, bf16[4,128,512]{2,1,0:T(8,128)(2,1)}, u32[]{:S(2)}, u32[]{:S(2)}) collective-permute-start(bf16[4,128,512]{2,1,0:T(8,128)(2,1)} %get-tuple-element.52), channel_id=1, source_target_pairs={{0,24},{8,0},{16,8},{24,16},{32,56},{40,32},{48,40},{56,48},{64,88... | collective-permute-start | bytes 1572872 | tf_op jit(solution)/shard_map/ppermute | solution.py:623
  94.5 37.9 %collective-permute-start.20 = (bf16[4,128,512]{2,1,0:T(8,128)(2,1)}, bf16[4,128,512]{2,1,0:T(8,128)(2,1)}, u32[]{:S(2)}, u32[]{:S(2)}) collective-permute-start(bf16[4,128,512]{2,1,0:T(8,128)(2,1)} %get-tuple-element.54), channel_id=1, source_target_pairs={{0,32},{8,40},{16,48},{24,56},{32,64},{40,72},{48,80},{56,88},{64,... | collective-permute-start | bytes 1572872 | tf_op jit(solution)/shard_map/ppermute | solution.py:624
  96.1 36.4 %collective-permute-start.21 = (bf16[4,128,512]{2,1,0:T(8,128)(2,1)}, bf16[4,128,512]{2,1,0:T(8,128)(2,1)}, u32[]{:S(2)}, u32[]{:S(2)}) collective-permute-start(bf16[4,128,512]{2,1,0:T(8,128)(2,1)} %get-tuple-element.55), channel_id=1, source_target_pairs={{0,96},{8,104},{16,112},{24,120},{32,0},{40,8},{48,16},{56,24},{64... | collective-permute-start | bytes 1572872 | tf_op jit(solution)/shard_map/ppermute | solution.py:624
  99.2 1.0 copy-start.7
  115.6 16.9 %collective-permute-start.22 = (bf16[4,128,512]{2,1,0:T(8,128)(2,1)}, bf16[4,128,512]{2,1,0:T(8,128)(2,1)S(1)}, u32[]{:S(2)}, u32[]{:S(2)}) collective-permute-start(bf16[4,128,512]{2,1,0:T(8,128)(2,1)} %gate.3), channel_id=1, source_target_pairs={{0,64},{8,72},{16,80},{24,88},{32,96},{40,104},{48,112},{56,120},{... | collective-permute-start | bytes 1572872 | tf_op jit(solution)/shard_map/ppermute | solution.py:627
  116.3 46.5 %all-to-all-start.2 = ((bf16[8,3,2,256,128]{4,3,2,1,0:T(8,128)(2,1)}), bf16[8,3,2,256,128]{4,3,2,1,0:T(8,128)(2,1)}, u32[]{:S(2)}, u32[]{:S(2)}) async-start(bf16[8,3,2,256,128]{4,3,2,1,0:T(8,128)(2,1)} %attention_backward.1.refs_12_.refs_1_), calls=%async_computation.2 | async-start | bytes 6291456 | tf_op jit(solution)/shard_map/all_to_all | solution.py:626
  132.4 28.0 %collective-permute-start.16 = (bf16[256,2048]{1,0:T(8,128)(2,1)}, bf16[256,2048]{1,0:T(8,128)(2,1)}, u32[]{:S(2)}, u32[]{:S(2)}) collective-permute-start(bf16[256,2048]{1,0:T(8,128)(2,1)} %get-tuple-element.46), channel_id=1, source_target_pairs={{0,1},{1,0},{2,3},{3,2},{4,5},{5,4},{6,7},{7,6},{8,9},{9,8},{10,11... | collective-permute-start | bytes 3145736 | tf_op jit(solution)/shard_map/ppermute | solution.py:631
  132.5 0.8 copy-start.29
  133.3 27.0 %copy-start.6 = (f32[256,2048]{1,0:T(8,128)S(1)}, f32[256,2048]{1,0:T(8,128)}, u32[]{:S(2)}) copy-start(f32[256,2048]{1,0:T(8,128)} %get-tuple-element.45) | copy-start | bytes 6291460
  136.7 6.3 %collective-permute-start.23 = (bf16[128,512]{1,0:T(8,128)(2,1)}, bf16[128,512]{1,0:T(8,128)(2,1)S(1)}, u32[]{:S(2)}, u32[]{:S(2)}) collective-permute-start(bf16[128,512]{1,0:T(8,128)(2,1)} %get-tuple-element.58), channel_id=1, source_target_pairs={{0,32},{8,40},{16,48},{24,56},{32,64},{40,72},{48,80},{56,88},{64,... | collective-permute-start | bytes 393224 | tf_op jit(solution)/shard_map/ppermute | solution.py:633
  138.0 7.8 %collective-permute-start.24 = (bf16[128,512]{1,0:T(8,128)(2,1)}, bf16[128,512]{1,0:T(8,128)(2,1)S(1)}, u32[]{:S(2)}, u32[]{:S(2)}) collective-permute-start(bf16[128,512]{1,0:T(8,128)(2,1)} %get-tuple-element.59), channel_id=1, source_target_pairs={{0,64},{8,72},{16,80},{24,88},{32,96},{40,104},{48,112},{56,120},{... | collective-permute-start | bytes 393224 | tf_op jit(solution)/shard_map/ppermute | solution.py:633
  139.7 8.0 %collective-permute-start.25 = (bf16[128,512]{1,0:T(8,128)(2,1)}, bf16[128,512]{1,0:T(8,128)(2,1)S(1)}, u32[]{:S(2)}, u32[]{:S(2)}) collective-permute-start(bf16[128,512]{1,0:T(8,128)(2,1)} %get-tuple-element.60), channel_id=1, source_target_pairs={{0,96},{8,104},{16,112},{24,120},{32,0},{40,8},{48,16},{56,24},{64... | collective-permute-start | bytes 393224 | tf_op jit(solution)/shard_map/ppermute | solution.py:633
  140.7 7.0 %collective-permute-start.26 = (bf16[128,512]{1,0:T(8,128)(2,1)}, bf16[128,512]{1,0:T(8,128)(2,1)S(1)}, u32[]{:S(2)}, u32[]{:S(2)}) collective-permute-start(bf16[128,512]{1,0:T(8,128)(2,1)} %get-tuple-element.62), channel_id=1, source_target_pairs={{0,8},{8,16},{16,24},{24,0},{32,40},{40,48},{48,56},{56,32},{64,72... | collective-permute-start | bytes 393224 | tf_op jit(solution)/shard_map/ppermute | solution.py:634
  143.0 8.4 %copy-start.15 = (bf16[128,512]{1,0:T(8,128)(2,1)}, bf16[128,512]{1,0:T(8,128)(2,1)S(1)}, u32[]{:S(2)}) copy-start(bf16[128,512]{1,0:T(8,128)(2,1)S(1)} %collective-permute-done.23.refs_1_) | copy-start | bytes 393220
  143.0 7.2 %collective-permute-start.27 = (bf16[128,512]{1,0:T(8,128)(2,1)}, bf16[128,512]{1,0:T(8,128)(2,1)S(1)}, u32[]{:S(2)}, u32[]{:S(2)}) collective-permute-start(bf16[128,512]{1,0:T(8,128)(2,1)} %get-tuple-element.63), channel_id=1, source_target_pairs={{0,16},{8,24},{16,0},{24,8},{32,48},{40,56},{48,32},{56,40},{64,80... | collective-permute-start | bytes 393224 | tf_op jit(solution)/shard_map/ppermute | solution.py:634
  145.8 5.6 %copy-start.16 = (bf16[128,512]{1,0:T(8,128)(2,1)}, bf16[128,512]{1,0:T(8,128)(2,1)S(1)}, u32[]{:S(2)}) copy-start(bf16[128,512]{1,0:T(8,128)(2,1)S(1)} %collective-permute-done.24.refs_2_) | copy-start | bytes 393220
  145.8 5.5 %collective-permute-start.28 = (bf16[128,512]{1,0:T(8,128)(2,1)}, bf16[128,512]{1,0:T(8,128)(2,1)S(1)}, u32[]{:S(2)}, u32[]{:S(2)}) collective-permute-start(bf16[128,512]{1,0:T(8,128)(2,1)} %get-tuple-element.64), channel_id=1, source_target_pairs={{0,24},{8,0},{16,8},{24,16},{32,56},{40,32},{48,40},{56,48},{64,88... | collective-permute-start | bytes 393224 | tf_op jit(solution)/shard_map/ppermute | solution.py:634
  147.7 3.7 %copy-start.17 = (bf16[128,512]{1,0:T(8,128)(2,1)}, bf16[128,512]{1,0:T(8,128)(2,1)S(1)}, u32[]{:S(2)}) copy-start(bf16[128,512]{1,0:T(8,128)(2,1)S(1)} %collective-permute-done.25.refs_3_) | copy-start | bytes 393220
  147.7 3.7 %copy-start.18 = (bf16[128,512]{1,0:T(8,128)(2,1)}, bf16[128,512]{1,0:T(8,128)(2,1)S(1)}, u32[]{:S(2)}) copy-start(bf16[128,512]{1,0:T(8,128)(2,1)S(1)} %collective-permute-done.26.refs_5_) | copy-start | bytes 393220
  150.2 1.2 copy-start.19
  151.3 0.7 copy-start.20
  154.1 19.5 %collective-permute-start.31 = (bf16[128,1024]{1,0:T(8,128)(2,1)}, bf16[128,1024]{1,0:T(8,128)(2,1)S(1)}, u32[]{:S(2)}, u32[]{:S(2)}) collective-permute-start(bf16[128,1024]{1,0:T(8,128)(2,1)} %summed_side_by_side.1.a_ref), channel_id=1, source_target_pairs={{0,6},{1,7},{2,4},{3,5},{4,2},{5,3},{6,0},{7,1},{8,14},{9,15},{10,... | collective-permute-start | bytes 786440 | tf_op jit(solution)/shard_map/ppermute | solution.py:637
  159.7 13.9 %collective-permute-start.30 = (bf16[128,1024]{1,0:T(8,128)(2,1)}, bf16[128,1024]{1,0:T(8,128)(2,1)S(1)}, u32[]{:S(2)}, u32[]{:S(2)}) collective-permute-start(bf16[128,1024]{1,0:T(8,128)(2,1)} %summed_side_by_side.1.a_ref), channel_id=1, source_target_pairs={{0,4},{1,5},{2,6},{3,7},{4,0},{5,1},{6,2},{7,3},{8,12},{9,13},{10,... | collective-permute-start | bytes 786440 | tf_op jit(solution)/shard_map/ppermute | solution.py:637
  160.1 13.5 %collective-permute-start.29 = (bf16[128,1024]{1,0:T(8,128)(2,1)}, bf16[128,1024]{1,0:T(8,128)(2,1)S(1)}, u32[]{:S(2)}, u32[]{:S(2)}) collective-permute-start(bf16[128,1024]{1,0:T(8,128)(2,1)} %summed_side_by_side.1.a_ref), channel_id=1, source_target_pairs={{0,2},{1,3},{2,0},{3,1},{4,6},{5,7},{6,4},{7,5},{8,10},{9,11},{10,... | collective-permute-start | bytes 786440 | tf_op jit(solution)/shard_map/ppermute | solution.py:637
  173.6 0.7 copy-start.12
  173.6 0.8 copy-start.13
  173.6 0.9 copy-start.14
  176.5 1.9 %collective-permute-start.32 = (bf16[128,1024]{1,0:T(8,128)(2,1)}, bf16[128,1024]{1,0:T(8,128)(2,1)S(1)}, u32[]{:S(2)}, u32[]{:S(2)}) collective-permute-start(bf16[128,1024]{1,0:T(8,128)(2,1)} %summed_over_chips.1.own_ref), channel_id=1, source_target_pairs={{0,1},{1,0},{2,3},{3,2},{4,5},{5,4},{6,7},{7,6},{8,9},{9,8},{10,11... | collective-permute-start | bytes 786440 | tf_op jit(solution)/shard_map/ppermute | solution.py:639
  178.5 0.7 copy-start.11
  (2 other events, 1.3 us)
